TPU v7x, 512 devices: a whole 4x4x16 slice. The times are simulated.
512 devices in a mesh: seq: 64 (over z, x), grp: 8 (over y, core).
Axes of the slice: x: 4, y: 4, z: 16, core: 2. Of those that a mesh axis runs over, the one named last changes fastest.
Arguments:
- queries: bfloat16 [8192, 5120], P('seq', 'grp'), may hold values from -52 to 52
- keys_in: bfloat16 [8192, 5120], P('seq', 'grp'), may hold values from -5 to 5
- values: bfloat16 [8192, 5120], P('seq', 'grp'), may hold values from -6 to 6
- cluster_ids: int32 [8192, 1], P('seq'), may hold values from 0 to 255, as said below
- out_weight: bfloat16 [5120, 5120], P('seq', 'grp'), may hold values from -0.078125 to 0.078125
Outputs:
- mixed: bfloat16 [8192, 5120], P('seq', 'grp')
Inputs may be any that keep to these rules, and one draw needn't show every extreme that they name: `cluster_ids`: among the 128 tokens of one index of seq, no cluster is named more than 2 times, and some cluster is named exactly 2 times.
All inputs are finite; a program needn't handle non-finite values.
Results may differ from a plain program's by a relative error of at most 0.014.
Values may be sent and summed in bfloat16 or wider, within the bound.
No kernel may reach another device: no remote copies, remote signals or barrier semaphores. Data moves between devices by JAX's collectives and lax.ppermute only.
A program may use at most 64 MiB of HBM per device.

v0:
```python
import jax
import jax.numpy as jnp
from jax import lax
from jax.sharding import PartitionSpec as P

HEAD = 128
CLUSTERS = 256
SLOT_CAP = 2


def attend_clusters(pair):
    blocks, slot_pos = pair
    sources, items, capacity, triple = blocks.shape
    local_width = triple // 3
    heads_here = local_width // HEAD
    length = sources * capacity
    flat = blocks.transpose(1, 0, 2, 3).reshape(items, length, 3, heads_here, HEAD)
    query_part = flat[:, :, 0]
    key_part = flat[:, :, 1]
    value_part = flat[:, :, 2]
    where_at = slot_pos.transpose(1, 0, 2).reshape(items, length)
    scores = jnp.einsum(
        "kqhd,kshd->khqs", query_part, key_part, preferred_element_type=jnp.float32
    ) * HEAD ** (-0.5)
    allowed = (where_at[:, None, :] >= 0) & (where_at[:, None, :] <= where_at[:, :, None])
    scores = jnp.where(allowed[:, None], scores, jnp.float32(-1e30))
    peak = jnp.max(scores, axis=-1, keepdims=True)
    expo = jnp.exp(scores - peak)
    totals = jnp.sum(expo, axis=-1, keepdims=True)
    weights = (expo / totals).astype(jnp.bfloat16)
    output = jnp.einsum(
        "khqs,kshd->kqhd", weights, value_part, preferred_element_type=jnp.float32
    ).astype(jnp.bfloat16)
    return output.reshape(items, sources, capacity, local_width).transpose(1, 0, 2, 3)


def local(queries, keys_in, values, cluster_ids, out_weight):
    tok_rows = queries.shape[0]
    local_width = queries.shape[1]
    seq_count = lax.axis_size("seq")
    per_owner = CLUSTERS // seq_count
    cluster_of = cluster_ids[:, 0]
    onehot = (cluster_of[:, None] == jnp.arange(CLUSTERS, dtype=jnp.int32)[None, :]).astype(
        jnp.bfloat16
    )
    lower = (jnp.arange(tok_rows)[:, None] > jnp.arange(tok_rows)[None, :]).astype(jnp.bfloat16)
    before = jnp.dot(lower, onehot, preferred_element_type=jnp.float32)
    slot_rank = jnp.sum(before * onehot.astype(jnp.float32), axis=1).astype(jnp.int32)
    target = cluster_of * SLOT_CAP + slot_rank
    positions = lax.axis_index("seq") * tok_rows + jnp.arange(tok_rows, dtype=jnp.int32)
    packed = jnp.concatenate([queries, keys_in, values], axis=1)
    outgoing = (
        jnp.zeros((CLUSTERS * SLOT_CAP, 3 * local_width), jnp.bfloat16).at[target].set(packed)
    )
    slot_pos = jnp.full((CLUSTERS * SLOT_CAP,), -1, jnp.int32).at[target].set(positions)
    outgoing = outgoing.reshape(seq_count, per_owner, SLOT_CAP, 3 * local_width)
    slot_pos = slot_pos.reshape(seq_count, per_owner, SLOT_CAP)
    attended = attend_clusters(
        (
            lax.all_to_all(outgoing, "seq", split_axis=0, concat_axis=0, tiled=True),
            lax.all_to_all(slot_pos, "seq", split_axis=0, concat_axis=0, tiled=True),
        )
    )
    returned = lax.all_to_all(attended, "seq", split_axis=0, concat_axis=0, tiled=True)
    own_rows = returned.reshape(CLUSTERS * SLOT_CAP, local_width)[target]
    all_heads = lax.all_gather(own_rows, "grp", axis=1, tiled=True)
    mixed = jnp.dot(
        all_heads,
        lax.all_gather(out_weight, "seq", axis=0, tiled=True),
        preferred_element_type=jnp.float32,
    )
    return mixed.astype(jnp.bfloat16)


def solution(mesh):
    return jax.shard_map(
        local,
        mesh=mesh,
        in_specs=(
            P("seq", "grp"),
            P("seq", "grp"),
            P("seq", "grp"),
            P("seq", None),
            P("seq", "grp"),
        ),
        out_specs=P("seq", "grp"),
        check_vma=False,
    )
```

profile of v0, /device:TPU:1, one launch (start us, length us, event | category | flops | bytes accessed | tf_op | source)
XLA Modules:
  0.0 385.9 jit_solution(8341205021097143625)
XLA Ops:
  6.5 1.0 fusion.5
  7.6 0.7 fusion.19
  8.3 1.0 scatter_custom_fusion.1
  9.2 0.2 reshape.38
  9.4 1.1 copy.22
  10.6 19.1 %all-to-all-start.1 = ((s32[64,4,2]{1,2,0:T(2,128)}), s32[64,4,2]{1,2,0:T(2,128)S(1)}, u32[]{:S(2)}, u32[]{:S(2)}) async-start(s32[64,4,2]{1,2,0:T(2,128)} %copy.22), calls=%async_computation.1 | async-start | bytes 131072 | tf_op jit(solution)/shard_map/all_to_all | solution.py:61
  29.7 2.6 scatter_custom_fusion
  32.3 1.8 reshape.36
  34.0 9.6 %all-to-all-done.1 = s32[64,4,2]{1,2,0:T(2,128)S(1)} async-done(((s32[64,4,2]{1,2,0:T(2,128)}), s32[64,4,2]{1,2,0:T(2,128)S(1)}, u32[]{:S(2)}, u32[]{:S(2)}) %all-to-all-start.1) | async-done | bytes 2080 | tf_op jit(solution)/shard_map/all_to_all | solution.py:61
  43.7 4.9 %all-to-all-start = ((bf16[64,4,2,1920]{3,2,1,0:T(2,128)(2,1)}), bf16[64,4,2,1920]{3,2,1,0:T(2,128)(2,1)S(1)}, u32[]{:S(2)}, u32[]{:S(2)}) async-start(bf16[64,4,2,1920]{3,2,1,0:T(2,128)(2,1)} %reshape.36), calls=%async_computation | async-start | bytes 3932160 | tf_op jit(solution)/shard_map/all_to_all | solution.py:60
  48.7 0.1 copy.23
  48.8 0.2 compare_and_fusion
  49.0 87.8 %all-to-all-done = bf16[64,4,2,1920]{3,2,1,0:T(2,128)(2,1)S(1)} async-done(((bf16[64,4,2,1920]{3,2,1,0:T(2,128)(2,1)}), bf16[64,4,2,1920]{3,2,1,0:T(2,128)(2,1)S(1)}, u32[]{:S(2)}, u32[]{:S(2)}) %all-to-all-start) | async-done | bytes 1966112 | tf_op jit(solution)/shard_map/all_to_all | solution.py:60
  136.8 2.6 copy.20
  139.4 5.1 %reshape.37 = bf16[4,128,3,5,128]{4,3,2,1,0:T(8,128)(2,1)S(1)} reshape(bf16[4,64,2,1920]{3,2,1,0:T(2,128)(2,1)} %copy.20) | data formatting | bytes 3932160 | tf_op jit(solution)/shard_map/reshape | solution.py:17
  144.5 1.5 fusion.21
  146.0 0.6 fusion.3
  146.6 0.3 fusion.22
  146.9 1.0 copy-done
  147.8 0.6 copy.32
  148.5 0.5 fusion.4
  149.0 0.7 copy.29
  149.7 0.4 reshape.39
  150.1 1.3 copy.30
  151.4 10.9 %all-to-all-start.2 = ((bf16[64,4,2,640]{3,2,1,0:T(2,128)(2,1)}), bf16[64,4,2,640]{3,2,1,0:T(2,128)(2,1)S(1)}, u32[]{:S(2)}, u32[]{:S(2)}) async-start(bf16[64,4,2,640]{3,2,1,0:T(2,128)(2,1)} %copy.30), calls=%async_computation.2 | async-start | bytes 1310720 | tf_op jit(solution)/shard_map/all_to_all | solution.py:64
  162.3 34.0 %all-to-all-done.2 = bf16[64,4,2,640]{3,2,1,0:T(2,128)(2,1)S(1)} async-done(((bf16[64,4,2,640]{3,2,1,0:T(2,128)(2,1)}), bf16[64,4,2,640]{3,2,1,0:T(2,128)(2,1)S(1)}, u32[]{:S(2)}, u32[]{:S(2)}) %all-to-all-start.2) | async-done | bytes 655392 | tf_op jit(solution)/shard_map/all_to_all | solution.py:64
  196.4 0.2 reshape.40
  196.6 1.5 gather_fusion
  198.2 0.7 all-gather.4.cloned.1.call-update
  198.9 27.9 %all-gather.6.cloned.1.call-done = bf16[128,5120]{1,0:T(8,128)(2,1)} async-done(((bf16[128,640]{1,0:T(8,128)(2,1)}), bf16[128,5120]{1,0:T(8,128)(2,1)}) %all-gather.6.cloned.1.call-update) | async-done | bytes 1310736 | tf_op jit(solution)/shard_map/all_gather | solution.py:66
  226.9 147.1 %all-gather.4.cloned.1.call-done = bf16[5120,640]{1,0:T(8,128)(2,1)} async-done(((bf16[80,640]{1,0:T(8,128)(2,1)}), bf16[5120,640]{1,0:T(8,128)(2,1)}) %all-gather.4.cloned.1.call-update) | async-done | bytes 6553616 | tf_op jit(solution)/shard_map/all_gather | solution.py:69
  373.9 5.1 %convolution_convert_fusion.1 = bf16[128,640]{1,0:T(8,128)(2,1)} fusion(bf16[128,5120]{1,0:T(8,128)(2,1)} %all-gather.6.cloned.1.call-done, bf16[5120,640]{1,0:T(8,128)(2,1)} %all-gather.4.cloned.1.call-done), kind=kOutput, calls=%fused_computation.11 | convolution fusion | flops 838942720 | bytes 8028160 | tf_op jit(solution)/shard_map/dot_general | solution.py:67
  (8 shorter events, 0.2 us)
Async XLA Ops:
  10.6 33.1 %all-to-all-start.1 = ((s32[64,4,2]{1,2,0:T(2,128)}), s32[64,4,2]{1,2,0:T(2,128)S(1)}, u32[]{:S(2)}, u32[]{:S(2)}) async-start(s32[64,4,2]{1,2,0:T(2,128)} %copy.22), calls=%async_computation.1 | async-start | bytes 131072 | tf_op jit(solution)/shard_map/all_to_all | solution.py:61
  43.7 93.1 %all-to-all-start = ((bf16[64,4,2,1920]{3,2,1,0:T(2,128)(2,1)}), bf16[64,4,2,1920]{3,2,1,0:T(2,128)(2,1)S(1)}, u32[]{:S(2)}, u32[]{:S(2)}) async-start(bf16[64,4,2,1920]{3,2,1,0:T(2,128)(2,1)} %reshape.36), calls=%async_computation | async-start | bytes 3932160 | tf_op jit(solution)/shard_map/all_to_all | solution.py:60
  146.6 1.2 copy-start
  151.4 45.0 %all-to-all-start.2 = ((bf16[64,4,2,640]{3,2,1,0:T(2,128)(2,1)}), bf16[64,4,2,640]{3,2,1,0:T(2,128)(2,1)S(1)}, u32[]{:S(2)}, u32[]{:S(2)}) async-start(bf16[64,4,2,640]{3,2,1,0:T(2,128)(2,1)} %copy.30), calls=%async_computation.2 | async-start | bytes 1310720 | tf_op jit(solution)/shard_map/all_to_all | solution.py:64
  162.3 64.6 %all-gather.6.cloned.1.call-start = ((), (), s32[]{:S(2)}) async-start(), calls=%async_computation.4 | async-start | bytes 1474560 | tf_op jit(solution)/shard_map/all_gather | solution.py:66
  198.2 175.7 %all-gather.4.cloned.1.call-start = ((), (), s32[]{:S(2)}) async-start(), calls=%async_computation.3 | async-start | bytes 6656000 | tf_op jit(solution)/shard_map/all_gather | solution.py:69
Sparse Core Ops, SparseCore 0:
  198.3 28.4 all-gather.5
  229.8 144.0 all-gather.3
where the time goes:
time: 394 us; the launch traced here: 386 us
  waiting for transfers between devices  307 us (78%)
  starting transfers between devices  35 us (9%)
  local copies, waits for them, and re-layouts  19.2 us (5%)
  between operations  13.6 us (3%)
  matrix products  7.26 us (2%)
    all_gather x1, waiting for transfers between devices, local(): lax.all_gather(out_weight, 'seq', axis=0, tiled=True)  147 us
    all_to_all x1, waiting for transfers between devices, local(): lax.all_to_all(outgoing, 'seq', split_axis=0, concat_axis=0, tiled=True)  87.8 us
    all_to_all x1, waiting for transfers between devices, local(): lax.all_to_all(attended, 'seq', split_axis=0, concat_axis=0, tiled=True)  34 us
    all_gather x1, waiting for transfers between devices, local(): all_heads = lax.all_gather(own_rows, 'grp', axis=1, tiled=True)  27.9 us
    all_to_all x1, starting transfers between devices, local(): lax.all_to_all(slot_pos, 'seq', split_axis=0, concat_axis=0, tiled=True)  19.1 us
    all_to_all x1, starting transfers between devices, local(): lax.all_to_all(attended, 'seq', split_axis=0, concat_axis=0, tiled=True)  10.9 us
    all_to_all x1, waiting for transfers between devices, local(): lax.all_to_all(slot_pos, 'seq', split_axis=0, concat_axis=0, tiled=True)  9.64 us
  transfers between devices with their start and end apart: 5, of which 5 were waited for; matrix products, arithmetic and copies ran while one was open for 1% of the time, Pallas kernels for 0%

commit v1 on v0

v1 whole, which is shorter than its diff:
```python
import functools

import jax
import jax.numpy as jnp
from jax import lax
from jax.experimental import pallas as pl
from jax.experimental.pallas import tpu as pltpu
from jax.sharding import Mesh
from jax.sharding import PartitionSpec as P

HEAD = 128
HEADS_HERE = 5
TOK = 128
Z, X, Y, C = 16, 4, 4, 2
PARTS = 3
STARTS = (0, 44, 88)
LENGTHS = (44, 44, 40)
SLOT = 48
ID_ROW = 46
POSITIONS = 8192
NEVER = 1e9
BLOCKED = -1e30
F32 = jnp.float32
BF16 = jnp.bfloat16
VMEM_LIMIT = 56 * 1024 * 1024


def vmem_call(body, out_shape, *operands):
    space = pl.BlockSpec(memory_space=pltpu.VMEM)
    many = isinstance(out_shape, (list, tuple))
    return pl.pallas_call(
        body,
        out_shape=out_shape,
        in_specs=[space] * len(operands),
        out_specs=[space] * len(out_shape) if many else space,
        compiler_params=pltpu.CompilerParams(vmem_limit_bytes=VMEM_LIMIT),
    )(*operands)


def scatter_heads(q_ref, k_ref, v_ref, ids_ref, out_ref):
    ids = ids_ref[...].astype(F32)
    lane = lax.broadcasted_iota(jnp.int32, (SLOT, HEAD), 1)
    row = lax.broadcasted_iota(jnp.int32, (SLOT, HEAD), 0)
    id_rows = []
    for start, length in zip(STARTS, LENGTHS):
        moved = ids if start == 0 else pltpu.roll(ids, TOK - start, 1)
        id_rows.append(jnp.where(lane < length, jnp.broadcast_to(moved, (SLOT, HEAD)), -1.0))
    every = jnp.broadcast_to(ids, (SLOT, HEAD))
    for h in range(HEADS_HERE):
        for part, source in enumerate((q_ref, k_ref, v_ref)):
            block = source[:, h * HEAD : (h + 1) * HEAD].astype(F32)
            block = jnp.concatenate([block, jnp.zeros((16, HEAD), F32)], axis=0)
            for r, (start, length) in enumerate(zip(STARTS, LENGTHS)):
                piece = jnp.where(row < length, block[start : start + SLOT], 0.0)
                if part == 0:
                    piece = jnp.where(row == ID_ROW, id_rows[r], piece)
                    piece = jnp.where(row == ID_ROW + 1, every, piece)
                out_ref[PARTS * h + r, part * SLOT : (part + 1) * SLOT, :] = piece.astype(BF16)
    out_ref[PARTS * HEADS_HERE] = jnp.zeros((3 * SLOT, HEAD), BF16)


def attend(q_ref, kv0_ref, kv1_ref, kv2_ref, qcode_ref, kcode_ref, out_ref):
    rows = Z * SLOT
    keys = [ref[:, :SLOT, :].reshape(rows, HEAD) for ref in (kv0_ref, kv1_ref, kv2_ref)]
    vals = [ref[:, SLOT:, :].reshape(rows, HEAD) for ref in (kv0_ref, kv1_ref, kv2_ref)]
    codes = qcode_ref[...].T
    lane = lax.broadcasted_iota(jnp.int32, (SLOT, HEAD), 1)
    stats = [jnp.zeros((SLOT, HEAD), F32) for _ in range(X)]
    group = 4
    for g in range(Z // group):
        count = -(-(g + 1) * group * SLOT // HEAD) * HEAD
        for x in range(X):
            code = jnp.concatenate(
                [codes[:SLOT, x * Z + z : x * Z + z + 1] for z in range(g * group, (g + 1) * group)], axis=0
            )
            base = jnp.floor(code * (1.0 / POSITIONS)) * POSITIONS
            query = q_ref[x, g * group * SLOT : (g + 1) * group * SLOT, :]
            scores = []
            for j in range(PARTS):
                score = lax.dot_general(
                    query, keys[j][:count], (((1,), (1,)), ((), ())), preferred_element_type=F32
                ) * HEAD ** (-0.5)
                key_code = kcode_ref[j : j + 1, :count]
                allowed = (key_code <= code) & (key_code >= base)
                scores.append(jnp.where(allowed, score, BLOCKED))
            peak = functools.reduce(jnp.maximum, [jnp.max(s, axis=1, keepdims=True) for s in scores])
            total = jnp.zeros_like(peak)
            output = jnp.zeros((group * SLOT, HEAD), F32)
            for j in range(PARTS):
                expo = jnp.exp(scores[j] - peak)
                total = total + jnp.sum(expo, axis=1, keepdims=True)
                output = output + jnp.dot(
                    expo.astype(BF16), vals[j][:count], preferred_element_type=F32
                )
            out_ref[x, g * group * SLOT : (g + 1) * group * SLOT, :] = (output / total).astype(BF16)
            logsum = peak + jnp.log(total)
            high = logsum.astype(BF16).astype(F32)
            rest = logsum - high
            middle = rest.astype(BF16).astype(F32)
            low = rest - middle
            for n in range(group):
                for part, column in enumerate((high, middle, low)):
                    stats[x] = jnp.where(
                        lane == part * Z + g * group + n, column[n * SLOT : (n + 1) * SLOT], stats[x]
                    )
    for x in range(X):
        out_ref[x, rows:, :] = stats[x].astype(BF16)


def join(part_ref, out_ref):
    rows = Z * SLOT
    sums = []
    for x in range(X):
        stat = part_ref[x, rows:, :].astype(F32)
        sums.append(stat + pltpu.roll(stat, HEAD - Z, 1) + pltpu.roll(stat, HEAD - 2 * Z, 1))
    peak = functools.reduce(jnp.maximum, sums)
    weights = [jnp.exp(s - peak) for s in sums]
    total = functools.reduce(jnp.add, weights)
    weights = [w / total for w in weights]
    for z in range(Z):
        joined = functools.reduce(
            jnp.add,
            [
                weights[x][:, z : z + 1] * part_ref[x, z * SLOT : (z + 1) * SLOT, :].astype(F32)
                for x in range(X)
            ],
        )
        out_ref[z] = joined.astype(BF16)


def assemble(part_ref, out_ref):
    width = HEADS_HERE * HEAD
    heads = []
    for h in range(HEADS_HERE):
        pieces = [
            part_ref[PARTS * h + r].astype(F32)[:length] for r, length in enumerate(LENGTHS)
        ]
        heads.append(jnp.concatenate(pieces, axis=0))
    whole = jnp.concatenate(heads, axis=1)
    chunk = width // (2 * X)
    for x in range(X):
        halves = [whole[:, a * width // 2 + x * chunk : a * width // 2 + (x + 1) * chunk] for a in range(2)]
        out_ref[x] = jnp.concatenate(halves, axis=1).astype(BF16)


def project(mine_ref, other_ref, weight_ref, core_ref, out_ref):
    depth = mine_ref.shape[2]
    core = core_ref[0]
    tokens = mine_ref.shape[1]
    for x in range(X):
        rows = slice(x * tokens // X, (x + 1) * tokens // X)
        total = jnp.zeros((tokens // X, weight_ref.shape[1]), F32)
        for y in range(Y):
            for source, which in ((mine_ref, core), (other_ref, 1 - core)):
                first = pl.multiple_of((C * y + which) * depth, 32)
                total = total + jnp.dot(
                    source[y, rows, :], weight_ref[pl.ds(first, depth), :], preferred_element_type=F32
                )
        out_ref[x] = total.astype(BF16)


def local(queries, keys_in, values, cluster_ids, out_weight):
    plane, side, core = lax.axis_index("z"), lax.axis_index("x"), lax.axis_index("c")
    third = lax.rem(plane, PARTS)
    weight = lax.all_gather(out_weight, "z", axis=0, tiled=True)

    send = vmem_call(
        scatter_heads,
        jax.ShapeDtypeStruct((Z, 3 * SLOT, HEAD), BF16),
        queries,
        keys_in,
        values,
        cluster_ids.reshape(1, TOK),
    )
    here = lax.all_to_all(send, "z", 0, 0, tiled=True)
    kv = here[:, SLOT:, :]
    turns = [
        [(PARTS * h + r, PARTS * h + (r + k) % PARTS) for h in range(HEADS_HERE) for r in range(PARTS)]
        for k in (1, 2)
    ]
    kv_others = [lax.ppermute(kv, "z", turn) for turn in turns]
    query = lax.all_gather(here[:, :SLOT, :].reshape(Z * SLOT, HEAD), "x", axis=0)

    lane = jnp.arange(HEAD, dtype=jnp.int32)
    home = (X * jnp.arange(Z, dtype=jnp.int32) + side) * TOK
    key_code = here[:, ID_ROW + 1, :].astype(F32) * POSITIONS + (home[:, None] + lane[None, :]).astype(F32)
    key_code = jnp.stack(
        [
            jnp.pad(
                key_code[:, start : start + length], ((0, 0), (0, SLOT - length)), constant_values=NEVER
            ).reshape(Z * SLOT)
            for start, length in zip(STARTS, LENGTHS)
        ]
    )
    order = [third, lax.rem(third + 2, PARTS), lax.rem(third + 1, PARTS)]
    key_code = jnp.concatenate(
        [lax.dynamic_slice_in_dim(key_code, turn, 1, axis=0) for turn in order], axis=0
    )
    first = jnp.where(third == 0, STARTS[0], jnp.where(third == 1, STARTS[1], STARTS[2]))
    all_home = (
        X * jnp.arange(Z, dtype=jnp.int32)[None, :] + jnp.arange(X, dtype=jnp.int32)[:, None]
    ) * TOK + first
    query_code = query.reshape(X, Z, SLOT, HEAD)[:, :, ID_ROW, :].astype(F32) * POSITIONS + (
        all_home[:, :, None] + lane[None, None, :]
    ).astype(F32)
    query_code = jnp.pad(query_code.reshape(X * Z, HEAD), ((0, HEAD - X * Z), (0, 0)))

    part = vmem_call(
        attend,
        jax.ShapeDtypeStruct((X, (Z + 1) * SLOT, HEAD), BF16),
        query,
        kv,
        kv_others[0],
        kv_others[1],
        query_code,
        key_code,
    )
    part = lax.all_to_all(part, "x", 0, 0, tiled=True)
    joined = vmem_call(join, jax.ShapeDtypeStruct((Z, SLOT, HEAD), BF16), part)
    joined = lax.all_to_all(joined, "z", 0, 0, tiled=True)
    depth = HEADS_HERE * HEAD // X
    rows = vmem_call(assemble, jax.ShapeDtypeStruct((X, TOK, depth), BF16), joined)
    rows = lax.all_to_all(rows, "x", 0, 0, tiled=True).reshape(X * TOK, depth)
    rows = lax.all_gather(rows, "y", axis=0)
    others = lax.ppermute(rows, "c", [(0, 1), (1, 0)])
    partial = pl.pallas_call(
        project,
        out_shape=jax.ShapeDtypeStruct((X, TOK, out_weight.shape[1]), BF16),
        in_specs=[pl.BlockSpec(memory_space=pltpu.VMEM)] * 3 + [pl.BlockSpec(memory_space=pltpu.SMEM)],
        out_specs=pl.BlockSpec(memory_space=pltpu.VMEM),
        compiler_params=pltpu.CompilerParams(vmem_limit_bytes=VMEM_LIMIT),
    )(rows, others, weight, core.reshape(1))
    partial = lax.all_to_all(partial, "x", 0, 0, tiled=True)
    return jnp.sum(partial.astype(F32), axis=0).astype(BF16)


def solution(mesh):
    fine = Mesh(mesh.devices.reshape(Z, X, Y, C), ("z", "x", "y", "c"))
    both = P(("z", "x"), ("y", "c"))
    return jax.shard_map(
        local,
        mesh=fine,
        in_specs=(both, both, both, P(("z", "x"), None), both),
        out_specs=both,
        check_vma=False,
    )
```

time: 394 us -> 200 us (0.51); the launches traced: 386 us -> 199 us
  waiting for transfers between devices: 307 us -> 31.6 us
  blocking collectives: 0 us -> 88.5 us
  Pallas kernels: 0 us -> 24.6 us
  local copies, waits for them, and re-layouts: 19.2 us -> 5.89 us
  matrix products: 7.26 us -> 0 us
    all_gather x2 -> x1, waiting for transfers between devices: 175 us -> 0.01 us  [local(): weight = lax.all_gather(out_weight, 'z', axis=0, tiled=True)]
    all_to_all x3 -> x1, waiting for transfers between devices: 131 us -> 24.3 us  [local(): here = lax.all_to_all(send, 'z', 0, 0, tiled=True)]
    all_to_all x0 -> x4, blocking collectives: none -> 65.9 us  [the longest x1 31.4 us: local(): joined = lax.all_to_all(joined, 'z', 0, 0, tiled=True)]
    pallas_call x0 -> x5, Pallas kernels: none -> 24.6 us  [the longest x4 19.9 us: vmem_call(): pl.pallas_call(body, out_shape=out_shape, in_specs=[space] * len(operands...]
    all_gather x0 -> x2, blocking collectives: none -> 22.6 us  [the longest x1 11.6 us: local(): lax.all_gather(here[:, :SLOT, :].reshape(Z * SLOT, HEAD), 'x', axis=0)]
    all_to_all x3 -> x1, starting transfers between devices: 34.9 us -> 15.9 us  [local(): here = lax.all_to_all(send, 'z', 0, 0, tiled=True)]
    ppermute x0 -> x3, starting transfers between devices: none -> 17.5 us  [the longest x1 10.9 us: local(): others = lax.ppermute(rows, 'c', [(0, 1), (1, 0)])]
    reshape x6 -> x0, local copies, waits for them, and re-layouts: 8.81 us -> none  [the longest x1 5.08 us: attend_clusters(): blocks.transpose(1, 0, 2, 3).reshape(items, length, 3, heads_here, HEAD)]
  transfers between devices with their start and end apart: 5 -> 5, of which waited for: 5 -> 3; matrix products, arithmetic and copies ran while one was open for 1% -> 3% of each run, Pallas kernels for 0% -> 9%
where the time goes in v1:
time: 200 us; the launch traced here: 199 us
  blocking collectives  88.5 us (44%)
  starting transfers between devices  33.4 us (17%)
  waiting for transfers between devices  31.6 us (16%)
  Pallas kernels  24.6 us (12%)
  between operations  13.6 us (7%)
  local copies, waits for them, and re-layouts  5.89 us (3%)
    all_to_all x1, blocking collectives, local(): joined = lax.all_to_all(joined, 'z', 0, 0, tiled=True)  31.4 us
    all_to_all x1, waiting for transfers between devices, local(): here = lax.all_to_all(send, 'z', 0, 0, tiled=True)  24.3 us
    pallas_call x4, Pallas kernels, vmem_call(): pl.pallas_call(body, out_shape=out_shape, in_specs=[space] * len(operands...  19.9 us
    all_to_all x1, starting transfers between devices, local(): here = lax.all_to_all(send, 'z', 0, 0, tiled=True)  15.9 us
    all_to_all x1, blocking collectives, local(): partial = lax.all_to_all(partial, 'x', 0, 0, tiled=True)  14.1 us
    all_to_all x1, blocking collectives, local(): part = lax.all_to_all(part, 'x', 0, 0, tiled=True)  13.1 us
    all_gather x1, blocking collectives, local(): lax.all_gather(here[:, :SLOT, :].reshape(Z * SLOT, HEAD), 'x', axis=0)  11.6 us
    all_gather x1, blocking collectives, local(): rows = lax.all_gather(rows, 'y', axis=0)  11 us
  transfers between devices with their start and end apart: 5, of which 3 were waited for; matrix products, arithmetic and copies ran while one was open for 3% of the time, Pallas kernels for 9%

profile of v1, /device:TPU:1, one launch (start us, length us, event | category | flops | bytes accessed | tf_op | source)
XLA Modules:
  0.0 199.2 jit_solution(15155390430077062281)
XLA Ops:
  6.5 2.0 %shard_map.55 = bf16[16,144,128]{2,1,0:T(8,128)(2,1)} custom-call(bf16[128,640]{1,0:T(8,128)(2,1)} %q_ref.1, bf16[128,640]{1,0:T(8,128)(2,1)} %k_ref.1, bf16[128,640]{1,0:T(8,128)(2,1)} %v_ref.1, s32[1,128]{1,0:T(1,128)} %bitcast.14), custom_call_target="tpu_custom_call" | custom-call | tf_op jit(solution)/shard_map/pallas_call | solution.py:31
  8.5 15.9 %all-to-all-start = ((bf16[16,144,128]{2,1,0:T(8,128)(2,1)}), bf16[16,144,128]{2,1,0:T(8,128)(2,1)S(1)}, u32[]{:S(2)}, u32[]{:S(2)}) async-start(bf16[16,144,128]{2,1,0:T(8,128)(2,1)} %shard_map.55), calls=%async_computation | async-start | bytes 1179648 | tf_op jit(solution)/shard_map/all_to_all | solution.py:175
  24.5 0.7 all-gather.2.cloned.1.call-update
  25.2 0.1 add.97
  25.3 0.1 add.99
  25.4 24.3 %all-to-all-done = bf16[16,144,128]{2,1,0:T(8,128)(2,1)S(1)} async-done(((bf16[16,144,128]{2,1,0:T(8,128)(2,1)}), bf16[16,144,128]{2,1,0:T(8,128)(2,1)S(1)}, u32[]{:S(2)}, u32[]{:S(2)}) %all-to-all-start) | async-done | bytes 589856 | tf_op jit(solution)/shard_map/all_to_all | solution.py:175
  49.8 4.6 %collective-permute-start = (bf16[16,96,128]{2,1,0:T(8,128)(2,1)S(1)}, bf16[16,96,128]{2,1,0:T(8,128)(2,1)S(1)}, u32[]{:S(2)}, u32[]{:S(2)}) collective-permute-start(bf16[16,96,128]{2,1,0:T(8,128)(2,1)S(1)} %slice.30.kv0_ref), channel_id=1, source_target_pairs={{0,32},{32,64},{64,0},{96,128},{128,160},{160,96},{192,224},{224,2... | collective-permute-start | bytes 1179656 | tf_op jit(solution)/shard_map/ppermute | solution.py:181
  54.4 2.0 %collective-permute-start.1 = (bf16[16,96,128]{2,1,0:T(8,128)(2,1)S(1)}, bf16[16,96,128]{2,1,0:T(8,128)(2,1)S(1)}, u32[]{:S(2)}, u32[]{:S(2)}) collective-permute-start(bf16[16,96,128]{2,1,0:T(8,128)(2,1)S(1)} %slice.30.kv0_ref), channel_id=1, source_target_pairs={{0,64},{32,0},{64,32},{96,160},{128,96},{160,128},{192,256},{224,1... | collective-permute-start | bytes 1179656 | tf_op jit(solution)/shard_map/ppermute | solution.py:181
  56.4 11.6 %all_gather.9.q_ref = bf16[4,768,128]{2,1,0:T(8,128)(2,1)S(1)} all-gather(bf16[1,768,128]{2,1,0:T(8,128)(2,1)S(1)} %bitcast.12), channel_id=1, replica_groups=mesh['z'=16,'x'=4,'y'=4,'c'=2] {'x'}, dimensions={0}, use_global_device_ids=true | all-gather | bytes 983040 | tf_op jit(solution)/shard_map/all_gather | solution.py:182
  68.4 0.1 stack_reshape.10
  68.5 0.1 stack_reshape.11
  68.6 0.1 stack_reshape.9
  68.7 0.6 pad.15.qcode_ref
  69.4 0.6 pad_maximum_fusion.1.kcode_ref
  70.0 6.2 %collective-permute-done.1.kv2_ref = bf16[16,96,128]{2,1,0:T(8,128)(2,1)S(1)} collective-permute-done((bf16[16,96,128]{2,1,0:T(8,128)(2,1)S(1)}, bf16[16,96,128]{2,1,0:T(8,128)(2,1)S(1)}, u32[]{:S(2)}, u32[]{:S(2)}) %collective-permute-start.1) | collective-permute-done | bytes 393248 | tf_op jit(solution)/shard_map/ppermute | solution.py:181
  76.2 0.7 copy-done.3
  76.9 13.7 %shard_map.56 = bf16[4,816,128]{2,1,0:T(8,128)(2,1)} custom-call(bf16[4,768,128]{2,1,0:T(8,128)(2,1)} %copy-done, bf16[16,96,128]{2,1,0:T(8,128)(2,1)} %copy-done.1, bf16[16,96,128]{2,1,0:T(8,128)(2,1)} %copy-done.2, bf16[16,96,128]{2,1,0:T(8,128)(2,1)} %copy-done.3, f32[128,128]{1,0:T(8,128)} %pad.15.qcode_ref, f32[3,768]{1,0:T(4,128)} %pad_maximum_fusion.1.kcode_ref), custom_call_target="tpu_custom_call" | custom-call | tf_op jit(solution)/shard_map/pallas_call | solution.py:31
  90.6 13.1 %all_to_all.25.part_ref = bf16[4,816,128]{2,1,0:T(8,128)(2,1)} all-to-all(bf16[4,816,128]{2,1,0:T(8,128)(2,1)} %shard_map.56), channel_id=1, replica_groups=mesh['z'=16,'x'=4,'y'=4,'c'=2] {'x'}, dimensions={0} | all-to-all | bytes 1671168 | tf_op jit(solution)/shard_map/all_to_all | solution.py:218
  103.7 2.4 %shard_map.57 = bf16[16,48,128]{2,1,0:T(8,128)(2,1)} custom-call(bf16[4,816,128]{2,1,0:T(8,128)(2,1)} %all_to_all.25.part_ref), custom_call_target="tpu_custom_call" | custom-call | tf_op jit(solution)/shard_map/pallas_call | solution.py:31
  106.1 31.4 %all_to_all.26.part_ref = bf16[16,48,128]{2,1,0:T(8,128)(2,1)} all-to-all(bf16[16,48,128]{2,1,0:T(8,128)(2,1)} %shard_map.57), channel_id=1, replica_groups=mesh['z'=16,'x'=4,'y'=4,'c'=2] {'z'}, dimensions={0} | all-to-all | bytes 393216 | tf_op jit(solution)/shard_map/all_to_all | solution.py:220
  137.5 1.8 shard_map.58
  139.3 1.1 copy.12
  140.4 7.4 %all_to_all.27 = bf16[4,128,160]{1,2,0:T(8,128)(2,1)S(1)} all-to-all(bf16[4,128,160]{1,2,0:T(8,128)(2,1)S(1)} %copy.12), channel_id=1, replica_groups=mesh['z'=16,'x'=4,'y'=4,'c'=2] {'x'}, dimensions={0} | all-to-all | bytes 327680 | tf_op jit(solution)/shard_map/all_to_all | solution.py:223
  147.8 0.1 copy.13
  147.9 11.0 %all_gather.10 = bf16[4,512,160]{1,2,0:T(8,128)(2,1)S(1)} all-gather(bf16[1,512,160]{1,2,0:T(8,128)(2,1)S(1)} %all_gather_reshape.7), channel_id=1, replica_groups=mesh['z'=16,'x'=4,'y'=4,'c'=2] {'y'}, dimensions={0}, use_global_device_ids=true | all-gather | bytes 819200 | tf_op jit(solution)/shard_map/all_gather | solution.py:224
  158.9 10.9 %collective-permute-start.2 = (bf16[4,512,160]{1,2,0:T(8,128)(2,1)S(1)}, bf16[4,512,160]{1,2,0:T(8,128)(2,1)S(1)}, u32[]{:S(2)}, u32[]{:S(2)}) collective-permute-start(bf16[4,512,160]{1,2,0:T(8,128)(2,1)S(1)} %all_gather.10), channel_id=1, source_target_pairs={{0,1},{1,0},{2,3},{3,2},{4,5},{5,4},{6,7},{7,6},{8,9},{9,8},{10,11... | collective-permute-start | bytes 1966088 | tf_op jit(solution)/shard_map/ppermute | solution.py:225
  169.8 1.3 copy.14.mine_ref
  171.1 0.4 collective-permute-done.2
  171.5 1.3 copy.15.other_ref
  172.8 4.7 %shard_map.59 = bf16[4,128,640]{2,1,0:T(8,128)(2,1)} custom-call(bf16[4,512,160]{2,1,0:T(8,128)(2,1)} %copy.14.mine_ref, bf16[4,512,160]{2,1,0:T(8,128)(2,1)} %copy.15.other_ref, bf16[1280,640]{1,0:T(8,128)(2,1)} %all-gather.2.cloned.1.call-done.weight_ref, s32[1]{0:T(128)} %bitcast.5.core_ref), custom_call_target="tpu_custom_call" | custom-call | tf_op jit(solution)/shard_map/pallas_call | solution.py:226
  177.5 14.1 %all_to_all.28 = bf16[4,128,640]{2,1,0:T(8,128)(2,1)S(1)} all-to-all(bf16[4,128,640]{2,1,0:T(8,128)(2,1)} %shard_map.59), channel_id=1, replica_groups=mesh['z'=16,'x'=4,'y'=4,'c'=2] {'x'}, dimensions={0} | all-to-all | bytes 1310720 | tf_op jit(solution)/shard_map/all_to_all | solution.py:233
  191.6 0.8 reduce_sum.12
  (32 shorter events, 0.6 us)
Async XLA Ops:
  8.5 59.7 %copy-start.4 = (pred[48]{0:T(512)(128)(4,1)S(1)}, pred[48]{0:T(512)(128)(4,1)}, u32[]{:S(2)}) copy-start(pred[48]{0:T(512)(128)(4,1)} %constant.16.clone.1) | copy-start | bytes 148
  8.5 41.2 %all-to-all-start = ((bf16[16,144,128]{2,1,0:T(8,128)(2,1)}), bf16[16,144,128]{2,1,0:T(8,128)(2,1)S(1)}, u32[]{:S(2)}, u32[]{:S(2)}) async-start(bf16[16,144,128]{2,1,0:T(8,128)(2,1)} %shard_map.55), calls=%async_computation | async-start | bytes 1179648 | tf_op jit(solution)/shard_map/all_to_all | solution.py:175
  24.4 148.4 %all-gather.2.cloned.1.call-start = ((), (), s32[]{:S(2)}) async-start(), calls=%async_computation.5 | async-start | bytes 1740800 | tf_op jit(solution)/shard_map/all_gather | solution.py:165
  49.8 26.4 %copy-start.1 = (bf16[16,96,128]{2,1,0:T(8,128)(2,1)}, bf16[16,96,128]{2,1,0:T(8,128)(2,1)S(1)}, u32[]{:S(2)}) copy-start(bf16[16,96,128]{2,1,0:T(8,128)(2,1)S(1)} %slice.30.kv0_ref) | copy-start | bytes 1179652
  49.8 20.2 %collective-permute-start = (bf16[16,96,128]{2,1,0:T(8,128)(2,1)S(1)}, bf16[16,96,128]{2,1,0:T(8,128)(2,1)S(1)}, u32[]{:S(2)}, u32[]{:S(2)}) collective-permute-start(bf16[16,96,128]{2,1,0:T(8,128)(2,1)S(1)} %slice.30.kv0_ref), channel_id=1, source_target_pairs={{0,32},{32,64},{64,0},{96,128},{128,160},{160,96},{192,224},{224,2... | collective-permute-start | bytes 1179656 | tf_op jit(solution)/shard_map/ppermute | solution.py:181
  54.4 21.8 %collective-permute-start.1 = (bf16[16,96,128]{2,1,0:T(8,128)(2,1)S(1)}, bf16[16,96,128]{2,1,0:T(8,128)(2,1)S(1)}, u32[]{:S(2)}, u32[]{:S(2)}) collective-permute-start(bf16[16,96,128]{2,1,0:T(8,128)(2,1)S(1)} %slice.30.kv0_ref), channel_id=1, source_target_pairs={{0,64},{32,0},{64,32},{96,160},{128,96},{160,128},{192,256},{224,1... | collective-permute-start | bytes 1179656 | tf_op jit(solution)/shard_map/ppermute | solution.py:181
  68.0 8.1 %copy-start = (bf16[4,768,128]{2,1,0:T(8,128)(2,1)}, bf16[4,768,128]{2,1,0:T(8,128)(2,1)S(1)}, u32[]{:S(2)}) copy-start(bf16[4,768,128]{2,1,0:T(8,128)(2,1)S(1)} %all_gather.9.q_ref) | copy-start | bytes 2359300
  70.0 6.2 %copy-start.2 = (bf16[16,96,128]{2,1,0:T(8,128)(2,1)}, bf16[16,96,128]{2,1,0:T(8,128)(2,1)S(1)}, u32[]{:S(2)}) copy-start(bf16[16,96,128]{2,1,0:T(8,128)(2,1)S(1)} %collective-permute-done.kv1_ref) | copy-start | bytes 1179652
  76.2 0.7 copy-start.3
  158.9 12.6 %collective-permute-start.2 = (bf16[4,512,160]{1,2,0:T(8,128)(2,1)S(1)}, bf16[4,512,160]{1,2,0:T(8,128)(2,1)S(1)}, u32[]{:S(2)}, u32[]{:S(2)}) collective-permute-start(bf16[4,512,160]{1,2,0:T(8,128)(2,1)S(1)} %all_gather.10), channel_id=1, source_target_pairs={{0,1},{1,0},{2,3},{3,2},{4,5},{5,4},{6,7},{7,6},{8,9},{9,8},{10,11... | collective-permute-start | bytes 1966088 | tf_op jit(solution)/shard_map/ppermute | solution.py:225
Sparse Core Ops, SparseCore 0:
  27.3 75.5 all-gather.1

commit v2 on v1

v2 whole, which is shorter than its diff:
```python
import functools

import jax
import jax.numpy as jnp
from jax import lax
from jax.experimental import pallas as pl
from jax.experimental.pallas import tpu as pltpu
from jax.sharding import Mesh
from jax.sharding import PartitionSpec as P

HEAD = 128
HEADS_HERE = 5
TOK = 128
Z, X, Y, C = 16, 4, 4, 2
PARTS = 3
STARTS = (0, 44, 88)
LENGTHS = (44, 44, 40)
SLOT = 48
ID_ROW = 46
POSITIONS = 8192
NEVER = 1e9
BLOCKED = -1e30
F32 = jnp.float32
BF16 = jnp.bfloat16
LOG2E = 1.4426950408889634
SHARE = 32
GRANULE = 16


def vmem_call(body, mebibytes, shape, *operands, scalars=None):
    specs = [pl.BlockSpec(memory_space=pltpu.VMEM)] * len(operands)
    if scalars is not None:
        specs = [pl.BlockSpec(memory_space=pltpu.SMEM)] + specs
        operands = (scalars,) + operands
    return pl.pallas_call(
        body,
        out_shape=jax.ShapeDtypeStruct(shape, BF16),
        in_specs=specs,
        out_specs=pl.BlockSpec(memory_space=pltpu.VMEM),
        compiler_params=pltpu.CompilerParams(vmem_limit_bytes=mebibytes * 1024 * 1024),
    )(*operands)


def scatter_heads(q_ref, k_ref, v_ref, ids_ref, out_ref):
    ids = ids_ref[...].astype(F32)
    lane = lax.broadcasted_iota(jnp.int32, (SLOT, HEAD), 1)
    row = lax.broadcasted_iota(jnp.int32, (SLOT, HEAD), 0)
    id_rows = []
    for start, length in zip(STARTS, LENGTHS):
        moved = ids if start == 0 else pltpu.roll(ids, TOK - start, 1)
        id_rows.append(jnp.where(lane < length, jnp.broadcast_to(moved, (SLOT, HEAD)), -1.0))
    every = jnp.broadcast_to(ids, (SLOT, HEAD))
    source = lax.broadcasted_iota(jnp.int32, (HEAD, HEAD), 0)
    to = lax.broadcasted_iota(jnp.int32, (HEAD, HEAD), 1)
    origin = (to % SHARE) // GRANULE * (X * GRANULE) + to // SHARE * GRANULE + to % GRANULE
    turn = jnp.where(source == origin, 1.0, 0.0).astype(BF16)
    for h in range(HEADS_HERE):
        for part, ref in enumerate((q_ref, k_ref, v_ref)):
            block = ref[:, h * HEAD : (h + 1) * HEAD]
            if part == 2:
                block = jnp.dot(block, turn, preferred_element_type=F32)
            block = jnp.concatenate([block.astype(F32), jnp.zeros((16, HEAD), F32)], axis=0)
            for r, (start, length) in enumerate(zip(STARTS, LENGTHS)):
                piece = jnp.where(row < length, block[start : start + SLOT], 0.0)
                if part == 0:
                    piece = jnp.where(row == ID_ROW, id_rows[r], piece)
                    piece = jnp.where(row == ID_ROW + 1, every, piece)
                out_ref[PARTS * h + r, part * SLOT : (part + 1) * SLOT, :] = piece.astype(BF16)
    out_ref[PARTS * HEADS_HERE] = jnp.zeros((3 * SLOT, HEAD), BF16)


def attend(third_ref, q_ref, kv0_ref, kv1_ref, kv2_ref, kcode_ref, out_ref):
    rows = Z * SLOT
    third = third_ref[0]
    order = [third, lax.rem(third + 2, PARTS), lax.rem(third + 1, PARTS)]
    key_codes = [kcode_ref[pl.ds(j, 1), :] for j in order]
    keys = [ref[:, :SLOT, :].reshape(rows, HEAD) for ref in (kv0_ref, kv1_ref, kv2_ref)]
    ones = jnp.ones((rows, HEAD), BF16)
    vals = [
        jnp.concatenate([ref[:, SLOT:, :].reshape(rows, HEAD), ones], axis=1)
        for ref in (kv0_ref, kv1_ref, kv2_ref)
    ]
    tile = 16
    at = ID_ROW % tile
    ids = jnp.concatenate(
        [
            q_ref[x, z * SLOT + ID_ROW - at : z * SLOT + ID_ROW - at + tile, :].astype(F32)[at : at + 1]
            for x in range(X)
            for z in range(Z)
        ],
        axis=0,
    )
    which = lax.broadcasted_iota(jnp.int32, (X * Z, HEAD), 0)
    home = (X * (which % Z) + which // Z) * TOK + third * STARTS[1]
    first = ids * POSITIONS
    last = first + (home + lax.broadcasted_iota(jnp.int32, (X * Z, HEAD), 1)).astype(F32)
    codes = jnp.concatenate([first, last], axis=0).T
    lane = lax.broadcasted_iota(jnp.int32, (SLOT, HEAD), 1)
    stats = [jnp.zeros((SLOT, HEAD), F32) for _ in range(X)]
    group = 4
    for g in range(Z // group):
        count = -(-(g + 1) * group * SLOT // HEAD) * HEAD
        zs = range(g * group, (g + 1) * group)
        for x in range(X):
            low_code = jnp.concatenate([codes[:SLOT, x * Z + z : x * Z + z + 1] for z in zs], axis=0)
            high_code = jnp.concatenate(
                [codes[:SLOT, (X + x) * Z + z : (X + x) * Z + z + 1] for z in zs], axis=0
            )
            query = q_ref[x, g * group * SLOT : (g + 1) * group * SLOT, :]
            scores = []
            for j in range(PARTS):
                score = lax.dot_general(
                    query, keys[j][:count], (((1,), (1,)), ((), ())), preferred_element_type=F32
                ) * (HEAD ** (-0.5) * LOG2E)
                key_code = key_codes[j][:, :count]
                allowed = (key_code <= high_code) & (key_code >= low_code)
                scores.append(jnp.where(allowed, score, BLOCKED))
            peak = functools.reduce(jnp.maximum, [jnp.max(s, axis=1, keepdims=True) for s in scores])
            output = jnp.zeros((group * SLOT, 2 * HEAD), F32)
            for j in range(PARTS):
                expo = jnp.exp2(scores[j] - peak)
                output = output + jnp.dot(
                    expo.astype(BF16), vals[j][:count], preferred_element_type=F32
                )
            out_ref[x, g * group * SLOT : (g + 1) * group * SLOT, :] = (
                output[:, :HEAD] / output[:, HEAD:]
            ).astype(BF16)
            logsum = peak + jnp.log2(output[:, HEAD : HEAD + 1])
            high = logsum.astype(BF16).astype(F32)
            rest = logsum - high
            middle = rest.astype(BF16).astype(F32)
            low = rest - middle
            for n in range(group):
                for part, column in enumerate((high, middle, low)):
                    stats[x] = jnp.where(
                        lane == part * Z + g * group + n, column[n * SLOT : (n + 1) * SLOT], stats[x]
                    )
    for x in range(X):
        out_ref[x, rows:, :] = stats[x].astype(BF16)


def join(part_ref, out_ref):
    rows = Z * SLOT
    sums = []
    for x in range(X):
        stat = part_ref[x, rows:, :].astype(F32)
        sums.append(stat + pltpu.roll(stat, HEAD - Z, 1) + pltpu.roll(stat, HEAD - 2 * Z, 1))
    peak = functools.reduce(jnp.maximum, sums)
    weights = [jnp.exp2(s - peak) for s in sums]
    total = functools.reduce(jnp.add, weights)
    weights = [w / total for w in weights]
    share = lax.broadcasted_iota(jnp.int32, (16, HEAD), 1) // SHARE
    for z in range(Z):
        joined = functools.reduce(
            jnp.add,
            [
                weights[x][:, z : z + 1] * part_ref[x, z * SLOT : (z + 1) * SLOT, :].astype(F32)
                for x in range(X)
            ],
        )
        for x in range(X):
            slot = jnp.zeros((16, HEAD), F32)
            for n in range(SLOT // 16):
                piece = joined[16 * n : 16 * (n + 1)]
                if n != x:
                    piece = pltpu.roll(piece, (SHARE * (n - x)) % HEAD, 1)
                slot = jnp.where(share == n, piece, slot)
            out_ref[X * z + x] = slot.astype(BF16)


def assemble(part_ref, out_ref):
    share = lax.broadcasted_iota(jnp.int32, (16, HEAD), 1) // SHARE
    pieces = SLOT // 16
    for x in range(X):
        for r in range(PARTS):
            came = [part_ref[(PARTS * h + r) * X + x] for h in range(HEADS_HERE)]
            wide = [c.astype(F32) for c in came[:4]]
            for n in range(pieces):
                block = jnp.zeros((16, HEAD), F32)
                for h in range(4):
                    piece = wide[h] if h == n else pltpu.roll(wide[h], (SHARE * (h - n)) % HEAD, 1)
                    block = jnp.where(share == h, piece, block)
                first = ((x * PARTS + r) * pieces + n) * 16
                for y in range(Y):
                    out_ref[y, first : first + 16, :] = block.astype(BF16)
            first = X * PARTS * SLOT + (x * PARTS + r) * 16
            for y in range(Y):
                out_ref[y, first : first + 16, :] = came[4]


def project(core_ref, mine_ref, other_ref, weight_ref, out_ref):
    core = core_ref[0]
    depth = HEADS_HERE * SHARE
    pieces = SLOT // 16
    share = lax.broadcasted_iota(jnp.int32, (16, HEAD), 1) // SHARE
    weights = []
    for y in range(Y):
        for which in (core, 1 - core):
            first = pl.multiple_of((C * y + which) * depth, SHARE)
            fifth = weight_ref[pl.ds(first + HEAD, SHARE), :]
            weights += [weight_ref[pl.ds(first, HEAD), :]] + [fifth] * (HEAD // SHARE)
    weights = jnp.concatenate(weights, axis=0)
    for x in range(X):
        span = PARTS * SLOT
        inputs = []
        for y in range(Y):
            for ref in (mine_ref, other_ref):
                inputs.append(ref[y, x * span : (x + 1) * span, :])
                blocks = []
                for r in range(PARTS):
                    first = X * span + (x * PARTS + r) * 16
                    block = ref[y, first : first + 16, :].astype(F32)
                    blocks += [jnp.where(share == n, block, 0.0) for n in range(pieces)]
                inputs.append(jnp.concatenate(blocks, axis=0).astype(BF16))
        total = jnp.dot(jnp.concatenate(inputs, axis=1), weights, preferred_element_type=F32)
        total = [total[r * SLOT : r * SLOT + length] for r, length in enumerate(LENGTHS)]
        out_ref[x] = jnp.concatenate(total, axis=0).astype(BF16)


def share_rows(out_weight, side):
    width = out_weight.shape[1]
    own = out_weight.reshape(X + 1, GRANULE, width)
    ring = jnp.concatenate([own[:X], own[:X]], axis=0)
    came = lax.all_to_all(lax.dynamic_slice_in_dim(ring, X - side, X, axis=0), "x", 0, 0, tiled=True)
    place = jnp.arange(X + 1, dtype=jnp.int32)[:, None, None]
    earlier = jnp.concatenate([came, came[X - 1 :]], axis=0)
    later = jnp.concatenate([came[:1], came], axis=0)
    rows = jnp.where(place <= side, earlier, jnp.where(place == side + 1, own[X:], later))
    return rows.reshape((X + 1) * GRANULE, width)


def local(queries, keys_in, values, cluster_ids, out_weight):
    plane, side, core = lax.axis_index("z"), lax.axis_index("x"), lax.axis_index("c")
    third = lax.rem(plane, PARTS)
    width = out_weight.shape[1]

    send = vmem_call(
        scatter_heads,
        8,
        (Z, 3 * SLOT, HEAD),
        queries,
        keys_in,
        values,
        cluster_ids.reshape(1, TOK),
    )
    here = lax.all_to_all(send, "z", 0, 0, tiled=True)
    rows = share_rows(out_weight, side)
    here, rows = lax.optimization_barrier((here, rows))
    weight = lax.all_gather(rows, "z", axis=0, tiled=True)
    kv = here[:, SLOT:, :]
    turns = [
        [(PARTS * h + r, PARTS * h + (r + k) % PARTS) for h in range(HEADS_HERE) for r in range(PARTS)]
        for k in (1, 2)
    ]
    kv_others = [lax.ppermute(kv, "z", turn) for turn in turns]
    query = here[:, :SLOT, :].reshape(1, Z * SLOT, HEAD)
    query = lax.all_to_all(jnp.broadcast_to(query, (X, Z * SLOT, HEAD)), "x", 0, 0, tiled=True)

    home = (X * jnp.arange(Z, dtype=jnp.int32) + side) * TOK
    key_code = here[:, ID_ROW + 1, :].astype(F32) * POSITIONS + (
        home[:, None] + jnp.arange(HEAD, dtype=jnp.int32)[None, :]
    ).astype(F32)
    key_code = jnp.stack(
        [
            jnp.pad(
                key_code[:, start : start + length], ((0, 0), (0, SLOT - length)), constant_values=NEVER
            ).reshape(Z * SLOT)
            for start, length in zip(STARTS, LENGTHS)
        ]
    )
    part = vmem_call(
        attend,
        32,
        (X, (Z + 1) * SLOT, HEAD),
        query,
        kv,
        kv_others[0],
        kv_others[1],
        key_code,
        scalars=third.reshape(1),
    )
    part = lax.all_to_all(part, "x", 0, 0, tiled=True)
    joined = vmem_call(join, 8, (Z * X, 16, HEAD), part)
    joined = lax.all_to_all(joined, ("z", "x"), 0, 0, tiled=True)
    packed = vmem_call(assemble, 8, (Y, X * PARTS * (SLOT + 16), HEAD), joined)
    packed = lax.all_to_all(packed, "y", 0, 0, tiled=True)
    others = lax.ppermute(packed, "c", [(0, 1), (1, 0)])
    partial = vmem_call(
        project, 24, (X, TOK, width), packed, others, weight, scalars=core.reshape(1)
    )
    partial = lax.all_to_all(partial, "x", 0, 0, tiled=True)
    return jnp.sum(partial.astype(F32), axis=0).astype(BF16)


def solution(mesh):
    fine = Mesh(mesh.devices.reshape(Z, X, Y, C), ("z", "x", "y", "c"))
    both = P(("z", "x"), ("y", "c"))
    return jax.shard_map(
        local,
        mesh=fine,
        in_specs=(both, both, both, P(("z", "x"), None), both),
        out_specs=both,
        check_vma=False,
    )
```

time: 200 us -> 195 us (0.975)
  Pallas kernels: 24.6 us -> 15.3 us
  starting transfers between devices: 33.4 us -> 37.8 us
  blocking collectives: 88.5 us -> 84.9 us
    all_gather x2 -> x0, blocking collectives: 22.6 us -> none  [the longest x1 11.6 us: local(): lax.all_gather(here[:, :SLOT, :].reshape(Z * SLOT, HEAD), 'x', axis=0)]
    all_to_all x2, blocking collectives: 38.7 us -> 59.2 us  [the longest x1 46.4 us: local(): joined = lax.all_to_all(joined, ('z', 'x'), 0, 0, tiled=True)]
    all_to_all x0 -> x2, starting transfers between devices: none -> 9.45 us  [the longest x1 4.84 us: share_rows(): lax.all_to_all(lax.dynamic_slice_in_dim(ring, X - side, X, axis=0), 'x',...]
    pallas_call x5, Pallas kernels: 24.6 us -> 15.3 us  [vmem_call(): pl.pallas_call(body, out_shape=jax.ShapeDtypeStruct(shape, BF16), in_spec...]
    ppermute x1, starting transfers between devices: 10.9 us -> 6.76 us  [local(): others = lax.ppermute(packed, 'c', [(0, 1), (1, 0)])]
    unnamed x10 -> x12, local copies, waits for them, and re-layouts: 0.74 us -> 4.84 us
  transfers between devices with their start and end apart: 5 -> 7, of which waited for: 3 -> 5; matrix products, arithmetic and copies ran while one was open for 3% -> 1% of each run, Pallas kernels for 9% -> 7%
where the time goes in v2:
time: 195 us
  blocking collectives  84.9 us (44%)
  starting transfers between devices  37.8 us (19%)
  waiting for transfers between devices  33.3 us (17%)
  Pallas kernels  15.3 us (8%)
  between operations  13.6 us (7%)
  local copies, waits for them, and re-layouts  7.5 us (4%)
  other arithmetic  2.35 us (1%)
    all_to_all x1, blocking collectives, local(): joined = lax.all_to_all(joined, ('z', 'x'), 0, 0, tiled=True)  46.4 us
    all_to_all x1, waiting for transfers between devices, local(): here = lax.all_to_all(send, 'z', 0, 0, tiled=True)  23.3 us
    pallas_call x5, Pallas kernels, vmem_call(): pl.pallas_call(body, out_shape=jax.ShapeDtypeStruct(shape, BF16), in_spec...  15.3 us
    all_to_all x1, starting transfers between devices, local(): here = lax.all_to_all(send, 'z', 0, 0, tiled=True)  14.9 us
    all_to_all x1, blocking collectives, local(): partial = lax.all_to_all(partial, 'x', 0, 0, tiled=True)  13.3 us
    all_to_all x1, blocking collectives, local(): packed = lax.all_to_all(packed, 'y', 0, 0, tiled=True)  12.8 us
    all_to_all x1, blocking collectives, local(): part = lax.all_to_all(part, 'x', 0, 0, tiled=True)  12.4 us
    ppermute x2, waiting for transfers between devices, local(): kv_others = [lax.ppermute(kv, 'z', turn) for turn in turns]  8 us
  transfers between devices with their start and end apart: 7, of which 5 were waited for; matrix products, arithmetic and copies ran while one was open for 1% of the time, Pallas kernels for 7%

profile of v2, /device:TPU:1, one launch (start us, length us, event | category | flops | bytes accessed | tf_op | source)
XLA Modules:
  0.0 194.7 jit_solution(10524559728200075966)
XLA Ops:
  6.5 0.9 slice.36
  7.4 0.7 fusion.1
  8.1 4.8 %all-to-all-start.1 = ((bf16[4,16,640]{2,1,0:T(8,128)(2,1)}), bf16[4,16,640]{2,1,0:T(8,128)(2,1)S(1)}, u32[]{:S(2)}, u32[]{:S(2)}) async-start(bf16[4,16,640]{2,1,0:T(8,128)(2,1)} %fusion.1), calls=%async_computation.1 | async-start | bytes 163840 | tf_op jit(solution)/shard_map/all_to_all | solution.py:224
  13.0 0.9 copy-done.1
  13.9 0.9 copy-done.2
  14.8 0.9 copy-done.3
  15.7 0.7 copy-done.4
  16.4 1.0 shard_map.55
  17.4 0.1 all-to-all-done.1
  17.5 14.9 %all-to-all-start = ((bf16[16,144,128]{2,1,0:T(8,128)(2,1)}), bf16[16,144,128]{2,1,0:T(8,128)(2,1)S(1)}, u32[]{:S(2)}, u32[]{:S(2)}) async-start(bf16[16,144,128]{2,1,0:T(8,128)(2,1)} %shard_map.55), calls=%async_computation | async-start | bytes 1179648 | tf_op jit(solution)/shard_map/all_to_all | solution.py:246
  32.5 0.1 broadcast_in_dim.48
  32.7 0.1 broadcast_in_dim.45
  32.9 0.7 fusion
  33.6 23.3 %all-to-all-done = bf16[16,144,128]{2,1,0:T(8,128)(2,1)S(1)} async-done(((bf16[16,144,128]{2,1,0:T(8,128)(2,1)}), bf16[16,144,128]{2,1,0:T(8,128)(2,1)S(1)}, u32[]{:S(2)}, u32[]{:S(2)}) %all-to-all-start) | async-done | bytes 589856 | tf_op jit(solution)/shard_map/all_to_all | solution.py:246
  56.9 1.0 broadcast_in_dim.53
  57.9 4.6 %all-to-all-start.2 = ((bf16[4,768,128]{2,1,0:T(8,128)(2,1)}), bf16[4,768,128]{2,1,0:T(8,128)(2,1)S(1)}, u32[]{:S(2)}, u32[]{:S(2)}) async-start(bf16[4,768,128]{2,1,0:T(8,128)(2,1)} %broadcast_in_dim.53), calls=%async_computation.2 | async-start | bytes 1572864 | tf_op jit(solution)/shard_map/all_to_all | solution.py:257
  62.6 4.8 %collective-permute-start = (bf16[16,96,128]{2,1,0:T(8,128)(2,1)S(1)}, bf16[16,96,128]{2,1,0:T(8,128)(2,1)S(1)}, u32[]{:S(2)}, u32[]{:S(2)}) collective-permute-start(bf16[16,96,128]{2,1,0:T(8,128)(2,1)S(1)} %slice.42.kv0_ref), channel_id=1, source_target_pairs={{0,32},{32,64},{64,0},{96,128},{128,160},{160,96},{192,224},{224,2... | collective-permute-start | bytes 1179656 | tf_op jit(solution)/shard_map/ppermute | solution.py:255
  67.3 1.9 collective-permute-start.1
  69.8 2.2 %collective-permute-done.kv1_ref = bf16[16,96,128]{2,1,0:T(8,128)(2,1)S(1)} collective-permute-done((bf16[16,96,128]{2,1,0:T(8,128)(2,1)S(1)}, bf16[16,96,128]{2,1,0:T(8,128)(2,1)S(1)}, u32[]{:S(2)}, u32[]{:S(2)}) %collective-permute-start) | collective-permute-done | bytes 393248 | tf_op jit(solution)/shard_map/ppermute | solution.py:255
  72.0 5.8 %collective-permute-done.1.kv2_ref = bf16[16,96,128]{2,1,0:T(8,128)(2,1)S(1)} collective-permute-done((bf16[16,96,128]{2,1,0:T(8,128)(2,1)S(1)}, bf16[16,96,128]{2,1,0:T(8,128)(2,1)S(1)}, u32[]{:S(2)}, u32[]{:S(2)}) %collective-permute-start.1) | collective-permute-done | bytes 393248 | tf_op jit(solution)/shard_map/ppermute | solution.py:255
  77.8 10.4 %shard_map.56 = bf16[4,816,128]{2,1,0:T(8,128)(2,1)S(1)} custom-call(s32[1]{0:T(128)} %bitcast.1.third_ref, bf16[4,768,128]{2,1,0:T(8,128)(2,1)S(1)} %all-to-all-done.2.q_ref, bf16[16,96,128]{2,1,0:T(8,128)(2,1)S(1)} %slice.42.kv0_ref, bf16[16,96,128]{2,1,0:T(8,128)(2,1)S(1)} %collective-permute-done.kv1_ref, ...), custom_call_target="tpu_custom_call" | custom-call | tf_op jit(solution)/shard_map/pallas_call | solution.py:35
  88.2 12.4 %all_to_all.35.part_ref = bf16[4,816,128]{2,1,0:T(8,128)(2,1)S(1)} all-to-all(bf16[4,816,128]{2,1,0:T(8,128)(2,1)S(1)} %shard_map.56), channel_id=1, replica_groups=mesh['z'=16,'x'=4,'y'=4,'c'=2] {'x'}, dimensions={0} | all-to-all | bytes 1671168 | tf_op jit(solution)/shard_map/all_to_all | solution.py:282
  100.6 1.6 shard_map.57
  102.2 46.4 %all_to_all.36.part_ref = bf16[64,16,128]{2,1,0:T(8,128)(2,1)S(1)} all-to-all(bf16[64,16,128]{2,1,0:T(8,128)(2,1)S(1)} %shard_map.57), channel_id=1, replica_groups=mesh['z'=16,'x'=4,'y'=4,'c'=2] {'z','x'}, dimensions={0} | all-to-all | bytes 524288 | tf_op jit(solution)/shard_map/all_to_all | solution.py:284
  148.6 0.2 shard_map.58
  148.8 12.8 %all_to_all.37.mine_ref = bf16[4,768,128]{2,1,0:T(8,128)(2,1)S(1)} all-to-all(bf16[4,768,128]{2,1,0:T(8,128)(2,1)S(1)} %shard_map.58), channel_id=1, replica_groups=mesh['z'=16,'x'=4,'y'=4,'c'=2] {'y'}, dimensions={0} | all-to-all | bytes 1572864 | tf_op jit(solution)/shard_map/all_to_all | solution.py:286
  161.6 6.8 %collective-permute-start.2 = (bf16[4,768,128]{2,1,0:T(8,128)(2,1)S(1)}, bf16[4,768,128]{2,1,0:T(8,128)(2,1)S(1)}, u32[]{:S(2)}, u32[]{:S(2)}) collective-permute-start(bf16[4,768,128]{2,1,0:T(8,128)(2,1)S(1)} %all_to_all.37.mine_ref), channel_id=1, source_target_pairs={{0,1},{1,0},{2,3},{3,2},{4,5},{5,4},{6,7},{7,6},{8,9},{9,8},{10,11... | collective-permute-start | bytes 2359304 | tf_op jit(solution)/shard_map/ppermute | solution.py:287
  168.4 1.9 collective-permute-done.2.other_ref
  170.3 1.4 copy-done
  171.7 2.1 %shard_map.59 = bf16[4,128,640]{2,1,0:T(8,128)(2,1)S(1)} custom-call(s32[1]{0:T(128)} %bitcast.core_ref, bf16[4,768,128]{2,1,0:T(8,128)(2,1)S(1)} %all_to_all.37.mine_ref, bf16[4,768,128]{2,1,0:T(8,128)(2,1)S(1)} %collective-permute-done.2.other_ref, bf16[1280,640]{1,0:T(8,128)(2,1)S(1)} %copy-done), custom_call_target="tpu_custom_call" | custom-call | tf_op jit(solution)/shard_map/pallas_call | solution.py:35
  173.8 13.3 %all_to_all.38 = bf16[4,128,640]{2,1,0:T(8,128)(2,1)S(1)} all-to-all(bf16[4,128,640]{2,1,0:T(8,128)(2,1)S(1)} %shard_map.59), channel_id=1, replica_groups=mesh['z'=16,'x'=4,'y'=4,'c'=2] {'x'}, dimensions={0} | all-to-all | bytes 1310720 | tf_op jit(solution)/shard_map/all_to_all | solution.py:291
  187.1 0.8 reduce_sum.12
  (33 shorter events, 0.8 us)
Async XLA Ops:
  6.5 26.3 %slice-start = ((bf16[80,640]{1,0:T(8,128)(2,1)}), bf16[16,640]{1,0:T(8,128)(2,1)S(1)}, s32[]{:S(2)}) async-start(bf16[80,640]{1,0:T(8,128)(2,1)} %param.9), calls=%async_computation.8 | async-start | bytes 40960 | tf_op jit(solution)/shard_map/slice | solution.py:228
  8.1 9.4 %all-to-all-start.1 = ((bf16[4,16,640]{2,1,0:T(8,128)(2,1)}), bf16[4,16,640]{2,1,0:T(8,128)(2,1)S(1)}, u32[]{:S(2)}, u32[]{:S(2)}) async-start(bf16[4,16,640]{2,1,0:T(8,128)(2,1)} %fusion.1), calls=%async_computation.1 | async-start | bytes 163840 | tf_op jit(solution)/shard_map/all_to_all | solution.py:224
  13.0 0.9 copy-start.1
  13.9 0.9 copy-start.2
  14.8 0.9 copy-start.3
  15.7 0.7 copy-start.4
  17.5 39.4 %all-to-all-start = ((bf16[16,144,128]{2,1,0:T(8,128)(2,1)}), bf16[16,144,128]{2,1,0:T(8,128)(2,1)S(1)}, u32[]{:S(2)}, u32[]{:S(2)}) async-start(bf16[16,144,128]{2,1,0:T(8,128)(2,1)} %shard_map.55), calls=%async_computation | async-start | bytes 1179648 | tf_op jit(solution)/shard_map/all_to_all | solution.py:246
  56.9 12.8 %copy-start.5 = (pred[48]{0:T(512)(128)(4,1)S(1)}, pred[48]{0:T(512)(128)(4,1)}, u32[]{:S(2)}) copy-start(pred[48]{0:T(512)(128)(4,1)} %constant.33.clone.1) | copy-start | bytes 148
  57.9 19.9 %all-to-all-start.2 = ((bf16[4,768,128]{2,1,0:T(8,128)(2,1)}), bf16[4,768,128]{2,1,0:T(8,128)(2,1)S(1)}, u32[]{:S(2)}, u32[]{:S(2)}) async-start(bf16[4,768,128]{2,1,0:T(8,128)(2,1)} %broadcast_in_dim.53), calls=%async_computation.2 | async-start | bytes 1572864 | tf_op jit(solution)/shard_map/all_to_all | solution.py:257
  62.5 105.9 %all-gather.2.cloned.1.call-start = ((), (), s32[]{:S(2)}) async-start(), calls=%async_computation.7 | async-start | bytes 1740800 | tf_op jit(solution)/shard_map/all_gather | solution.py:249
  62.6 9.5 %collective-permute-start = (bf16[16,96,128]{2,1,0:T(8,128)(2,1)S(1)}, bf16[16,96,128]{2,1,0:T(8,128)(2,1)S(1)}, u32[]{:S(2)}, u32[]{:S(2)}) collective-permute-start(bf16[16,96,128]{2,1,0:T(8,128)(2,1)S(1)} %slice.42.kv0_ref), channel_id=1, source_target_pairs={{0,32},{32,64},{64,0},{96,128},{128,160},{160,96},{192,224},{224,2... | collective-permute-start | bytes 1179656 | tf_op jit(solution)/shard_map/ppermute | solution.py:255
  67.3 10.5 %collective-permute-start.1 = (bf16[16,96,128]{2,1,0:T(8,128)(2,1)S(1)}, bf16[16,96,128]{2,1,0:T(8,128)(2,1)S(1)}, u32[]{:S(2)}, u32[]{:S(2)}) collective-permute-start(bf16[16,96,128]{2,1,0:T(8,128)(2,1)S(1)} %slice.42.kv0_ref), channel_id=1, source_target_pairs={{0,64},{32,0},{64,32},{96,160},{128,96},{160,128},{192,256},{224,1... | collective-permute-start | bytes 1179656 | tf_op jit(solution)/shard_map/ppermute | solution.py:255
  161.6 8.7 %collective-permute-start.2 = (bf16[4,768,128]{2,1,0:T(8,128)(2,1)S(1)}, bf16[4,768,128]{2,1,0:T(8,128)(2,1)S(1)}, u32[]{:S(2)}, u32[]{:S(2)}) collective-permute-start(bf16[4,768,128]{2,1,0:T(8,128)(2,1)S(1)} %all_to_all.37.mine_ref), channel_id=1, source_target_pairs={{0,1},{1,0},{2,3},{3,2},{4,5},{5,4},{6,7},{7,6},{8,9},{9,8},{10,11... | collective-permute-start | bytes 2359304 | tf_op jit(solution)/shard_map/ppermute | solution.py:287
  170.3 1.4 copy-start
Sparse Core Ops, SparseCore 0:
  69.9 73.8 all-gather.1

commit v3 on v2

--- a/solution.py
+++ b/solution.py
@@ -27,16 +27,16 @@
 GRANULE = 16
 
 
-def vmem_call(body, mebibytes, shape, *operands, scalars=None):
+def vmem_call(body, mebibytes, shapes, *operands, scalars=None):
     specs = [pl.BlockSpec(memory_space=pltpu.VMEM)] * len(operands)
     if scalars is not None:
         specs = [pl.BlockSpec(memory_space=pltpu.SMEM)] + specs
         operands = (scalars,) + operands
     return pl.pallas_call(
         body,
-        out_shape=jax.ShapeDtypeStruct(shape, BF16),
+        out_shape=[jax.ShapeDtypeStruct(shape, BF16) for shape in shapes],
         in_specs=specs,
-        out_specs=pl.BlockSpec(memory_space=pltpu.VMEM),
+        out_specs=[pl.BlockSpec(memory_space=pltpu.VMEM)] * len(shapes),
         compiler_params=pltpu.CompilerParams(vmem_limit_bytes=mebibytes * 1024 * 1024),
     )(*operands)
 
@@ -64,7 +64,8 @@
                 piece = jnp.where(row < length, block[start : start + SLOT], 0.0)
                 if part == 0:
                     piece = jnp.where(row == ID_ROW, id_rows[r], piece)
-                    piece = jnp.where(row == ID_ROW + 1, every, piece)
+                elif part == 1:
+                    piece = jnp.where(row == ID_ROW, every, piece)
                 out_ref[PARTS * h + r, part * SLOT : (part + 1) * SLOT, :] = piece.astype(BF16)
     out_ref[PARTS * HEADS_HERE] = jnp.zeros((3 * SLOT, HEAD), BF16)
 
@@ -96,11 +97,13 @@
     last = first + (home + lax.broadcasted_iota(jnp.int32, (X * Z, HEAD), 1)).astype(F32)
     codes = jnp.concatenate([first, last], axis=0).T
     lane = lax.broadcasted_iota(jnp.int32, (SLOT, HEAD), 1)
-    stats = [jnp.zeros((SLOT, HEAD), F32) for _ in range(X)]
+    stats = [jnp.zeros((SLOT, HEAD), F32) for _ in range(2)]
     group = 4
+    share = lax.broadcasted_iota(jnp.int32, (group * SLOT, HEAD), 1) // SHARE
     for g in range(Z // group):
         count = -(-(g + 1) * group * SLOT // HEAD) * HEAD
         zs = range(g * group, (g + 1) * group)
+        slots = [jnp.zeros((group * SLOT, HEAD), F32) for _ in range(X)]
         for x in range(X):
             low_code = jnp.concatenate([codes[:SLOT, x * Z + z : x * Z + z + 1] for z in zs], axis=0)
             high_code = jnp.concatenate(
@@ -122,9 +125,10 @@
                 output = output + jnp.dot(
                     expo.astype(BF16), vals[j][:count], preferred_element_type=F32
                 )
-            out_ref[x, g * group * SLOT : (g + 1) * group * SLOT, :] = (
-                output[:, :HEAD] / output[:, HEAD:]
-            ).astype(BF16)
+            normal = output[:, :HEAD] / output[:, HEAD:]
+            for to in range(X):
+                piece = normal if to == x else pltpu.roll(normal, (SHARE * (x - to)) % HEAD, 1)
+                slots[to] = jnp.where(share == x, piece, slots[to])
             logsum = peak + jnp.log2(output[:, HEAD : HEAD + 1])
             high = logsum.astype(BF16).astype(F32)
             rest = logsum - high
@@ -132,67 +136,64 @@
             low = rest - middle
             for n in range(group):
                 for part, column in enumerate((high, middle, low)):
-                    stats[x] = jnp.where(
-                        lane == part * Z + g * group + n, column[n * SLOT : (n + 1) * SLOT], stats[x]
+                    at = part * X * Z + x * Z + g * group + n
+                    stats[at // HEAD] = jnp.where(
+                        lane == at % HEAD, column[n * SLOT : (n + 1) * SLOT], stats[at // HEAD]
                     )
+        for x in range(X):
+            out_ref[x, g * group * SLOT : (g + 1) * group * SLOT, :] = slots[x].astype(BF16)
     for x in range(X):
-        out_ref[x, rows:, :] = stats[x].astype(BF16)
+        out_ref[x, rows : rows + SLOT, :] = stats[0].astype(BF16)
+        out_ref[x, rows + SLOT :, :] = stats[1].astype(BF16)
 
 
 def join(part_ref, out_ref):
     rows = Z * SLOT
     sums = []
     for x in range(X):
-        stat = part_ref[x, rows:, :].astype(F32)
-        sums.append(stat + pltpu.roll(stat, HEAD - Z, 1) + pltpu.roll(stat, HEAD - 2 * Z, 1))
+        stat = part_ref[x, rows : rows + SLOT, :].astype(F32)
+        rest = part_ref[x, rows + SLOT :, :].astype(F32)
+        sums.append(stat + pltpu.roll(stat, HEAD // 2, 1) + rest)
     peak = functools.reduce(jnp.maximum, sums)
     weights = [jnp.exp2(s - peak) for s in sums]
     total = functools.reduce(jnp.add, weights)
     weights = [w / total for w in weights]
-    share = lax.broadcasted_iota(jnp.int32, (16, HEAD), 1) // SHARE
+    share = lax.broadcasted_iota(jnp.int32, (SLOT, HEAD), 1) // SHARE
     for z in range(Z):
         joined = functools.reduce(
             jnp.add,
             [
-                weights[x][:, z : z + 1] * part_ref[x, z * SLOT : (z + 1) * SLOT, :].astype(F32)
+                jnp.take_along_axis(weights[x], share * Z + z, axis=1)
+                * part_ref[x, z * SLOT : (z + 1) * SLOT, :].astype(F32)
                 for x in range(X)
             ],
         )
+        out_ref[z] = joined.astype(BF16)
+
+
+def assemble(part_ref, out_ref):
+    share = lax.broadcasted_iota(jnp.int32, (SLOT, HEAD), 1) // SHARE
+    for r in range(PARTS):
+        came = [part_ref[PARTS * h + r] for h in range(HEADS_HERE)]
+        wide = [c.astype(F32) for c in came[:4]]
         for x in range(X):
-            slot = jnp.zeros((16, HEAD), F32)
-            for n in range(SLOT // 16):
-                piece = joined[16 * n : 16 * (n + 1)]
-                if n != x:
-                    piece = pltpu.roll(piece, (SHARE * (n - x)) % HEAD, 1)
-                slot = jnp.where(share == n, piece, slot)
-            out_ref[X * z + x] = slot.astype(BF16)
-
-
-def assemble(part_ref, out_ref):
-    share = lax.broadcasted_iota(jnp.int32, (16, HEAD), 1) // SHARE
-    pieces = SLOT // 16
-    for x in range(X):
-        for r in range(PARTS):
-            came = [part_ref[(PARTS * h + r) * X + x] for h in range(HEADS_HERE)]
-            wide = [c.astype(F32) for c in came[:4]]
-            for n in range(pieces):
-                block = jnp.zeros((16, HEAD), F32)
-                for h in range(4):
-                    piece = wide[h] if h == n else pltpu.roll(wide[h], (SHARE * (h - n)) % HEAD, 1)
-                    block = jnp.where(share == h, piece, block)
-                first = ((x * PARTS + r) * pieces + n) * 16
-                for y in range(Y):
-                    out_ref[y, first : first + 16, :] = block.astype(BF16)
-            first = X * PARTS * SLOT + (x * PARTS + r) * 16
+            block = jnp.zeros((SLOT, HEAD), F32)
+            for h in range(4):
+                piece = wide[h] if h == x else pltpu.roll(wide[h], (SHARE * (h - x)) % HEAD, 1)
+                block = jnp.where(share == h, piece, block)
+            first = (x * PARTS + r) * SLOT
             for y in range(Y):
-                out_ref[y, first : first + 16, :] = came[4]
+                out_ref[y, first : first + SLOT, :] = block.astype(BF16)
+        first = (X * PARTS + r) * SLOT
+        for y in range(Y):
+            out_ref[y, first : first + SLOT, :] = came[4]
 
 
 def project(core_ref, mine_ref, other_ref, weight_ref, out_ref):
     core = core_ref[0]
     depth = HEADS_HERE * SHARE
-    pieces = SLOT // 16
-    share = lax.broadcasted_iota(jnp.int32, (16, HEAD), 1) // SHARE
+    span = PARTS * SLOT
+    share = lax.broadcasted_iota(jnp.int32, (span, HEAD), 1) // SHARE
     weights = []
     for y in range(Y):
         for which in (core, 1 - core):
@@ -201,17 +202,12 @@
             weights += [weight_ref[pl.ds(first, HEAD), :]] + [fifth] * (HEAD // SHARE)
     weights = jnp.concatenate(weights, axis=0)
     for x in range(X):
-        span = PARTS * SLOT
         inputs = []
         for y in range(Y):
             for ref in (mine_ref, other_ref):
                 inputs.append(ref[y, x * span : (x + 1) * span, :])
-                blocks = []
-                for r in range(PARTS):
-                    first = X * span + (x * PARTS + r) * 16
-                    block = ref[y, first : first + 16, :].astype(F32)
-                    blocks += [jnp.where(share == n, block, 0.0) for n in range(pieces)]
-                inputs.append(jnp.concatenate(blocks, axis=0).astype(BF16))
+                fifth = ref[y, X * span :, :].astype(F32)
+                inputs.append(jnp.where(share == x, fifth, 0.0).astype(BF16))
         total = jnp.dot(jnp.concatenate(inputs, axis=1), weights, preferred_element_type=F32)
         total = [total[r * SLOT : r * SLOT + length] for r, length in enumerate(LENGTHS)]
         out_ref[x] = jnp.concatenate(total, axis=0).astype(BF16)
@@ -234,30 +230,28 @@
     third = lax.rem(plane, PARTS)
     width = out_weight.shape[1]
 
-    send = vmem_call(
+    (send,) = vmem_call(
         scatter_heads,
-        8,
-        (Z, 3 * SLOT, HEAD),
+        56,
+        [(Z, 3 * SLOT, HEAD)],
         queries,
         keys_in,
         values,
         cluster_ids.reshape(1, TOK),
     )
+    weight = lax.all_gather(share_rows(out_weight, side), "z", axis=0, tiled=True)
     here = lax.all_to_all(send, "z", 0, 0, tiled=True)
-    rows = share_rows(out_weight, side)
-    here, rows = lax.optimization_barrier((here, rows))
-    weight = lax.all_gather(rows, "z", axis=0, tiled=True)
     kv = here[:, SLOT:, :]
     turns = [
         [(PARTS * h + r, PARTS * h + (r + k) % PARTS) for h in range(HEADS_HERE) for r in range(PARTS)]
         for k in (1, 2)
     ]
     kv_others = [lax.ppermute(kv, "z", turn) for turn in turns]
-    query = here[:, :SLOT, :].reshape(1, Z * SLOT, HEAD)
-    query = lax.all_to_all(jnp.broadcast_to(query, (X, Z * SLOT, HEAD)), "x", 0, 0, tiled=True)
+    query = jnp.broadcast_to(here[:, :SLOT, :].reshape(1, Z * SLOT, HEAD), (X, Z * SLOT, HEAD))
+    query = lax.all_to_all(query, "x", 0, 0, tiled=True)
 
     home = (X * jnp.arange(Z, dtype=jnp.int32) + side) * TOK
-    key_code = here[:, ID_ROW + 1, :].astype(F32) * POSITIONS + (
+    key_code = kv[:, ID_ROW, :].astype(F32) * POSITIONS + (
         home[:, None] + jnp.arange(HEAD, dtype=jnp.int32)[None, :]
     ).astype(F32)
     key_code = jnp.stack(
@@ -268,10 +262,10 @@
             for start, length in zip(STARTS, LENGTHS)
         ]
     )
-    part = vmem_call(
+    (part,) = vmem_call(
         attend,
         32,
-        (X, (Z + 1) * SLOT, HEAD),
+        [(X, (Z + 2) * SLOT, HEAD)],
         query,
         kv,
         kv_others[0],
@@ -280,13 +274,13 @@
         scalars=third.reshape(1),
     )
     part = lax.all_to_all(part, "x", 0, 0, tiled=True)
-    joined = vmem_call(join, 8, (Z * X, 16, HEAD), part)
-    joined = lax.all_to_all(joined, ("z", "x"), 0, 0, tiled=True)
-    packed = vmem_call(assemble, 8, (Y, X * PARTS * (SLOT + 16), HEAD), joined)
+    (joined,) = vmem_call(join, 8, [(Z, SLOT, HEAD)], part)
+    joined = lax.all_to_all(joined, "z", 0, 0, tiled=True)
+    (packed,) = vmem_call(assemble, 8, [(Y, (X + 1) * PARTS * SLOT, HEAD)], joined)
     packed = lax.all_to_all(packed, "y", 0, 0, tiled=True)
     others = lax.ppermute(packed, "c", [(0, 1), (1, 0)])
-    partial = vmem_call(
-        project, 24, (X, TOK, width), packed, others, weight, scalars=core.reshape(1)
+    (partial,) = vmem_call(
+        project, 24, [(X, TOK, width)], packed, others, weight, scalars=core.reshape(1)
     )
     partial = lax.all_to_all(partial, "x", 0, 0, tiled=True)
     return jnp.sum(partial.astype(F32), axis=0).astype(BF16)

time: 195 us -> 186 us (0.954)
  blocking collectives: 84.9 us -> 67 us
  waiting for transfers between devices: 33.3 us -> 43.5 us
  local copies, waits for them, and re-layouts: 7.5 us -> 4.09 us
    all_to_all x1, blocking collectives: 46.4 us -> 28.7 us  [local(): joined = lax.all_to_all(joined, 'z', 0, 0, tiled=True)]
    ppermute x2, waiting for transfers between devices: 8 us -> 16 us  [local(): kv_others = [lax.ppermute(kv, 'z', turn) for turn in turns]]
    unnamed x12 -> x4, local copies, waits for them, and re-layouts: 4.84 us -> 1.44 us
    all_to_all x1, waiting for transfers between devices: 0.13 us -> 2.46 us  [share_rows(): lax.all_to_all(lax.dynamic_slice_in_dim(ring, X - side, X, axis=0), 'x',...]
where the time goes in v3:
time: 186 us; the launch traced here: 185 us
  blocking collectives  67 us (36%)
  waiting for transfers between devices  43.5 us (23%)
  starting transfers between devices  38.9 us (21%)
  Pallas kernels  15.7 us (8%)
  between operations  13.6 us (7%)
  local copies, waits for them, and re-layouts  4.09 us (2%)
  other arithmetic  2.35 us (1%)
    all_to_all x1, blocking collectives, local(): joined = lax.all_to_all(joined, 'z', 0, 0, tiled=True)  28.7 us
    all_to_all x1, waiting for transfers between devices, local(): here = lax.all_to_all(send, 'z', 0, 0, tiled=True)  23.2 us
    ppermute x2, waiting for transfers between devices, local(): kv_others = [lax.ppermute(kv, 'z', turn) for turn in turns]  16 us
    pallas_call x5, Pallas kernels, vmem_call(): pl.pallas_call(body, out_shape=[jax.ShapeDtypeStruct(shape, BF16) for sha...  15.7 us
    all_to_all x1, starting transfers between devices, local(): here = lax.all_to_all(send, 'z', 0, 0, tiled=True)  14.9 us
    all_to_all x1, blocking collectives, local(): part = lax.all_to_all(part, 'x', 0, 0, tiled=True)  13.3 us
    all_to_all x1, blocking collectives, local(): partial = lax.all_to_all(partial, 'x', 0, 0, tiled=True)  13.1 us
    all_to_all x1, blocking collectives, local(): packed = lax.all_to_all(packed, 'y', 0, 0, tiled=True)  12 us
  transfers between devices with their start and end apart: 7, of which 5 were waited for; matrix products, arithmetic and copies ran while one was open for 1% of the time, Pallas kernels for 7%

profile of v3, /device:TPU:1, one launch (start us, length us, event | category | flops | bytes accessed | tf_op | source)
XLA Modules:
  0.0 185.0 jit_solution(3707973680101545414)
XLA Ops:
  6.5 0.9 slice.43
  7.4 0.7 fusion.1
  8.1 4.8 %all-to-all-start.5 = ((bf16[4,16,640]{2,1,0:T(8,128)(2,1)}), bf16[4,16,640]{2,1,0:T(8,128)(2,1)S(1)}, u32[]{:S(2)}, u32[]{:S(2)}) async-start(bf16[4,16,640]{2,1,0:T(8,128)(2,1)} %fusion.1), calls=%async_computation.5 | async-start | bytes 163840 | tf_op jit(solution)/shard_map/all_to_all | solution.py:220
  13.0 2.1 %shard_map.55 = bf16[16,144,128]{2,1,0:T(8,128)(2,1)} custom-call(bf16[128,640]{1,0:T(8,128)(2,1)} %q_ref.1, bf16[128,640]{1,0:T(8,128)(2,1)} %k_ref.1, bf16[128,640]{1,0:T(8,128)(2,1)} %v_ref.1, s32[1,128]{1,0:T(1,128)} %bitcast.17), custom_call_target="tpu_custom_call" | custom-call | tf_op jit(solution)/shard_map/pallas_call | solution.py:35
  15.1 2.5 %all-to-all-done.5 = bf16[4,16,640]{2,1,0:T(8,128)(2,1)S(1)} async-done(((bf16[4,16,640]{2,1,0:T(8,128)(2,1)}), bf16[4,16,640]{2,1,0:T(8,128)(2,1)S(1)}, u32[]{:S(2)}, u32[]{:S(2)}) %all-to-all-start.5) | async-done | bytes 81952 | tf_op jit(solution)/shard_map/all_to_all | solution.py:220
  17.5 14.9 %all-to-all-start = ((bf16[16,144,128]{2,1,0:T(8,128)(2,1)}), bf16[16,144,128]{2,1,0:T(8,128)(2,1)S(1)}, u32[]{:S(2)}, u32[]{:S(2)}) async-start(bf16[16,144,128]{2,1,0:T(8,128)(2,1)} %shard_map.55), calls=%async_computation | async-start | bytes 1179648 | tf_op jit(solution)/shard_map/all_to_all | solution.py:243
  32.6 0.1 broadcast_in_dim.50
  32.7 0.1 broadcast_in_dim.46
  32.8 0.1 broadcast_in_dim.47
  32.9 0.7 fusion
  33.7 23.2 %all-to-all-done = bf16[16,144,128]{2,1,0:T(8,128)(2,1)S(1)} async-done(((bf16[16,144,128]{2,1,0:T(8,128)(2,1)}), bf16[16,144,128]{2,1,0:T(8,128)(2,1)S(1)}, u32[]{:S(2)}, u32[]{:S(2)}) %all-to-all-start) | async-done | bytes 589856 | tf_op jit(solution)/shard_map/all_to_all | solution.py:243
  56.9 5.0 %collective-permute-start = (bf16[16,96,128]{2,1,0:T(8,128)(2,1)S(1)}, bf16[16,96,128]{2,1,0:T(8,128)(2,1)S(1)}, u32[]{:S(2)}, u32[]{:S(2)}) collective-permute-start(bf16[16,96,128]{2,1,0:T(8,128)(2,1)S(1)} %slice.49.kv0_ref), channel_id=1, source_target_pairs={{0,32},{32,64},{64,0},{96,128},{128,160},{160,96},{192,224},{224,2... | collective-permute-start | bytes 1179656 | tf_op jit(solution)/shard_map/ppermute | solution.py:249
  62.0 1.9 %collective-permute-start.1 = (bf16[16,96,128]{2,1,0:T(8,128)(2,1)S(1)}, bf16[16,96,128]{2,1,0:T(8,128)(2,1)S(1)}, u32[]{:S(2)}, u32[]{:S(2)}) collective-permute-start(bf16[16,96,128]{2,1,0:T(8,128)(2,1)S(1)} %slice.49.kv0_ref), channel_id=1, source_target_pairs={{0,64},{32,0},{64,32},{96,160},{128,96},{160,128},{192,256},{224,1... | collective-permute-start | bytes 1179656 | tf_op jit(solution)/shard_map/ppermute | solution.py:249
  63.9 1.0 broadcast_in_dim.45
  64.9 3.5 %all-to-all-start.1 = ((bf16[4,768,128]{2,1,0:T(8,128)(2,1)}), bf16[4,768,128]{2,1,0:T(8,128)(2,1)S(1)}, u32[]{:S(2)}, u32[]{:S(2)}) async-start(bf16[4,768,128]{2,1,0:T(8,128)(2,1)} %broadcast_in_dim.45), calls=%async_computation.1 | async-start | bytes 1572864 | tf_op jit(solution)/shard_map/all_to_all | solution.py:251
  68.6 0.1 stack_reshape.11
  68.8 0.1 stack_reshape.10
  68.9 0.1 stack_reshape.9
  69.0 0.5 collective-permute-done.kv1_ref
  69.4 15.5 %collective-permute-done.1.kv2_ref = bf16[16,96,128]{2,1,0:T(8,128)(2,1)S(1)} collective-permute-done((bf16[16,96,128]{2,1,0:T(8,128)(2,1)S(1)}, bf16[16,96,128]{2,1,0:T(8,128)(2,1)S(1)}, u32[]{:S(2)}, u32[]{:S(2)}) %collective-permute-start.1) | collective-permute-done | bytes 393248 | tf_op jit(solution)/shard_map/ppermute | solution.py:249
  84.9 10.7 %shard_map.56 = bf16[4,864,128]{2,1,0:T(8,128)(2,1)S(1)} custom-call(s32[1]{0:T(128)} %bitcast.1.third_ref, bf16[4,768,128]{2,1,0:T(8,128)(2,1)S(1)} %all-to-all-done.1.q_ref, bf16[16,96,128]{2,1,0:T(8,128)(2,1)S(1)} %slice.49.kv0_ref, bf16[16,96,128]{2,1,0:T(8,128)(2,1)S(1)} %collective-permute-done.kv1_ref, ...), custom_call_target="tpu_custom_call" | custom-call | tf_op jit(solution)/shard_map/pallas_call | solution.py:35
  95.7 13.3 %all_to_all.35.part_ref = bf16[4,864,128]{2,1,0:T(8,128)(2,1)S(1)} all-to-all(bf16[4,864,128]{2,1,0:T(8,128)(2,1)S(1)} %shard_map.56), channel_id=1, replica_groups=mesh['z'=16,'x'=4,'y'=4,'c'=2] {'x'}, dimensions={0} | all-to-all | bytes 1769472 | tf_op jit(solution)/shard_map/all_to_all | solution.py:276
  108.9 0.6 shard_map.57
  109.6 28.7 %all_to_all.36.part_ref = bf16[16,48,128]{2,1,0:T(8,128)(2,1)S(1)} all-to-all(bf16[16,48,128]{2,1,0:T(8,128)(2,1)S(1)} %shard_map.57), channel_id=1, replica_groups=mesh['z'=16,'x'=4,'y'=4,'c'=2] {'z'}, dimensions={0} | all-to-all | bytes 393216 | tf_op jit(solution)/shard_map/all_to_all | solution.py:278
  138.2 0.2 shard_map.58
  138.4 12.0 %all_to_all.37.mine_ref = bf16[4,720,128]{2,1,0:T(8,128)(2,1)S(1)} all-to-all(bf16[4,720,128]{2,1,0:T(8,128)(2,1)S(1)} %shard_map.58), channel_id=1, replica_groups=mesh['z'=16,'x'=4,'y'=4,'c'=2] {'y'}, dimensions={0} | all-to-all | bytes 1474560 | tf_op jit(solution)/shard_map/all_to_all | solution.py:280
  150.4 8.6 %collective-permute-start.2 = (bf16[4,720,128]{2,1,0:T(8,128)(2,1)S(1)}, bf16[4,720,128]{2,1,0:T(8,128)(2,1)S(1)}, u32[]{:S(2)}, u32[]{:S(2)}) collective-permute-start(bf16[4,720,128]{2,1,0:T(8,128)(2,1)S(1)} %all_to_all.37.mine_ref), channel_id=1, source_target_pairs={{0,1},{1,0},{2,3},{3,2},{4,5},{5,4},{6,7},{7,6},{8,9},{9,8},{10,11... | collective-permute-start | bytes 2211848 | tf_op jit(solution)/shard_map/ppermute | solution.py:281
  159.1 1.8 collective-permute-done.2.other_ref
  160.9 1.4 copy-done
  162.3 2.0 %shard_map.59 = bf16[4,128,640]{2,1,0:T(8,128)(2,1)S(1)} custom-call(s32[1]{0:T(128)} %bitcast.core_ref, bf16[4,720,128]{2,1,0:T(8,128)(2,1)S(1)} %all_to_all.37.mine_ref, bf16[4,720,128]{2,1,0:T(8,128)(2,1)S(1)} %collective-permute-done.2.other_ref, bf16[1280,640]{1,0:T(8,128)(2,1)S(1)} %copy-done), custom_call_target="tpu_custom_call" | custom-call | tf_op jit(solution)/shard_map/pallas_call | solution.py:35
  164.4 13.1 %all_to_all.38 = bf16[4,128,640]{2,1,0:T(8,128)(2,1)S(1)} all-to-all(bf16[4,128,640]{2,1,0:T(8,128)(2,1)S(1)} %shard_map.59), channel_id=1, replica_groups=mesh['z'=16,'x'=4,'y'=4,'c'=2] {'x'}, dimensions={0} | all-to-all | bytes 1310720 | tf_op jit(solution)/shard_map/all_to_all | solution.py:285
  177.4 0.8 reduce_sum.12
  (25 shorter events, 0.5 us)
Async XLA Ops:
  6.5 26.4 %slice-start = ((bf16[80,640]{1,0:T(8,128)(2,1)}), bf16[16,640]{1,0:T(8,128)(2,1)S(1)}, s32[]{:S(2)}) async-start(bf16[80,640]{1,0:T(8,128)(2,1)} %param.9), calls=%async_computation.8 | async-start | bytes 40960 | tf_op jit(solution)/shard_map/slice | solution.py:224
  8.1 9.4 %all-to-all-start.5 = ((bf16[4,16,640]{2,1,0:T(8,128)(2,1)}), bf16[4,16,640]{2,1,0:T(8,128)(2,1)S(1)}, u32[]{:S(2)}, u32[]{:S(2)}) async-start(bf16[4,16,640]{2,1,0:T(8,128)(2,1)} %fusion.1), calls=%async_computation.5 | async-start | bytes 163840 | tf_op jit(solution)/shard_map/all_to_all | solution.py:220
  17.5 39.4 %all-to-all-start = ((bf16[16,144,128]{2,1,0:T(8,128)(2,1)}), bf16[16,144,128]{2,1,0:T(8,128)(2,1)S(1)}, u32[]{:S(2)}, u32[]{:S(2)}) async-start(bf16[16,144,128]{2,1,0:T(8,128)(2,1)} %shard_map.55), calls=%async_computation | async-start | bytes 1179648 | tf_op jit(solution)/shard_map/all_to_all | solution.py:243
  32.4 126.6 %all-gather.2.cloned.1.call-start = ((), (), s32[]{:S(2)}) async-start(), calls=%async_computation.7 | async-start | bytes 1740800 | tf_op jit(solution)/shard_map/all_gather | solution.py:242
  56.9 11.9 %copy-start.1 = (pred[48]{0:T(512)(128)(4,1)S(1)}, pred[48]{0:T(512)(128)(4,1)}, u32[]{:S(2)}) copy-start(pred[48]{0:T(512)(128)(4,1)} %constant.10.clone.1) | copy-start | bytes 148
  56.9 12.5 %collective-permute-start = (bf16[16,96,128]{2,1,0:T(8,128)(2,1)S(1)}, bf16[16,96,128]{2,1,0:T(8,128)(2,1)S(1)}, u32[]{:S(2)}, u32[]{:S(2)}) collective-permute-start(bf16[16,96,128]{2,1,0:T(8,128)(2,1)S(1)} %slice.49.kv0_ref), channel_id=1, source_target_pairs={{0,32},{32,64},{64,0},{96,128},{128,160},{160,96},{192,224},{224,2... | collective-permute-start | bytes 1179656 | tf_op jit(solution)/shard_map/ppermute | solution.py:249
  62.0 23.0 %collective-permute-start.1 = (bf16[16,96,128]{2,1,0:T(8,128)(2,1)S(1)}, bf16[16,96,128]{2,1,0:T(8,128)(2,1)S(1)}, u32[]{:S(2)}, u32[]{:S(2)}) collective-permute-start(bf16[16,96,128]{2,1,0:T(8,128)(2,1)S(1)} %slice.49.kv0_ref), channel_id=1, source_target_pairs={{0,64},{32,0},{64,32},{96,160},{128,96},{160,128},{192,256},{224,1... | collective-permute-start | bytes 1179656 | tf_op jit(solution)/shard_map/ppermute | solution.py:249
  64.9 20.0 %all-to-all-start.1 = ((bf16[4,768,128]{2,1,0:T(8,128)(2,1)}), bf16[4,768,128]{2,1,0:T(8,128)(2,1)S(1)}, u32[]{:S(2)}, u32[]{:S(2)}) async-start(bf16[4,768,128]{2,1,0:T(8,128)(2,1)} %broadcast_in_dim.45), calls=%async_computation.1 | async-start | bytes 1572864 | tf_op jit(solution)/shard_map/all_to_all | solution.py:251
  150.4 10.5 %collective-permute-start.2 = (bf16[4,720,128]{2,1,0:T(8,128)(2,1)S(1)}, bf16[4,720,128]{2,1,0:T(8,128)(2,1)S(1)}, u32[]{:S(2)}, u32[]{:S(2)}) collective-permute-start(bf16[4,720,128]{2,1,0:T(8,128)(2,1)S(1)} %all_to_all.37.mine_ref), channel_id=1, source_target_pairs={{0,1},{1,0},{2,3},{3,2},{4,5},{5,4},{6,7},{7,6},{8,9},{9,8},{10,11... | collective-permute-start | bytes 2211848 | tf_op jit(solution)/shard_map/ppermute | solution.py:281
  160.9 1.4 copy-start
Sparse Core Ops, SparseCore 0:
  35.4 75.7 all-gather.1

commit v4 on v3

--- a/solution.py
+++ b/solution.py
@@ -41,7 +41,9 @@
     )(*operands)
 
 
-def scatter_heads(q_ref, k_ref, v_ref, ids_ref, out_ref):
+def scatter_heads(q_ref, k_ref, v_ref, ids_ref, weight_ref, out_ref, granules_ref):
+    for n in range(X + 1):
+        granules_ref[n] = weight_ref[n * GRANULE : (n + 1) * GRANULE, :]
     ids = ids_ref[...].astype(F32)
     lane = lax.broadcasted_iota(jnp.int32, (SLOT, HEAD), 1)
     row = lax.broadcasted_iota(jnp.int32, (SLOT, HEAD), 0)
@@ -189,17 +191,21 @@
             out_ref[y, first : first + SLOT, :] = came[4]
 
 
-def project(core_ref, mine_ref, other_ref, weight_ref, out_ref):
-    core = core_ref[0]
-    depth = HEADS_HERE * SHARE
+def project(place_ref, mine_ref, other_ref, weight_ref, out_ref):
+    core, side = place_ref[0], place_ref[1]
+    places = [lax.rem(side + (X + 1) - m, X + 1) * GRANULE for m in range(X + 1)]
+    plane_rows = (X + 1) * GRANULE
+    pieces = SHARE // GRANULE
     span = PARTS * SLOT
     share = lax.broadcasted_iota(jnp.int32, (span, HEAD), 1) // SHARE
     weights = []
     for y in range(Y):
         for which in (core, 1 - core):
-            first = pl.multiple_of((C * y + which) * depth, SHARE)
-            fifth = weight_ref[pl.ds(first + HEAD, SHARE), :]
-            weights += [weight_ref[pl.ds(first, HEAD), :]] + [fifth] * (HEAD // SHARE)
+            rows = []
+            for n in range(HEADS_HERE * pieces):
+                first = (C * y + which) * pieces * plane_rows + n // (X + 1) * plane_rows + places[n % (X + 1)]
+                rows.append(weight_ref[pl.ds(pl.multiple_of(first, GRANULE), GRANULE), :])
+            weights += rows[: 4 * pieces] + rows[4 * pieces :] * (HEAD // SHARE)
     weights = jnp.concatenate(weights, axis=0)
     for x in range(X):
         inputs = []
@@ -213,16 +219,11 @@
         out_ref[x] = jnp.concatenate(total, axis=0).astype(BF16)
 
 
-def share_rows(out_weight, side):
-    width = out_weight.shape[1]
-    own = out_weight.reshape(X + 1, GRANULE, width)
-    ring = jnp.concatenate([own[:X], own[:X]], axis=0)
-    came = lax.all_to_all(lax.dynamic_slice_in_dim(ring, X - side, X, axis=0), "x", 0, 0, tiled=True)
-    place = jnp.arange(X + 1, dtype=jnp.int32)[:, None, None]
-    earlier = jnp.concatenate([came, came[X - 1 :]], axis=0)
-    later = jnp.concatenate([came[:1], came], axis=0)
-    rows = jnp.where(place <= side, earlier, jnp.where(place == side + 1, own[X:], later))
-    return rows.reshape((X + 1) * GRANULE, width)
+def share_rows(granules):
+    came = [granules[0]]
+    for n in range(1, X):
+        came.append(lax.ppermute(granules[n], "x", [(x, (x + n) % X) for x in range(X)]))
+    return jnp.concatenate(came + [granules[X]], axis=0)
 
 
 def local(queries, keys_in, values, cluster_ids, out_weight):
@@ -230,17 +231,18 @@
     third = lax.rem(plane, PARTS)
     width = out_weight.shape[1]
 
-    (send,) = vmem_call(
+    send, granules = vmem_call(
         scatter_heads,
         56,
-        [(Z, 3 * SLOT, HEAD)],
+        [(Z, 3 * SLOT, HEAD), (X + 1, GRANULE, width)],
         queries,
         keys_in,
         values,
         cluster_ids.reshape(1, TOK),
-    )
-    weight = lax.all_gather(share_rows(out_weight, side), "z", axis=0, tiled=True)
+        out_weight,
+    )
     here = lax.all_to_all(send, "z", 0, 0, tiled=True)
+    weight = lax.all_gather(share_rows(granules), "z", axis=0, tiled=True)
     kv = here[:, SLOT:, :]
     turns = [
         [(PARTS * h + r, PARTS * h + (r + k) % PARTS) for h in range(HEADS_HERE) for r in range(PARTS)]
@@ -280,7 +282,7 @@
     packed = lax.all_to_all(packed, "y", 0, 0, tiled=True)
     others = lax.ppermute(packed, "c", [(0, 1), (1, 0)])
     (partial,) = vmem_call(
-        project, 24, [(X, TOK, width)], packed, others, weight, scalars=core.reshape(1)
+        project, 24, [(X, TOK, width)], packed, others, weight, scalars=jnp.stack([core, side])
     )
     partial = lax.all_to_all(partial, "x", 0, 0, tiled=True)
     return jnp.sum(partial.astype(F32), axis=0).astype(BF16)

time: 186 us -> 179 us (0.962)
  waiting for transfers between devices: 43.5 us -> 25.3 us
  starting transfers between devices: 38.9 us -> 45.5 us
  blocking collectives: 67 us -> 70.9 us
    all_to_all x1, waiting for transfers between devices: 23.2 us -> 10.8 us  [local(): here = lax.all_to_all(send, 'z', 0, 0, tiled=True)]
    ppermute x0 -> x3, starting transfers between devices: none -> 10.5 us  [share_rows(): lax.ppermute(granules[n], 'x', [(x, (x + n) % X) for x in range(X)])]
    all_to_all x1 -> x0, starting transfers between devices: 4.84 us -> none  [share_rows(): lax.all_to_all(lax.dynamic_slice_in_dim(ring, X - side, X, axis=0), 'x',...]
    all_to_all x1, blocking collectives: 28.7 us -> 33 us  [local(): joined = lax.all_to_all(joined, 'z', 0, 0, tiled=True)]
    ppermute x2, waiting for transfers between devices: 16 us -> 11.8 us  [local(): kv_others = [lax.ppermute(kv, 'z', turn) for turn in turns]]
    all_to_all x1 -> x0, waiting for transfers between devices: 2.46 us -> none  [share_rows(): lax.all_to_all(lax.dynamic_slice_in_dim(ring, X - side, X, axis=0), 'x',...]
  transfers between devices with their start and end apart: 7 -> 9, of which waited for: 5 -> 4; matrix products, arithmetic and copies ran while one was open for 1% -> 2% of each run, Pallas kernels for 7% -> 6%
where the time goes in v4:
time: 179 us; the launch traced here: 178 us
  blocking collectives  70.9 us (40%)
  starting transfers between devices  45.5 us (25%)
  waiting for transfers between devices  25.3 us (14%)
  Pallas kernels  16.4 us (9%)
  between operations  13.6 us (8%)
  local copies, waits for them, and re-layouts  5.77 us (3%)
    all_to_all x1, blocking collectives, local(): joined = lax.all_to_all(joined, 'z', 0, 0, tiled=True)  33 us
    pallas_call x5, Pallas kernels, vmem_call(): pl.pallas_call(body, out_shape=[jax.ShapeDtypeStruct(shape, BF16) for sha...  16.4 us
    all_to_all x1, starting transfers between devices, local(): here = lax.all_to_all(send, 'z', 0, 0, tiled=True)  15.7 us
    all_to_all x1, blocking collectives, local(): partial = lax.all_to_all(partial, 'x', 0, 0, tiled=True)  13 us
    all_to_all x1, blocking collectives, local(): part = lax.all_to_all(part, 'x', 0, 0, tiled=True)  12.7 us
    all_to_all x1, blocking collectives, local(): packed = lax.all_to_all(packed, 'y', 0, 0, tiled=True)  12.2 us
    ppermute x2, waiting for transfers between devices, local(): kv_others = [lax.ppermute(kv, 'z', turn) for turn in turns]  11.8 us
    all_to_all x1, waiting for transfers between devices, local(): here = lax.all_to_all(send, 'z', 0, 0, tiled=True)  10.8 us
  transfers between devices with their start and end apart: 9, of which 4 were waited for; matrix products, arithmetic and copies ran while one was open for 2% of the time, Pallas kernels for 6%

profile of v4, /device:TPU:1, one launch (start us, length us, event | category | flops | bytes accessed | tf_op | source)
XLA Modules:
  0.0 178.4 jit_solution(8197124444262294258)
XLA Ops:
  6.5 2.2 %shard_map.55 = (bf16[16,144,128]{2,1,0:T(8,128)(2,1)}, bf16[5,16,640]{2,1,0:T(8,128)(2,1)}) custom-call(bf16[128,640]{1,0:T(8,128)(2,1)} %q_ref.1, bf16[128,640]{1,0:T(8,128)(2,1)} %k_ref.1, bf16[128,640]{1,0:T(8,128)(2,1)} %v_ref.1, s32[1,128]{1,0:T(1,128)} %bitcast.18, bf16[80,640]{1,0:T(8,128)(2,1)} %weight_ref.1), custom_call_target="tpu_custom_call" | custom-call | tf_op jit(solution)/shard_map/pallas_call | solution.py:35
  8.7 15.7 %all-to-all-start = ((bf16[16,144,128]{2,1,0:T(8,128)(2,1)}), bf16[16,144,128]{2,1,0:T(8,128)(2,1)S(1)}, u32[]{:S(2)}, u32[]{:S(2)}) async-start(bf16[16,144,128]{2,1,0:T(8,128)(2,1)} %get-tuple-element.7), calls=%async_computation | async-start | bytes 1179648 | tf_op jit(solution)/shard_map/all_to_all | solution.py:244
  24.5 0.8 slice_bitcast_fusion
  25.3 3.1 %collective-permute-start.3 = (bf16[16,640]{1,0:T(8,128)(2,1)S(1)}, bf16[16,640]{1,0:T(8,128)(2,1)S(1)}, u32[]{:S(2)}, u32[]{:S(2)}) collective-permute-start(bf16[16,640]{1,0:T(8,128)(2,1)S(1)} %get-tuple-element.11), channel_id=1, source_target_pairs={{0,8},{8,16},{16,24},{24,0},{1,9},{9,17},{17,25},{25,1},{2,10},{10... | collective-permute-start | bytes 61448 | tf_op jit(solution)/shard_map/ppermute | solution.py:225
  28.4 4.4 %collective-permute-start.4 = (bf16[16,640]{1,0:T(8,128)(2,1)S(1)}, bf16[16,640]{1,0:T(8,128)(2,1)S(1)}, u32[]{:S(2)}, u32[]{:S(2)}) collective-permute-start(bf16[16,640]{1,0:T(8,128)(2,1)S(1)} %get-tuple-element.10), channel_id=1, source_target_pairs={{0,16},{8,24},{16,0},{24,8},{1,17},{9,25},{17,1},{25,9},{2,18},{10... | collective-permute-start | bytes 61448 | tf_op jit(solution)/shard_map/ppermute | solution.py:225
  32.8 3.1 %collective-permute-start.5 = (bf16[16,640]{1,0:T(8,128)(2,1)S(1)}, bf16[16,640]{1,0:T(8,128)(2,1)S(1)}, u32[]{:S(2)}, u32[]{:S(2)}) collective-permute-start(bf16[16,640]{1,0:T(8,128)(2,1)S(1)} %get-tuple-element.9), channel_id=1, source_target_pairs={{0,24},{8,0},{16,8},{24,16},{1,25},{9,1},{17,9},{25,17},{2,26},{10... | collective-permute-start | bytes 61448 | tf_op jit(solution)/shard_map/ppermute | solution.py:225
  35.8 0.7 bitcast_dynamic-update-slice_fusion.1
  36.6 1.0 collective-permute-done.5
  37.6 0.7 bitcast_dynamic-update-slice_fusion
  38.3 0.6 copy-done.1
  39.0 10.8 %all-to-all-done = bf16[16,144,128]{2,1,0:T(8,128)(2,1)S(1)} async-done(((bf16[16,144,128]{2,1,0:T(8,128)(2,1)}), bf16[16,144,128]{2,1,0:T(8,128)(2,1)S(1)}, u32[]{:S(2)}, u32[]{:S(2)}) %all-to-all-start) | async-done | bytes 589856 | tf_op jit(solution)/shard_map/all_to_all | solution.py:244
  49.8 4.6 %collective-permute-start = (bf16[16,96,128]{2,1,0:T(8,128)(2,1)S(1)}, bf16[16,96,128]{2,1,0:T(8,128)(2,1)S(1)}, u32[]{:S(2)}, u32[]{:S(2)}) collective-permute-start(bf16[16,96,128]{2,1,0:T(8,128)(2,1)S(1)} %slice.47.kv0_ref), channel_id=1, source_target_pairs={{0,32},{32,64},{64,0},{96,128},{128,160},{160,96},{192,224},{224,2... | collective-permute-start | bytes 1179656 | tf_op jit(solution)/shard_map/ppermute | solution.py:251
  54.5 2.0 %collective-permute-start.1 = (bf16[16,96,128]{2,1,0:T(8,128)(2,1)S(1)}, bf16[16,96,128]{2,1,0:T(8,128)(2,1)S(1)}, u32[]{:S(2)}, u32[]{:S(2)}) collective-permute-start(bf16[16,96,128]{2,1,0:T(8,128)(2,1)S(1)} %slice.47.kv0_ref), channel_id=1, source_target_pairs={{0,64},{32,0},{64,32},{96,160},{128,96},{160,128},{192,256},{224,1... | collective-permute-start | bytes 1179656 | tf_op jit(solution)/shard_map/ppermute | solution.py:251
  56.5 1.0 broadcast_in_dim.10
  57.5 4.0 %all-to-all-start.1 = ((bf16[4,768,128]{2,1,0:T(8,128)(2,1)}), bf16[4,768,128]{2,1,0:T(8,128)(2,1)S(1)}, u32[]{:S(2)}, u32[]{:S(2)}) async-start(bf16[4,768,128]{2,1,0:T(8,128)(2,1)} %broadcast_in_dim.10), calls=%async_computation.1 | async-start | bytes 1572864 | tf_op jit(solution)/shard_map/all_to_all | solution.py:253
  61.7 0.1 stack_reshape.10
  61.8 0.1 stack_reshape.11
  61.9 0.1 stack_reshape.9
  62.1 11.8 %collective-permute-done.1.kv2_ref = bf16[16,96,128]{2,1,0:T(8,128)(2,1)S(1)} collective-permute-done((bf16[16,96,128]{2,1,0:T(8,128)(2,1)S(1)}, bf16[16,96,128]{2,1,0:T(8,128)(2,1)S(1)}, u32[]{:S(2)}, u32[]{:S(2)}) %collective-permute-start.1) | collective-permute-done | bytes 393248 | tf_op jit(solution)/shard_map/ppermute | solution.py:251
  73.9 10.7 %shard_map.56 = bf16[4,864,128]{2,1,0:T(8,128)(2,1)S(1)} custom-call(s32[1]{0:T(128)} %bitcast.2.third_ref, bf16[4,768,128]{2,1,0:T(8,128)(2,1)S(1)} %all-to-all-done.1.q_ref, bf16[16,96,128]{2,1,0:T(8,128)(2,1)S(1)} %slice.47.kv0_ref, bf16[16,96,128]{2,1,0:T(8,128)(2,1)S(1)} %collective-permute-done.kv1_ref, ...), custom_call_target="tpu_custom_call" | custom-call | tf_op jit(solution)/shard_map/pallas_call | solution.py:35
  84.6 12.7 %all_to_all.30.part_ref = bf16[4,864,128]{2,1,0:T(8,128)(2,1)S(1)} all-to-all(bf16[4,864,128]{2,1,0:T(8,128)(2,1)S(1)} %shard_map.56), channel_id=1, replica_groups=mesh['z'=16,'x'=4,'y'=4,'c'=2] {'x'}, dimensions={0} | all-to-all | bytes 1769472 | tf_op jit(solution)/shard_map/all_to_all | solution.py:278
  97.3 0.6 shard_map.57
  97.9 33.0 %all_to_all.31.part_ref = bf16[16,48,128]{2,1,0:T(8,128)(2,1)S(1)} all-to-all(bf16[16,48,128]{2,1,0:T(8,128)(2,1)S(1)} %shard_map.57), channel_id=1, replica_groups=mesh['z'=16,'x'=4,'y'=4,'c'=2] {'z'}, dimensions={0} | all-to-all | bytes 393216 | tf_op jit(solution)/shard_map/all_to_all | solution.py:280
  130.9 0.2 shard_map.58
  131.1 12.2 %all_to_all.32.mine_ref = bf16[4,720,128]{2,1,0:T(8,128)(2,1)S(1)} all-to-all(bf16[4,720,128]{2,1,0:T(8,128)(2,1)S(1)} %shard_map.58), channel_id=1, replica_groups=mesh['z'=16,'x'=4,'y'=4,'c'=2] {'y'}, dimensions={0} | all-to-all | bytes 1474560 | tf_op jit(solution)/shard_map/all_to_all | solution.py:282
  143.3 8.5 %collective-permute-start.2 = (bf16[4,720,128]{2,1,0:T(8,128)(2,1)S(1)}, bf16[4,720,128]{2,1,0:T(8,128)(2,1)S(1)}, u32[]{:S(2)}, u32[]{:S(2)}) collective-permute-start(bf16[4,720,128]{2,1,0:T(8,128)(2,1)S(1)} %all_to_all.32.mine_ref), channel_id=1, source_target_pairs={{0,1},{1,0},{2,3},{3,2},{4,5},{5,4},{6,7},{7,6},{8,9},{9,8},{10,11... | collective-permute-start | bytes 2211848 | tf_op jit(solution)/shard_map/ppermute | solution.py:283
  151.8 0.1 pad_add_fusion.place_ref
  151.9 1.7 collective-permute-done.2.other_ref
  153.7 1.4 copy-done
  155.1 2.6 %shard_map.59 = bf16[4,128,640]{2,1,0:T(8,128)(2,1)S(1)} custom-call(s32[2]{0:T(128)S(1)} %pad_add_fusion.place_ref, bf16[4,720,128]{2,1,0:T(8,128)(2,1)S(1)} %all_to_all.32.mine_ref, bf16[4,720,128]{2,1,0:T(8,128)(2,1)S(1)} %collective-permute-done.2.other_ref, bf16[1280,640]{1,0:T(8,128)(2,1)S(1)} %copy-done), custom_call_target="tpu_custom_call" | custom-call | tf_op jit(solution)/shard_map/pallas_call | solution.py:35
  157.7 13.0 %all_to_all.33 = bf16[4,128,640]{2,1,0:T(8,128)(2,1)S(1)} all-to-all(bf16[4,128,640]{2,1,0:T(8,128)(2,1)S(1)} %shard_map.59), channel_id=1, replica_groups=mesh['z'=16,'x'=4,'y'=4,'c'=2] {'x'}, dimensions={0} | all-to-all | bytes 1310720 | tf_op jit(solution)/shard_map/all_to_all | solution.py:287
  170.8 0.8 reduce_sum.12
  (25 shorter events, 0.4 us)
Async XLA Ops:
  8.7 41.1 %all-to-all-start = ((bf16[16,144,128]{2,1,0:T(8,128)(2,1)}), bf16[16,144,128]{2,1,0:T(8,128)(2,1)S(1)}, u32[]{:S(2)}, u32[]{:S(2)}) async-start(bf16[16,144,128]{2,1,0:T(8,128)(2,1)} %get-tuple-element.7), calls=%async_computation | async-start | bytes 1179648 | tf_op jit(solution)/shard_map/all_to_all | solution.py:244
  24.5 127.4 %all-gather.2.cloned.1.call-start = ((), (), s32[]{:S(2)}) async-start(), calls=%async_computation.6 | async-start | bytes 1740800 | tf_op jit(solution)/shard_map/all_gather | solution.py:245
  25.3 11.3 %collective-permute-start.3 = (bf16[16,640]{1,0:T(8,128)(2,1)S(1)}, bf16[16,640]{1,0:T(8,128)(2,1)S(1)}, u32[]{:S(2)}, u32[]{:S(2)}) collective-permute-start(bf16[16,640]{1,0:T(8,128)(2,1)S(1)} %get-tuple-element.11), channel_id=1, source_target_pairs={{0,8},{8,16},{16,24},{24,0},{1,9},{9,17},{17,25},{25,1},{2,10},{10... | collective-permute-start | bytes 61448 | tf_op jit(solution)/shard_map/ppermute | solution.py:225
  28.4 8.2 %collective-permute-start.4 = (bf16[16,640]{1,0:T(8,128)(2,1)S(1)}, bf16[16,640]{1,0:T(8,128)(2,1)S(1)}, u32[]{:S(2)}, u32[]{:S(2)}) collective-permute-start(bf16[16,640]{1,0:T(8,128)(2,1)S(1)} %get-tuple-element.10), channel_id=1, source_target_pairs={{0,16},{8,24},{16,0},{24,8},{1,17},{9,25},{17,1},{25,9},{2,18},{10... | collective-permute-start | bytes 61448 | tf_op jit(solution)/shard_map/ppermute | solution.py:225
  32.8 4.8 %collective-permute-start.5 = (bf16[16,640]{1,0:T(8,128)(2,1)S(1)}, bf16[16,640]{1,0:T(8,128)(2,1)S(1)}, u32[]{:S(2)}, u32[]{:S(2)}) collective-permute-start(bf16[16,640]{1,0:T(8,128)(2,1)S(1)} %get-tuple-element.9), channel_id=1, source_target_pairs={{0,24},{8,0},{16,8},{24,16},{1,25},{9,1},{17,9},{25,17},{2,26},{10... | collective-permute-start | bytes 61448 | tf_op jit(solution)/shard_map/ppermute | solution.py:225
  38.3 0.6 copy-start.1
  49.8 12.1 %copy-start.2 = (pred[48]{0:T(512)(128)(4,1)S(1)}, pred[48]{0:T(512)(128)(4,1)}, u32[]{:S(2)}) copy-start(pred[48]{0:T(512)(128)(4,1)} %constant.24.clone.1) | copy-start | bytes 148
  49.8 12.2 %collective-permute-start = (bf16[16,96,128]{2,1,0:T(8,128)(2,1)S(1)}, bf16[16,96,128]{2,1,0:T(8,128)(2,1)S(1)}, u32[]{:S(2)}, u32[]{:S(2)}) collective-permute-start(bf16[16,96,128]{2,1,0:T(8,128)(2,1)S(1)} %slice.47.kv0_ref), channel_id=1, source_target_pairs={{0,32},{32,64},{64,0},{96,128},{128,160},{160,96},{192,224},{224,2... | collective-permute-start | bytes 1179656 | tf_op jit(solution)/shard_map/ppermute | solution.py:251
  54.5 19.4 %collective-permute-start.1 = (bf16[16,96,128]{2,1,0:T(8,128)(2,1)S(1)}, bf16[16,96,128]{2,1,0:T(8,128)(2,1)S(1)}, u32[]{:S(2)}, u32[]{:S(2)}) collective-permute-start(bf16[16,96,128]{2,1,0:T(8,128)(2,1)S(1)} %slice.47.kv0_ref), channel_id=1, source_target_pairs={{0,64},{32,0},{64,32},{96,160},{128,96},{160,128},{192,256},{224,1... | collective-permute-start | bytes 1179656 | tf_op jit(solution)/shard_map/ppermute | solution.py:251
  57.5 16.4 %all-to-all-start.1 = ((bf16[4,768,128]{2,1,0:T(8,128)(2,1)}), bf16[4,768,128]{2,1,0:T(8,128)(2,1)S(1)}, u32[]{:S(2)}, u32[]{:S(2)}) async-start(bf16[4,768,128]{2,1,0:T(8,128)(2,1)} %broadcast_in_dim.10), calls=%async_computation.1 | async-start | bytes 1572864 | tf_op jit(solution)/shard_map/all_to_all | solution.py:253
  143.3 10.4 %collective-permute-start.2 = (bf16[4,720,128]{2,1,0:T(8,128)(2,1)S(1)}, bf16[4,720,128]{2,1,0:T(8,128)(2,1)S(1)}, u32[]{:S(2)}, u32[]{:S(2)}) collective-permute-start(bf16[4,720,128]{2,1,0:T(8,128)(2,1)S(1)} %all_to_all.32.mine_ref), channel_id=1, source_target_pairs={{0,1},{1,0},{2,3},{3,2},{4,5},{5,4},{6,7},{7,6},{8,9},{9,8},{10,11... | collective-permute-start | bytes 2211848 | tf_op jit(solution)/shard_map/ppermute | solution.py:283
  153.6 1.4 copy-start
Sparse Core Ops, SparseCore 0:
  39.1 71.8 all-gather.1

commit v5 on v4

--- a/solution.py
+++ b/solution.py
@@ -27,7 +27,7 @@
 GRANULE = 16
 
 
-def vmem_call(body, mebibytes, shapes, *operands, scalars=None):
+def vmem_call(body, mebibytes, shapes, *operands, scalars=None, scratch=()):
     specs = [pl.BlockSpec(memory_space=pltpu.VMEM)] * len(operands)
     if scalars is not None:
         specs = [pl.BlockSpec(memory_space=pltpu.SMEM)] + specs
@@ -37,6 +37,7 @@
         out_shape=[jax.ShapeDtypeStruct(shape, BF16) for shape in shapes],
         in_specs=specs,
         out_specs=[pl.BlockSpec(memory_space=pltpu.VMEM)] * len(shapes),
+        scratch_shapes=[pltpu.VMEM(shape, BF16) for shape in scratch],
         compiler_params=pltpu.CompilerParams(vmem_limit_bytes=mebibytes * 1024 * 1024),
     )(*operands)
 
@@ -191,8 +192,13 @@
             out_ref[y, first : first + SLOT, :] = came[4]
 
 
-def project(place_ref, mine_ref, other_ref, weight_ref, out_ref):
-    core, side = place_ref[0], place_ref[1]
+def project(place_ref, mine_ref, other_ref, *refs):
+    parts, out_ref, weight_ref = refs[:Z], refs[Z], refs[Z + 1]
+    core, side, plane = place_ref[0], place_ref[1], place_ref[2]
+    for n, part in enumerate(parts):
+        turn = Z - n if n <= Z // 2 else n - Z // 2
+        first = pl.multiple_of(lax.rem(plane + turn, Z) * part.shape[0], GRANULE)
+        weight_ref[pl.ds(first, part.shape[0]), :] = part[...]
     places = [lax.rem(side + (X + 1) - m, X + 1) * GRANULE for m in range(X + 1)]
     plane_rows = (X + 1) * GRANULE
     pieces = SHARE // GRANULE
@@ -226,6 +232,24 @@
     return jnp.concatenate(came + [granules[X]], axis=0)
 
 
+class Ring:
+    def __init__(self, block):
+        self.up, self.down = [block], [block]
+
+    def step(self):
+        if len(self.up) <= Z // 2:
+            self.up.append(lax.ppermute(self.up[-1], "z", [(z, (z + 1) % Z) for z in range(Z)]))
+        if len(self.down) < Z // 2:
+            self.down.append(lax.ppermute(self.down[-1], "z", [(z, (z - 1) % Z) for z in range(Z)]))
+
+    def meet(self, value):
+        value, self.up[-1], self.down[-1] = lax.optimization_barrier((value, self.up[-1], self.down[-1]))
+        return value
+
+    def blocks(self):
+        return self.up + self.down[1:]
+
+
 def local(queries, keys_in, values, cluster_ids, out_weight):
     plane, side, core = lax.axis_index("z"), lax.axis_index("x"), lax.axis_index("c")
     third = lax.rem(plane, PARTS)
@@ -242,13 +266,16 @@
         out_weight,
     )
     here = lax.all_to_all(send, "z", 0, 0, tiled=True)
-    weight = lax.all_gather(share_rows(granules), "z", axis=0, tiled=True)
+    ring = Ring(share_rows(granules))
+    ring.step()
+    here = ring.meet(here)
     kv = here[:, SLOT:, :]
     turns = [
         [(PARTS * h + r, PARTS * h + (r + k) % PARTS) for h in range(HEADS_HERE) for r in range(PARTS)]
         for k in (1, 2)
     ]
     kv_others = [lax.ppermute(kv, "z", turn) for turn in turns]
+    ring.step()
     query = jnp.broadcast_to(here[:, :SLOT, :].reshape(1, Z * SLOT, HEAD), (X, Z * SLOT, HEAD))
     query = lax.all_to_all(query, "x", 0, 0, tiled=True)
 
@@ -275,14 +302,28 @@
         key_code,
         scalars=third.reshape(1),
     )
-    part = lax.all_to_all(part, "x", 0, 0, tiled=True)
+    part = lax.all_to_all(ring.meet(part), "x", 0, 0, tiled=True)
+    ring.step()
+    ring.step()
     (joined,) = vmem_call(join, 8, [(Z, SLOT, HEAD)], part)
-    joined = lax.all_to_all(joined, "z", 0, 0, tiled=True)
+    joined = lax.all_to_all(ring.meet(joined), "z", 0, 0, tiled=True)
+    ring.step()
+    ring.step()
     (packed,) = vmem_call(assemble, 8, [(Y, (X + 1) * PARTS * SLOT, HEAD)], joined)
-    packed = lax.all_to_all(packed, "y", 0, 0, tiled=True)
+    packed = lax.all_to_all(ring.meet(packed), "y", 0, 0, tiled=True)
+    ring.step()
+    ring.step()
+    packed = ring.meet(packed)
     others = lax.ppermute(packed, "c", [(0, 1), (1, 0)])
     (partial,) = vmem_call(
-        project, 24, [(X, TOK, width)], packed, others, weight, scalars=jnp.stack([core, side])
+        project,
+        24,
+        [(X, TOK, width)],
+        packed,
+        others,
+        *ring.blocks(),
+        scalars=jnp.stack([core, side, plane]),
+        scratch=[(Z * out_weight.shape[0], width)],
     )
     partial = lax.all_to_all(partial, "x", 0, 0, tiled=True)
     return jnp.sum(partial.astype(F32), axis=0).astype(BF16)

time: 179 us -> 187 us (1.045)
  starting transfers between devices: 45.5 us -> 120 us
  blocking collectives: 70.9 us -> 14.7 us
  between operations: 13.6 us -> 0.36 us
  local copies, waits for them, and re-layouts: 5.77 us -> 2.06 us
  Pallas kernels: 16.4 us -> 19.4 us
  waiting for transfers between devices: 25.3 us -> 27.8 us
    all_to_all x3 -> x0, blocking collectives: 57.8 us -> none  [the longest x1 33 us: local(): joined = lax.all_to_all(joined, 'z', 0, 0, tiled=True)]
    ppermute x0 -> x15, starting transfers between devices: none -> 52.3 us  [the longest x8 27.1 us: step(): lax.ppermute(self.up[-1], 'z', [(z, (z + 1) % Z) for z in range(Z)])]
    all_to_all x0 -> x3, starting transfers between devices: none -> 24.3 us  [the longest x1 16.2 us: local(): joined = lax.all_to_all(ring.meet(joined), 'z', 0, 0, tiled=True)]
    ppermute x0 -> x15, waiting for transfers between devices: none -> 18.8 us  [the longest x7 12.3 us: step(): lax.ppermute(self.down[-1], 'z', [(z, (z - 1) % Z) for z in range(Z)])]
    all_to_all x1, waiting for transfers between devices: 10.8 us -> 0.01 us  [local(): here = lax.all_to_all(send, 'z', 0, 0, tiled=True)]
    ppermute x2, waiting for transfers between devices: 11.8 us -> 3.75 us  [local(): kv_others = [lax.ppermute(kv, 'z', turn) for turn in turns]]
    pallas_call x5, Pallas kernels: 16.4 us -> 19.4 us  [vmem_call(): pl.pallas_call(body, out_shape=[jax.ShapeDtypeStruct(shape, BF16) for sha...]
    ppermute x3, waiting for transfers between devices: 0.97 us -> 3.49 us  [share_rows(): lax.ppermute(granules[n], 'x', [(x, (x + n) % X) for x in range(X)])]
  transfers between devices with their start and end apart: 9 -> 26, of which waited for: 4 -> 12; matrix products, arithmetic and copies ran while one was open for 2% -> 0% of each run, Pallas kernels for 6% -> 8%
where the time goes in v5:
time: 187 us; the launch traced here: 185 us
  starting transfers between devices  120 us (64%)
  waiting for transfers between devices  27.8 us (15%)
  Pallas kernels  19.4 us (10%)
  blocking collectives  14.7 us (8%)
  local copies, waits for them, and re-layouts  2.06 us (1%)
    ppermute x8, starting transfers between devices, step(): lax.ppermute(self.up[-1], 'z', [(z, (z + 1) % Z) for z in range(Z)])  27.1 us
    ppermute x7, starting transfers between devices, step(): lax.ppermute(self.down[-1], 'z', [(z, (z - 1) % Z) for z in range(Z)])  25.2 us
    pallas_call x5, Pallas kernels, vmem_call(): pl.pallas_call(body, out_shape=[jax.ShapeDtypeStruct(shape, BF16) for sha...  19.4 us
    all_to_all x1, starting transfers between devices, local(): joined = lax.all_to_all(ring.meet(joined), 'z', 0, 0, tiled=True)  16.2 us
    all_to_all x1, starting transfers between devices, local(): here = lax.all_to_all(send, 'z', 0, 0, tiled=True)  15.9 us
    all_to_all x1, blocking collectives, local(): partial = lax.all_to_all(partial, 'x', 0, 0, tiled=True)  14.7 us
    ppermute x7, waiting for transfers between devices, step(): lax.ppermute(self.down[-1], 'z', [(z, (z - 1) % Z) for z in range(Z)])  12.3 us
    ppermute x3, starting transfers between devices, share_rows(): lax.ppermute(granules[n], 'x', [(x, (x + n) % X) for x in range(X)])  9.33 us
  transfers between devices with their start and end apart: 26, of which 12 were waited for; matrix products, arithmetic and copies ran while one was open for 0% of the time, Pallas kernels for 8%

profile of v5, /device:TPU:1, one launch (start us, length us, event | category | flops | bytes accessed | tf_op | source)
XLA Modules:
  0.0 185.2 jit_solution(11516713707096779110)
XLA Ops:
  0.0 2.2 %shard_map.55 = (bf16[16,144,128]{2,1,0:T(8,128)(2,1)}, bf16[5,16,640]{2,1,0:T(8,128)(2,1)}) custom-call(bf16[128,640]{1,0:T(8,128)(2,1)} %q_ref.1, bf16[128,640]{1,0:T(8,128)(2,1)} %k_ref.1, bf16[128,640]{1,0:T(8,128)(2,1)} %v_ref.1, s32[1,128]{1,0:T(1,128)} %bitcast.19, bf16[80,640]{1,0:T(8,128)(2,1)} %weight_ref.1), custom_call_target="tpu_custom_call" | custom-call | tf_op jit(solution)/shard_map/pallas_call | solution.py:35
  2.2 15.9 %all-to-all-start = ((bf16[16,144,128]{2,1,0:T(8,128)(2,1)}), bf16[16,144,128]{2,1,0:T(8,128)(2,1)S(1)}, u32[]{:S(2)}, u32[]{:S(2)}) async-start(bf16[16,144,128]{2,1,0:T(8,128)(2,1)} %get-tuple-element.22), calls=%async_computation | async-start | bytes 1179648 | tf_op jit(solution)/shard_map/all_to_all | solution.py:268
  18.1 4.4 %collective-permute-start.2 = (bf16[16,640]{1,0:T(8,128)(2,1)S(1)}, bf16[16,640]{1,0:T(8,128)(2,1)S(1)}, u32[]{:S(2)}, u32[]{:S(2)}) collective-permute-start(bf16[16,640]{1,0:T(8,128)(2,1)S(1)} %get-tuple-element.39), channel_id=1, source_target_pairs={{0,24},{8,0},{16,8},{24,16},{1,25},{9,1},{17,9},{25,17},{2,26},{10... | collective-permute-start | bytes 61448 | tf_op jit(solution)/shard_map/ppermute | solution.py:231
  22.5 2.4 %collective-permute-start.1 = (bf16[16,640]{1,0:T(8,128)(2,1)S(1)}, bf16[16,640]{1,0:T(8,128)(2,1)S(1)}, u32[]{:S(2)}, u32[]{:S(2)}) collective-permute-start(bf16[16,640]{1,0:T(8,128)(2,1)S(1)} %get-tuple-element.40), channel_id=1, source_target_pairs={{0,16},{8,24},{16,0},{24,8},{1,17},{9,25},{17,1},{25,9},{2,18},{10... | collective-permute-start | bytes 61448 | tf_op jit(solution)/shard_map/ppermute | solution.py:231
  24.9 2.5 %collective-permute-start = (bf16[16,640]{1,0:T(8,128)(2,1)S(1)}, bf16[16,640]{1,0:T(8,128)(2,1)S(1)}, u32[]{:S(2)}, u32[]{:S(2)}) collective-permute-start(bf16[16,640]{1,0:T(8,128)(2,1)S(1)} %get-tuple-element.41), channel_id=1, source_target_pairs={{0,8},{8,16},{16,24},{24,0},{1,9},{9,17},{17,25},{25,1},{2,10},{10... | collective-permute-start | bytes 61448 | tf_op jit(solution)/shard_map/ppermute | solution.py:231
  27.5 3.5 %collective-permute-done = bf16[16,640]{1,0:T(8,128)(2,1)S(1)} collective-permute-done((bf16[16,640]{1,0:T(8,128)(2,1)S(1)}, bf16[16,640]{1,0:T(8,128)(2,1)S(1)}, u32[]{:S(2)}, u32[]{:S(2)}) %collective-permute-start) | collective-permute-done | bytes 20512 | tf_op jit(solution)/shard_map/ppermute | solution.py:231
  31.0 4.6 %collective-permute-start.4 = (bf16[80,640]{1,0:T(8,128)(2,1)S(1)}, bf16[80,640]{1,0:T(8,128)(2,1)S(1)}, u32[]{:S(2)}, u32[]{:S(2)}) collective-permute-start(bf16[80,640]{1,0:T(8,128)(2,1)S(1)} %bitcast_dynamic-update-slice_fusion.refs_0_), channel_id=1, source_target_pairs={{0,480},{32,0},{64,32},{96,64},{128,96},{160,128},{192,160},{224,1... | collective-permute-start | bytes 307208 | tf_op jit(solution)/shard_map/ppermute | solution.py:243
  37.6 9.3 %collective-permute-done.4.refs_9_ = bf16[80,640]{1,0:T(8,128)(2,1)S(1)} collective-permute-done((bf16[80,640]{1,0:T(8,128)(2,1)S(1)}, bf16[80,640]{1,0:T(8,128)(2,1)S(1)}, u32[]{:S(2)}, u32[]{:S(2)}) %collective-permute-start.4) | collective-permute-done | bytes 102432 | tf_op jit(solution)/shard_map/ppermute | solution.py:243
  48.4 3.7 %all-to-all-start.1 = ((bf16[4,768,128]{2,1,0:T(8,128)(2,1)}), bf16[4,768,128]{2,1,0:T(8,128)(2,1)S(1)}, u32[]{:S(2)}, u32[]{:S(2)}) async-start(bf16[4,768,128]{2,1,0:T(8,128)(2,1)} %broadcast_in_dim.10), calls=%async_computation.1 | async-start | bytes 1572864 | tf_op jit(solution)/shard_map/all_to_all | solution.py:280
  52.2 3.5 %collective-permute-start.6 = (bf16[16,96,128]{2,1,0:T(8,128)(2,1)S(1)}, bf16[16,96,128]{2,1,0:T(8,128)(2,1)S(1)}, u32[]{:S(2)}, u32[]{:S(2)}) collective-permute-start(bf16[16,96,128]{2,1,0:T(8,128)(2,1)S(1)} %slice.41.kv0_ref), channel_id=1, source_target_pairs={{0,64},{32,0},{64,32},{96,160},{128,96},{160,128},{192,256},{224,1... | collective-permute-start | bytes 1179656 | tf_op jit(solution)/shard_map/ppermute | solution.py:277
  58.7 2.7 %collective-permute-start.7 = (bf16[80,640]{1,0:T(8,128)(2,1)S(1)}, bf16[80,640]{1,0:T(8,128)(2,1)S(1)}, u32[]{:S(2)}, u32[]{:S(2)}) collective-permute-start(bf16[80,640]{1,0:T(8,128)(2,1)S(1)} %collective-permute-done.3.refs_1_), channel_id=1, source_target_pairs={{0,32},{32,64},{64,96},{96,128},{128,160},{160,192},{192,224},{224... | collective-permute-start | bytes 307208 | tf_op jit(solution)/shard_map/ppermute | solution.py:241
  61.5 3.7 %collective-permute-start.8 = (bf16[80,640]{1,0:T(8,128)(2,1)S(1)}, bf16[80,640]{1,0:T(8,128)(2,1)S(1)}, u32[]{:S(2)}, u32[]{:S(2)}) collective-permute-start(bf16[80,640]{1,0:T(8,128)(2,1)S(1)} %collective-permute-done.4.refs_9_), channel_id=1, source_target_pairs={{0,480},{32,0},{64,32},{96,64},{128,96},{160,128},{192,160},{224,1... | collective-permute-start | bytes 307208 | tf_op jit(solution)/shard_map/ppermute | solution.py:243
  65.3 3.7 %collective-permute-done.5.kv1_ref = bf16[16,96,128]{2,1,0:T(8,128)(2,1)S(1)} collective-permute-done((bf16[16,96,128]{2,1,0:T(8,128)(2,1)S(1)}, bf16[16,96,128]{2,1,0:T(8,128)(2,1)S(1)}, u32[]{:S(2)}, u32[]{:S(2)}) %collective-permute-start.5) | collective-permute-done | bytes 393248 | tf_op jit(solution)/shard_map/ppermute | solution.py:277
  69.0 12.1 %shard_map.56 = bf16[4,864,128]{2,1,0:T(8,128)(2,1)} custom-call(s32[1]{0:T(128)} %bitcast.3.third_ref, bf16[4,768,128]{2,1,0:T(8,128)(2,1)S(1)} %all-to-all-done.1.q_ref, bf16[16,96,128]{2,1,0:T(8,128)(2,1)S(1)} %slice.41.kv0_ref, bf16[16,96,128]{2,1,0:T(8,128)(2,1)S(1)} %collective-permute-done.5.kv1_ref, ...), custom_call_target="tpu_custom_call" | custom-call | tf_op jit(solution)/shard_map/pallas_call | solution.py:35
  81.1 4.0 %all-to-all-start.2 = ((bf16[4,864,128]{2,1,0:T(8,128)(2,1)}), bf16[4,864,128]{2,1,0:T(8,128)(2,1)S(1)}, u32[]{:S(2)}, u32[]{:S(2)}) async-start(bf16[4,864,128]{2,1,0:T(8,128)(2,1)} %shard_map.56), calls=%async_computation.2 | async-start | bytes 1769472 | tf_op jit(solution)/shard_map/all_to_all | solution.py:305
  85.0 4.8 %collective-permute-start.9 = (bf16[80,640]{1,0:T(8,128)(2,1)S(1)}, bf16[80,640]{1,0:T(8,128)(2,1)S(1)}, u32[]{:S(2)}, u32[]{:S(2)}) collective-permute-start(bf16[80,640]{1,0:T(8,128)(2,1)S(1)} %collective-permute-done.7.refs_2_), channel_id=1, source_target_pairs={{0,32},{32,64},{64,96},{96,128},{128,160},{160,192},{192,224},{224... | collective-permute-start | bytes 307208 | tf_op jit(solution)/shard_map/ppermute | solution.py:241
  91.7 4.2 %collective-permute-start.10 = (bf16[80,640]{1,0:T(8,128)(2,1)S(1)}, bf16[80,640]{1,0:T(8,128)(2,1)S(1)}, u32[]{:S(2)}, u32[]{:S(2)}) collective-permute-start(bf16[80,640]{1,0:T(8,128)(2,1)S(1)} %collective-permute-done.9.refs_3_), channel_id=1, source_target_pairs={{0,32},{32,64},{64,96},{96,128},{128,160},{160,192},{192,224},{224... | collective-permute-start | bytes 307208 | tf_op jit(solution)/shard_map/ppermute | solution.py:241
  96.1 5.3 %collective-permute-start.12 = (bf16[80,640]{1,0:T(8,128)(2,1)S(1)}, bf16[80,640]{1,0:T(8,128)(2,1)S(1)}, u32[]{:S(2)}, u32[]{:S(2)}) collective-permute-start(bf16[80,640]{1,0:T(8,128)(2,1)S(1)} %collective-permute-done.11.refs_11_), channel_id=1, source_target_pairs={{0,480},{32,0},{64,32},{96,64},{128,96},{160,128},{192,160},{224,1... | collective-permute-start | bytes 307208 | tf_op jit(solution)/shard_map/ppermute | solution.py:243
  103.1 16.2 %all-to-all-start.3 = ((bf16[16,48,128]{2,1,0:T(8,128)(2,1)}), bf16[16,48,128]{2,1,0:T(8,128)(2,1)S(1)}, u32[]{:S(2)}, u32[]{:S(2)}) async-start(bf16[16,48,128]{2,1,0:T(8,128)(2,1)} %shard_map.57), calls=%async_computation.3 | async-start | bytes 393216 | tf_op jit(solution)/shard_map/all_to_all | solution.py:309
  119.2 3.3 %collective-permute-start.13 = (bf16[80,640]{1,0:T(8,128)(2,1)S(1)}, bf16[80,640]{1,0:T(8,128)(2,1)S(1)}, u32[]{:S(2)}, u32[]{:S(2)}) collective-permute-start(bf16[80,640]{1,0:T(8,128)(2,1)S(1)} %collective-permute-done.10.refs_4_), channel_id=1, source_target_pairs={{0,32},{32,64},{64,96},{96,128},{128,160},{160,192},{192,224},{224... | collective-permute-start | bytes 307208 | tf_op jit(solution)/shard_map/ppermute | solution.py:241
  122.5 3.2 %collective-permute-start.15 = (bf16[80,640]{1,0:T(8,128)(2,1)S(1)}, bf16[80,640]{1,0:T(8,128)(2,1)S(1)}, u32[]{:S(2)}, u32[]{:S(2)}) collective-permute-start(bf16[80,640]{1,0:T(8,128)(2,1)S(1)} %collective-permute-done.12.refs_12_), channel_id=1, source_target_pairs={{0,480},{32,0},{64,32},{96,64},{128,96},{160,128},{192,160},{224,1... | collective-permute-start | bytes 307208 | tf_op jit(solution)/shard_map/ppermute | solution.py:243
  125.7 2.3 %collective-permute-done.13.refs_5_ = bf16[80,640]{1,0:T(8,128)(2,1)S(1)} collective-permute-done((bf16[80,640]{1,0:T(8,128)(2,1)S(1)}, bf16[80,640]{1,0:T(8,128)(2,1)S(1)}, u32[]{:S(2)}, u32[]{:S(2)}) %collective-permute-start.13) | collective-permute-done | bytes 102432 | tf_op jit(solution)/shard_map/ppermute | solution.py:241
  128.0 5.3 %collective-permute-start.14 = (bf16[80,640]{1,0:T(8,128)(2,1)S(1)}, bf16[80,640]{1,0:T(8,128)(2,1)S(1)}, u32[]{:S(2)}, u32[]{:S(2)}) collective-permute-start(bf16[80,640]{1,0:T(8,128)(2,1)S(1)} %collective-permute-done.13.refs_5_), channel_id=1, source_target_pairs={{0,32},{32,64},{64,96},{96,128},{128,160},{160,192},{192,224},{224... | collective-permute-start | bytes 307208 | tf_op jit(solution)/shard_map/ppermute | solution.py:241
  136.6 2.2 %collective-permute-done.16.refs_14_ = bf16[80,640]{1,0:T(8,128)(2,1)S(1)} collective-permute-done((bf16[80,640]{1,0:T(8,128)(2,1)S(1)}, bf16[80,640]{1,0:T(8,128)(2,1)S(1)}, u32[]{:S(2)}, u32[]{:S(2)}) %collective-permute-start.16) | collective-permute-done | bytes 102432 | tf_op jit(solution)/shard_map/ppermute | solution.py:243
  138.8 4.2 %all-to-all-start.4 = ((bf16[4,720,128]{2,1,0:T(8,128)(2,1)}), bf16[4,720,128]{2,1,0:T(8,128)(2,1)S(1)}, u32[]{:S(2)}, u32[]{:S(2)}) async-start(bf16[4,720,128]{2,1,0:T(8,128)(2,1)} %shard_map.58), calls=%async_computation.4 | async-start | bytes 1474560 | tf_op jit(solution)/shard_map/all_to_all | solution.py:313
  142.9 2.2 %collective-permute-start.17 = (bf16[80,640]{1,0:T(8,128)(2,1)S(1)}, bf16[80,640]{1,0:T(8,128)(2,1)S(1)}, u32[]{:S(2)}, u32[]{:S(2)}) collective-permute-start(bf16[80,640]{1,0:T(8,128)(2,1)S(1)} %collective-permute-done.14.refs_6_), channel_id=1, source_target_pairs={{0,32},{32,64},{64,96},{96,128},{128,160},{160,192},{192,224},{224... | collective-permute-start | bytes 307208 | tf_op jit(solution)/shard_map/ppermute | solution.py:241
  145.2 4.3 %collective-permute-start.19 = (bf16[80,640]{1,0:T(8,128)(2,1)S(1)}, bf16[80,640]{1,0:T(8,128)(2,1)S(1)}, u32[]{:S(2)}, u32[]{:S(2)}) collective-permute-start(bf16[80,640]{1,0:T(8,128)(2,1)S(1)} %collective-permute-done.16.refs_14_), channel_id=1, source_target_pairs={{0,480},{32,0},{64,32},{96,64},{128,96},{160,128},{192,160},{224,1... | collective-permute-start | bytes 307208 | tf_op jit(solution)/shard_map/ppermute | solution.py:243
  149.6 2.6 %collective-permute-start.18 = (bf16[80,640]{1,0:T(8,128)(2,1)S(1)}, bf16[80,640]{1,0:T(8,128)(2,1)S(1)}, u32[]{:S(2)}, u32[]{:S(2)}) collective-permute-start(bf16[80,640]{1,0:T(8,128)(2,1)S(1)} %collective-permute-done.17.refs_7_), channel_id=1, source_target_pairs={{0,32},{32,64},{64,96},{96,128},{128,160},{160,192},{192,224},{224... | collective-permute-start | bytes 307208 | tf_op jit(solution)/shard_map/ppermute | solution.py:241
  152.6 3.6 %collective-permute-done.18.refs_8_ = bf16[80,640]{1,0:T(8,128)(2,1)S(1)} collective-permute-done((bf16[80,640]{1,0:T(8,128)(2,1)S(1)}, bf16[80,640]{1,0:T(8,128)(2,1)S(1)}, u32[]{:S(2)}, u32[]{:S(2)}) %collective-permute-start.18) | collective-permute-done | bytes 102432 | tf_op jit(solution)/shard_map/ppermute | solution.py:241
  156.2 8.9 %collective-permute-start.20 = (bf16[4,720,128]{2,1,0:T(8,128)(2,1)S(1)}, bf16[4,720,128]{2,1,0:T(8,128)(2,1)S(1)}, u32[]{:S(2)}, u32[]{:S(2)}) collective-permute-start(bf16[4,720,128]{2,1,0:T(8,128)(2,1)S(1)} %all-to-all-done.4.mine_ref), channel_id=1, source_target_pairs={{0,1},{1,0},{2,3},{3,2},{4,5},{5,4},{6,7},{7,6},{8,9},{9,8},{10,11... | collective-permute-start | bytes 2211848 | tf_op jit(solution)/shard_map/ppermute | solution.py:317
  166.9 2.8 %shard_map.59 = bf16[4,128,640]{2,1,0:T(8,128)(2,1)S(1)} custom-call(s32[3]{0:T(128)S(1)} %pad_add_fusion.place_ref, bf16[4,720,128]{2,1,0:T(8,128)(2,1)S(1)} %all-to-all-done.4.mine_ref, bf16[4,720,128]{2,1,0:T(8,128)(2,1)S(1)} %collective-permute-done.20.other_ref, bf16[80,640]{1,0:T(8,128)(2,1)S(1)} %bitcast_dynamic-update-slice_fusion.refs_0_, ...), custom_call_target="tpu_custom_call" | custom-call | tf_op jit(solution)/shard_map/pallas_call | solution.py:35
  169.7 14.7 %all_to_all.30 = bf16[4,128,640]{2,1,0:T(8,128)(2,1)S(1)} all-to-all(bf16[4,128,640]{2,1,0:T(8,128)(2,1)S(1)} %shard_map.59), channel_id=1, replica_groups=mesh['z'=16,'x'=4,'y'=4,'c'=2] {'x'}, dimensions={0} | all-to-all | bytes 1310720 | tf_op jit(solution)/shard_map/all_to_all | solution.py:328
  (53 shorter events, 16.5 us)
Async XLA Ops:
  2.2 15.9 %copy-start = (bf16[5,16,640]{2,1,0:T(8,128)(2,1)S(1)}, bf16[5,16,640]{2,1,0:T(8,128)(2,1)}, u32[]{:S(2)}) copy-start(bf16[5,16,640]{2,1,0:T(8,128)(2,1)} %get-tuple-element.23) | copy-start | bytes 307204
  2.2 45.2 %all-to-all-start = ((bf16[16,144,128]{2,1,0:T(8,128)(2,1)}), bf16[16,144,128]{2,1,0:T(8,128)(2,1)S(1)}, u32[]{:S(2)}, u32[]{:S(2)}) async-start(bf16[16,144,128]{2,1,0:T(8,128)(2,1)} %get-tuple-element.22), calls=%async_computation | async-start | bytes 1179648 | tf_op jit(solution)/shard_map/all_to_all | solution.py:268
  18.1 12.9 %collective-permute-start.2 = (bf16[16,640]{1,0:T(8,128)(2,1)S(1)}, bf16[16,640]{1,0:T(8,128)(2,1)S(1)}, u32[]{:S(2)}, u32[]{:S(2)}) collective-permute-start(bf16[16,640]{1,0:T(8,128)(2,1)S(1)} %get-tuple-element.39), channel_id=1, source_target_pairs={{0,24},{8,0},{16,8},{24,16},{1,25},{9,1},{17,9},{25,17},{2,26},{10... | collective-permute-start | bytes 61448 | tf_op jit(solution)/shard_map/ppermute | solution.py:231
  22.5 8.5 %collective-permute-start.1 = (bf16[16,640]{1,0:T(8,128)(2,1)S(1)}, bf16[16,640]{1,0:T(8,128)(2,1)S(1)}, u32[]{:S(2)}, u32[]{:S(2)}) collective-permute-start(bf16[16,640]{1,0:T(8,128)(2,1)S(1)} %get-tuple-element.40), channel_id=1, source_target_pairs={{0,16},{8,24},{16,0},{24,8},{1,17},{9,25},{17,1},{25,9},{2,18},{10... | collective-permute-start | bytes 61448 | tf_op jit(solution)/shard_map/ppermute | solution.py:231
  24.9 6.0 %collective-permute-start = (bf16[16,640]{1,0:T(8,128)(2,1)S(1)}, bf16[16,640]{1,0:T(8,128)(2,1)S(1)}, u32[]{:S(2)}, u32[]{:S(2)}) collective-permute-start(bf16[16,640]{1,0:T(8,128)(2,1)S(1)} %get-tuple-element.41), channel_id=1, source_target_pairs={{0,8},{8,16},{16,24},{24,0},{1,9},{9,17},{17,25},{25,1},{2,10},{10... | collective-permute-start | bytes 61448 | tf_op jit(solution)/shard_map/ppermute | solution.py:231
  31.0 15.9 %collective-permute-start.4 = (bf16[80,640]{1,0:T(8,128)(2,1)S(1)}, bf16[80,640]{1,0:T(8,128)(2,1)S(1)}, u32[]{:S(2)}, u32[]{:S(2)}) collective-permute-start(bf16[80,640]{1,0:T(8,128)(2,1)S(1)} %bitcast_dynamic-update-slice_fusion.refs_0_), channel_id=1, source_target_pairs={{0,480},{32,0},{64,32},{96,64},{128,96},{160,128},{192,160},{224,1... | collective-permute-start | bytes 307208 | tf_op jit(solution)/shard_map/ppermute | solution.py:243
  35.6 11.7 %collective-permute-start.3 = (bf16[80,640]{1,0:T(8,128)(2,1)S(1)}, bf16[80,640]{1,0:T(8,128)(2,1)S(1)}, u32[]{:S(2)}, u32[]{:S(2)}) collective-permute-start(bf16[80,640]{1,0:T(8,128)(2,1)S(1)} %bitcast_dynamic-update-slice_fusion.refs_0_), channel_id=1, source_target_pairs={{0,32},{32,64},{64,96},{96,128},{128,160},{160,192},{192,224},{224... | collective-permute-start | bytes 307208 | tf_op jit(solution)/shard_map/ppermute | solution.py:241
  48.4 20.6 %all-to-all-start.1 = ((bf16[4,768,128]{2,1,0:T(8,128)(2,1)}), bf16[4,768,128]{2,1,0:T(8,128)(2,1)S(1)}, u32[]{:S(2)}, u32[]{:S(2)}) async-start(bf16[4,768,128]{2,1,0:T(8,128)(2,1)} %broadcast_in_dim.10), calls=%async_computation.1 | async-start | bytes 1572864 | tf_op jit(solution)/shard_map/all_to_all | solution.py:280
  52.2 13.1 %collective-permute-start.6 = (bf16[16,96,128]{2,1,0:T(8,128)(2,1)S(1)}, bf16[16,96,128]{2,1,0:T(8,128)(2,1)S(1)}, u32[]{:S(2)}, u32[]{:S(2)}) collective-permute-start(bf16[16,96,128]{2,1,0:T(8,128)(2,1)S(1)} %slice.41.kv0_ref), channel_id=1, source_target_pairs={{0,64},{32,0},{64,32},{96,160},{128,96},{160,128},{192,256},{224,1... | collective-permute-start | bytes 1179656 | tf_op jit(solution)/shard_map/ppermute | solution.py:277
  55.7 13.3 %collective-permute-start.5 = (bf16[16,96,128]{2,1,0:T(8,128)(2,1)S(1)}, bf16[16,96,128]{2,1,0:T(8,128)(2,1)S(1)}, u32[]{:S(2)}, u32[]{:S(2)}) collective-permute-start(bf16[16,96,128]{2,1,0:T(8,128)(2,1)S(1)} %slice.41.kv0_ref), channel_id=1, source_target_pairs={{0,32},{32,64},{64,0},{96,128},{128,160},{160,96},{192,224},{224,2... | collective-permute-start | bytes 1179656 | tf_op jit(solution)/shard_map/ppermute | solution.py:277
  57.9 0.7 copy-start.1
  58.7 22.4 %collective-permute-start.7 = (bf16[80,640]{1,0:T(8,128)(2,1)S(1)}, bf16[80,640]{1,0:T(8,128)(2,1)S(1)}, u32[]{:S(2)}, u32[]{:S(2)}) collective-permute-start(bf16[80,640]{1,0:T(8,128)(2,1)S(1)} %collective-permute-done.3.refs_1_), channel_id=1, source_target_pairs={{0,32},{32,64},{64,96},{96,128},{128,160},{160,192},{192,224},{224... | collective-permute-start | bytes 307208 | tf_op jit(solution)/shard_map/ppermute | solution.py:241
  61.5 19.6 %collective-permute-start.8 = (bf16[80,640]{1,0:T(8,128)(2,1)S(1)}, bf16[80,640]{1,0:T(8,128)(2,1)S(1)}, u32[]{:S(2)}, u32[]{:S(2)}) collective-permute-start(bf16[80,640]{1,0:T(8,128)(2,1)S(1)} %collective-permute-done.4.refs_9_), channel_id=1, source_target_pairs={{0,480},{32,0},{64,32},{96,64},{128,96},{160,128},{192,160},{224,1... | collective-permute-start | bytes 307208 | tf_op jit(solution)/shard_map/ppermute | solution.py:243
  81.1 20.3 %all-to-all-start.2 = ((bf16[4,864,128]{2,1,0:T(8,128)(2,1)}), bf16[4,864,128]{2,1,0:T(8,128)(2,1)S(1)}, u32[]{:S(2)}, u32[]{:S(2)}) async-start(bf16[4,864,128]{2,1,0:T(8,128)(2,1)} %shard_map.56), calls=%async_computation.2 | async-start | bytes 1769472 | tf_op jit(solution)/shard_map/all_to_all | solution.py:305
  85.0 6.7 %collective-permute-start.9 = (bf16[80,640]{1,0:T(8,128)(2,1)S(1)}, bf16[80,640]{1,0:T(8,128)(2,1)S(1)}, u32[]{:S(2)}, u32[]{:S(2)}) collective-permute-start(bf16[80,640]{1,0:T(8,128)(2,1)S(1)} %collective-permute-done.7.refs_2_), channel_id=1, source_target_pairs={{0,32},{32,64},{64,96},{96,128},{128,160},{160,192},{192,224},{224... | collective-permute-start | bytes 307208 | tf_op jit(solution)/shard_map/ppermute | solution.py:241
  89.8 6.3 %collective-permute-start.11 = (bf16[80,640]{1,0:T(8,128)(2,1)S(1)}, bf16[80,640]{1,0:T(8,128)(2,1)S(1)}, u32[]{:S(2)}, u32[]{:S(2)}) collective-permute-start(bf16[80,640]{1,0:T(8,128)(2,1)S(1)} %collective-permute-done.8.refs_10_), channel_id=1, source_target_pairs={{0,480},{32,0},{64,32},{96,64},{128,96},{160,128},{192,160},{224,1... | collective-permute-start | bytes 307208 | tf_op jit(solution)/shard_map/ppermute | solution.py:243
  91.7 11.0 %collective-permute-start.10 = (bf16[80,640]{1,0:T(8,128)(2,1)S(1)}, bf16[80,640]{1,0:T(8,128)(2,1)S(1)}, u32[]{:S(2)}, u32[]{:S(2)}) collective-permute-start(bf16[80,640]{1,0:T(8,128)(2,1)S(1)} %collective-permute-done.9.refs_3_), channel_id=1, source_target_pairs={{0,32},{32,64},{64,96},{96,128},{128,160},{160,192},{192,224},{224... | collective-permute-start | bytes 307208 | tf_op jit(solution)/shard_map/ppermute | solution.py:241
  96.1 7.0 %collective-permute-start.12 = (bf16[80,640]{1,0:T(8,128)(2,1)S(1)}, bf16[80,640]{1,0:T(8,128)(2,1)S(1)}, u32[]{:S(2)}, u32[]{:S(2)}) collective-permute-start(bf16[80,640]{1,0:T(8,128)(2,1)S(1)} %collective-permute-done.11.refs_11_), channel_id=1, source_target_pairs={{0,480},{32,0},{64,32},{96,64},{128,96},{160,128},{192,160},{224,1... | collective-permute-start | bytes 307208 | tf_op jit(solution)/shard_map/ppermute | solution.py:243
  103.1 32.4 %all-to-all-start.3 = ((bf16[16,48,128]{2,1,0:T(8,128)(2,1)}), bf16[16,48,128]{2,1,0:T(8,128)(2,1)S(1)}, u32[]{:S(2)}, u32[]{:S(2)}) async-start(bf16[16,48,128]{2,1,0:T(8,128)(2,1)} %shard_map.57), calls=%async_computation.3 | async-start | bytes 393216 | tf_op jit(solution)/shard_map/all_to_all | solution.py:309
  119.2 8.8 %collective-permute-start.13 = (bf16[80,640]{1,0:T(8,128)(2,1)S(1)}, bf16[80,640]{1,0:T(8,128)(2,1)S(1)}, u32[]{:S(2)}, u32[]{:S(2)}) collective-permute-start(bf16[80,640]{1,0:T(8,128)(2,1)S(1)} %collective-permute-done.10.refs_4_), channel_id=1, source_target_pairs={{0,32},{32,64},{64,96},{96,128},{128,160},{160,192},{192,224},{224... | collective-permute-start | bytes 307208 | tf_op jit(solution)/shard_map/ppermute | solution.py:241
  122.5 10.8 %collective-permute-start.15 = (bf16[80,640]{1,0:T(8,128)(2,1)S(1)}, bf16[80,640]{1,0:T(8,128)(2,1)S(1)}, u32[]{:S(2)}, u32[]{:S(2)}) collective-permute-start(bf16[80,640]{1,0:T(8,128)(2,1)S(1)} %collective-permute-done.12.refs_12_), channel_id=1, source_target_pairs={{0,480},{32,0},{64,32},{96,64},{128,96},{160,128},{192,160},{224,1... | collective-permute-start | bytes 307208 | tf_op jit(solution)/shard_map/ppermute | solution.py:243
  128.0 8.6 %collective-permute-start.14 = (bf16[80,640]{1,0:T(8,128)(2,1)S(1)}, bf16[80,640]{1,0:T(8,128)(2,1)S(1)}, u32[]{:S(2)}, u32[]{:S(2)}) collective-permute-start(bf16[80,640]{1,0:T(8,128)(2,1)S(1)} %collective-permute-done.13.refs_5_), channel_id=1, source_target_pairs={{0,32},{32,64},{64,96},{96,128},{128,160},{160,192},{192,224},{224... | collective-permute-start | bytes 307208 | tf_op jit(solution)/shard_map/ppermute | solution.py:241
  133.4 5.4 %collective-permute-start.16 = (bf16[80,640]{1,0:T(8,128)(2,1)S(1)}, bf16[80,640]{1,0:T(8,128)(2,1)S(1)}, u32[]{:S(2)}, u32[]{:S(2)}) collective-permute-start(bf16[80,640]{1,0:T(8,128)(2,1)S(1)} %collective-permute-done.15.refs_13_), channel_id=1, source_target_pairs={{0,480},{32,0},{64,32},{96,64},{128,96},{160,128},{192,160},{224,1... | collective-permute-start | bytes 307208 | tf_op jit(solution)/shard_map/ppermute | solution.py:243
  138.8 17.4 %all-to-all-start.4 = ((bf16[4,720,128]{2,1,0:T(8,128)(2,1)}), bf16[4,720,128]{2,1,0:T(8,128)(2,1)S(1)}, u32[]{:S(2)}, u32[]{:S(2)}) async-start(bf16[4,720,128]{2,1,0:T(8,128)(2,1)} %shard_map.58), calls=%async_computation.4 | async-start | bytes 1474560 | tf_op jit(solution)/shard_map/all_to_all | solution.py:313
  142.9 6.6 %collective-permute-start.17 = (bf16[80,640]{1,0:T(8,128)(2,1)S(1)}, bf16[80,640]{1,0:T(8,128)(2,1)S(1)}, u32[]{:S(2)}, u32[]{:S(2)}) collective-permute-start(bf16[80,640]{1,0:T(8,128)(2,1)S(1)} %collective-permute-done.14.refs_6_), channel_id=1, source_target_pairs={{0,32},{32,64},{64,96},{96,128},{128,160},{160,192},{192,224},{224... | collective-permute-start | bytes 307208 | tf_op jit(solution)/shard_map/ppermute | solution.py:241
  145.2 7.4 %collective-permute-start.19 = (bf16[80,640]{1,0:T(8,128)(2,1)S(1)}, bf16[80,640]{1,0:T(8,128)(2,1)S(1)}, u32[]{:S(2)}, u32[]{:S(2)}) collective-permute-start(bf16[80,640]{1,0:T(8,128)(2,1)S(1)} %collective-permute-done.16.refs_14_), channel_id=1, source_target_pairs={{0,480},{32,0},{64,32},{96,64},{128,96},{160,128},{192,160},{224,1... | collective-permute-start | bytes 307208 | tf_op jit(solution)/shard_map/ppermute | solution.py:243
  149.6 6.6 %collective-permute-start.18 = (bf16[80,640]{1,0:T(8,128)(2,1)S(1)}, bf16[80,640]{1,0:T(8,128)(2,1)S(1)}, u32[]{:S(2)}, u32[]{:S(2)}) collective-permute-start(bf16[80,640]{1,0:T(8,128)(2,1)S(1)} %collective-permute-done.17.refs_7_), channel_id=1, source_target_pairs={{0,32},{32,64},{64,96},{96,128},{128,160},{160,192},{192,224},{224... | collective-permute-start | bytes 307208 | tf_op jit(solution)/shard_map/ppermute | solution.py:241
  156.2 10.7 %collective-permute-start.20 = (bf16[4,720,128]{2,1,0:T(8,128)(2,1)S(1)}, bf16[4,720,128]{2,1,0:T(8,128)(2,1)S(1)}, u32[]{:S(2)}, u32[]{:S(2)}) collective-permute-start(bf16[4,720,128]{2,1,0:T(8,128)(2,1)S(1)} %all-to-all-done.4.mine_ref), channel_id=1, source_target_pairs={{0,1},{1,0},{2,3},{3,2},{4,5},{5,4},{6,7},{7,6},{8,9},{9,8},{10,11... | collective-permute-start | bytes 2211848 | tf_op jit(solution)/shard_map/ppermute | solution.py:317

commit v6 on v5

--- a/solution.py
+++ b/solution.py
@@ -27,8 +27,10 @@
 GRANULE = 16
 
 
-def vmem_call(body, mebibytes, shapes, *operands, scalars=None, scratch=()):
+def vmem_call(body, mebibytes, shapes, *operands, scalars=None, left=(), scratch=()):
     specs = [pl.BlockSpec(memory_space=pltpu.VMEM)] * len(operands)
+    specs += [pl.BlockSpec(memory_space=pl.ANY)] * len(left)
+    operands += tuple(left)
     if scalars is not None:
         specs = [pl.BlockSpec(memory_space=pltpu.SMEM)] + specs
         operands = (scalars,) + operands
@@ -37,7 +39,7 @@
         out_shape=[jax.ShapeDtypeStruct(shape, BF16) for shape in shapes],
         in_specs=specs,
         out_specs=[pl.BlockSpec(memory_space=pltpu.VMEM)] * len(shapes),
-        scratch_shapes=[pltpu.VMEM(shape, BF16) for shape in scratch],
+        scratch_shapes=list(scratch),
         compiler_params=pltpu.CompilerParams(vmem_limit_bytes=mebibytes * 1024 * 1024),
     )(*operands)
 
@@ -193,12 +195,24 @@
 
 
 def project(place_ref, mine_ref, other_ref, *refs):
-    parts, out_ref, weight_ref = refs[:Z], refs[Z], refs[Z + 1]
+    half = Z // 2
+    own, others, out_ref, weight_ref, sems = refs
     core, side, plane = place_ref[0], place_ref[1], place_ref[2]
-    for n, part in enumerate(parts):
-        turn = Z - n if n <= Z // 2 else n - Z // 2
-        first = pl.multiple_of(lax.rem(plane + turn, Z) * part.shape[0], GRANULE)
-        weight_ref[pl.ds(first, part.shape[0]), :] = part[...]
+    depth = weight_ref.shape[0] // Z
+    way = 1 - 2 * core
+    copies = []
+    for n in range(half + 1):
+        pairs = [(own.at[n], Z - way * n)]
+        if 0 < n < half:
+            pairs.append((others.at[n - 1], Z + way * n))
+        for source, turn in pairs:
+            first = pl.multiple_of(lax.rem(plane + turn, Z) * depth, GRANULE)
+            place = weight_ref.at[pl.ds(first, depth), :]
+            copies.append(pltpu.make_async_copy(source, place, sems.at[len(copies)]))
+    for copy in copies:
+        copy.start()
+    for copy in copies:
+        copy.wait()
     places = [lax.rem(side + (X + 1) - m, X + 1) * GRANULE for m in range(X + 1)]
     plane_rows = (X + 1) * GRANULE
     pieces = SHARE // GRANULE
@@ -234,20 +248,19 @@
 
 class Ring:
     def __init__(self, block):
-        self.up, self.down = [block], [block]
+        self.came = [jnp.stack([block, swap_cores(block)])]
 
     def step(self):
-        if len(self.up) <= Z // 2:
-            self.up.append(lax.ppermute(self.up[-1], "z", [(z, (z + 1) % Z) for z in range(Z)]))
-        if len(self.down) < Z // 2:
-            self.down.append(lax.ppermute(self.down[-1], "z", [(z, (z - 1) % Z) for z in range(Z)]))
+        turn = [(C * z + c, C * ((z + 1 - 2 * c) % Z) + c) for z in range(Z) for c in range(C)]
+        self.came.append(lax.ppermute(self.came[-1], ("z", "c"), turn))
 
     def meet(self, value):
-        value, self.up[-1], self.down[-1] = lax.optimization_barrier((value, self.up[-1], self.down[-1]))
+        value, self.came[-1] = lax.optimization_barrier((value, self.came[-1]))
         return value
 
-    def blocks(self):
-        return self.up + self.down[1:]
+
+def swap_cores(value):
+    return lax.ppermute(value, "c", [(0, 1), (1, 0)])
 
 
 def local(queries, keys_in, values, cluster_ids, out_weight):
@@ -275,6 +288,7 @@
         for k in (1, 2)
     ]
     kv_others = [lax.ppermute(kv, "z", turn) for turn in turns]
+    ring.step()
     ring.step()
     query = jnp.broadcast_to(here[:, :SLOT, :].reshape(1, Z * SLOT, HEAD), (X, Z * SLOT, HEAD))
     query = lax.all_to_all(query, "x", 0, 0, tiled=True)
@@ -293,7 +307,7 @@
     )
     (part,) = vmem_call(
         attend,
-        32,
+        18,
         [(X, (Z + 2) * SLOT, HEAD)],
         query,
         kv,
@@ -312,18 +326,19 @@
     (packed,) = vmem_call(assemble, 8, [(Y, (X + 1) * PARTS * SLOT, HEAD)], joined)
     packed = lax.all_to_all(ring.meet(packed), "y", 0, 0, tiled=True)
     ring.step()
-    ring.step()
+    rows = swap_cores(jnp.stack([block[1] for block in ring.came[1 : Z // 2]]))
+    packed, rows = lax.optimization_barrier((packed, rows))
     packed = ring.meet(packed)
-    others = lax.ppermute(packed, "c", [(0, 1), (1, 0)])
+    others = swap_cores(packed)
     (partial,) = vmem_call(
         project,
-        24,
+        16,
         [(X, TOK, width)],
         packed,
         others,
-        *ring.blocks(),
         scalars=jnp.stack([core, side, plane]),
-        scratch=[(Z * out_weight.shape[0], width)],
+        left=[jnp.stack([block[0] for block in ring.came]), rows],
+        scratch=[pltpu.VMEM((Z * out_weight.shape[0], width), BF16), pltpu.SemaphoreType.DMA((Z,))],
     )
     partial = lax.all_to_all(partial, "x", 0, 0, tiled=True)
     return jnp.sum(partial.astype(F32), axis=0).astype(BF16)

time: 187 us -> 191 us (1.021)
  starting transfers between devices: 120 us -> 96.5 us
  waiting for transfers between devices: 27.8 us -> 50.6 us
  local copies, waits for them, and re-layouts: 2.06 us -> 6.15 us
    ppermute x16 -> x11, starting transfers between devices: 61.2 us -> 38.1 us  [the longest x8 25.3 us: step(): self.came.append(lax.ppermute(self.came[-1], ('z', 'c'), turn))]
    ppermute x16 -> x11, waiting for transfers between devices: 20.5 us -> 39.1 us  [the longest x8 36.5 us: step(): self.came.append(lax.ppermute(self.came[-1], ('z', 'c'), turn))]
    all_to_all x1, waiting for transfers between devices: 0.01 us -> 9.53 us  [local(): packed = lax.all_to_all(ring.meet(packed), 'y', 0, 0, tiled=True)]
    unnamed x8 -> x16, local copies, waits for them, and re-layouts: 0.61 us -> 4.67 us
    ppermute x2, waiting for transfers between devices: 3.75 us -> 0.01 us  [local(): kv_others = [lax.ppermute(kv, 'z', turn) for turn in turns]]
    all_to_all x1, starting transfers between devices: 16.2 us -> 13.3 us  [local(): joined = lax.all_to_all(ring.meet(joined), 'z', 0, 0, tiled=True)]
  transfers between devices with their start and end apart: 26 -> 21, of which waited for: 12 -> 11; matrix products, arithmetic and copies ran while one was open for 0% -> 2% of each run, Pallas kernels for 8% -> 7%
where the time goes in v6:
time: 191 us; the launch traced here: 190 us
  starting transfers between devices  96.5 us (51%)
  waiting for transfers between devices  50.6 us (26%)
  Pallas kernels  21.2 us (11%)
  blocking collectives  14.1 us (7%)
  local copies, waits for them, and re-layouts  6.15 us (3%)
    ppermute x8, waiting for transfers between devices, step(): self.came.append(lax.ppermute(self.came[-1], ('z', 'c'), turn))  36.5 us
    ppermute x8, starting transfers between devices, step(): self.came.append(lax.ppermute(self.came[-1], ('z', 'c'), turn))  25.3 us
    pallas_call x5, Pallas kernels, vmem_call(): pl.pallas_call(body, out_shape=[jax.ShapeDtypeStruct(shape, BF16) for sha...  21.2 us
    all_to_all x1, starting transfers between devices, local(): here = lax.all_to_all(send, 'z', 0, 0, tiled=True)  15.9 us
    all_to_all x1, blocking collectives, local(): partial = lax.all_to_all(partial, 'x', 0, 0, tiled=True)  14.1 us
    all_to_all x1, starting transfers between devices, local(): joined = lax.all_to_all(ring.meet(joined), 'z', 0, 0, tiled=True)  13.3 us
    ppermute x3, starting transfers between devices, swap_cores(): return lax.ppermute(value, 'c', [(0, 1), (1, 0)])  12.8 us
    ppermute x3, starting transfers between devices, share_rows(): lax.ppermute(granules[n], 'x', [(x, (x + n) % X) for x in range(X)])  10.5 us
  transfers between devices with their start and end apart: 21, of which 11 were waited for; matrix products, arithmetic and copies ran while one was open for 2% of the time, Pallas kernels for 7%

profile of v6, /device:TPU:1, one launch (start us, length us, event | category | flops | bytes accessed | tf_op | source)
XLA Modules:
  0.0 189.9 jit_solution(16445794606610755710)
XLA Ops:
  0.0 2.2 %shard_map.55 = (bf16[16,144,128]{2,1,0:T(8,128)(2,1)}, bf16[5,16,640]{2,1,0:T(8,128)(2,1)}) custom-call(bf16[128,640]{1,0:T(8,128)(2,1)} %q_ref.1, bf16[128,640]{1,0:T(8,128)(2,1)} %k_ref.1, bf16[128,640]{1,0:T(8,128)(2,1)} %v_ref.1, s32[1,128]{1,0:T(1,128)} %bitcast.24, bf16[80,640]{1,0:T(8,128)(2,1)} %weight_ref.1), custom_call_target="tpu_custom_call" | custom-call | tf_op jit(solution)/shard_map/pallas_call | solution.py:37
  2.2 15.9 %all-to-all-start = ((bf16[16,144,128]{2,1,0:T(8,128)(2,1)}), bf16[16,144,128]{2,1,0:T(8,128)(2,1)S(1)}, u32[]{:S(2)}, u32[]{:S(2)}) async-start(bf16[16,144,128]{2,1,0:T(8,128)(2,1)} %get-tuple-element.19), calls=%async_computation | async-start | bytes 1179648 | tf_op jit(solution)/shard_map/all_to_all | solution.py:281
  18.1 3.1 %collective-permute-start = (bf16[16,640]{1,0:T(8,128)(2,1)S(1)}, bf16[16,640]{1,0:T(8,128)(2,1)S(1)}, u32[]{:S(2)}, u32[]{:S(2)}) collective-permute-start(bf16[16,640]{1,0:T(8,128)(2,1)S(1)} %get-tuple-element.49), channel_id=1, source_target_pairs={{0,8},{8,16},{16,24},{24,0},{1,9},{9,17},{17,25},{25,1},{2,10},{10... | collective-permute-start | bytes 61448 | tf_op jit(solution)/shard_map/ppermute | solution.py:245
  21.2 4.4 %collective-permute-start.1 = (bf16[16,640]{1,0:T(8,128)(2,1)S(1)}, bf16[16,640]{1,0:T(8,128)(2,1)S(1)}, u32[]{:S(2)}, u32[]{:S(2)}) collective-permute-start(bf16[16,640]{1,0:T(8,128)(2,1)S(1)} %get-tuple-element.48), channel_id=1, source_target_pairs={{0,16},{8,24},{16,0},{24,8},{1,17},{9,25},{17,1},{25,9},{2,18},{10... | collective-permute-start | bytes 61448 | tf_op jit(solution)/shard_map/ppermute | solution.py:245
  25.6 3.1 %collective-permute-start.2 = (bf16[16,640]{1,0:T(8,128)(2,1)S(1)}, bf16[16,640]{1,0:T(8,128)(2,1)S(1)}, u32[]{:S(2)}, u32[]{:S(2)}) collective-permute-start(bf16[16,640]{1,0:T(8,128)(2,1)S(1)} %get-tuple-element.47), channel_id=1, source_target_pairs={{0,24},{8,0},{16,8},{24,16},{1,25},{9,1},{17,9},{25,17},{2,26},{10... | collective-permute-start | bytes 61448 | tf_op jit(solution)/shard_map/ppermute | solution.py:245
  28.7 1.7 collective-permute-done.2
  30.4 4.3 %collective-permute-start.3 = (bf16[80,640]{1,0:T(8,128)(2,1)S(1)}, bf16[80,640]{1,0:T(8,128)(2,1)S(1)}, u32[]{:S(2)}, u32[]{:S(2)}) collective-permute-start(bf16[80,640]{1,0:T(8,128)(2,1)S(1)} %constant_dynamic-update-slice_fusion), channel_id=1, source_target_pairs={{0,1},{1,0},{2,3},{3,2},{4,5},{5,4},{6,7},{7,6},{8,9},{9,8},{10,11... | collective-permute-start | bytes 307208 | tf_op jit(solution)/shard_map/ppermute | solution.py:263
  35.6 4.8 %collective-permute-start.4 = (bf16[2,80,640]{2,1,0:T(8,128)(2,1)S(1)}, bf16[2,80,640]{2,1,0:T(8,128)(2,1)S(1)}, u32[]{:S(2)}, u32[]{:S(2)}) collective-permute-start(bf16[2,80,640]{2,1,0:T(8,128)(2,1)S(1)} %pad_maximum_fusion), channel_id=1, source_target_pairs={{0,32},{1,481},{32,64},{33,1},{64,96},{65,33},{96,128},{97,65},{12... | collective-permute-start | bytes 614408 | tf_op jit(solution)/shard_map/ppermute | solution.py:255
  40.5 7.6 %collective-permute-done.4 = bf16[2,80,640]{2,1,0:T(8,128)(2,1)S(1)} collective-permute-done((bf16[2,80,640]{2,1,0:T(8,128)(2,1)S(1)}, bf16[2,80,640]{2,1,0:T(8,128)(2,1)S(1)}, u32[]{:S(2)}, u32[]{:S(2)}) %collective-permute-start.4) | collective-permute-done | bytes 204832 | tf_op jit(solution)/shard_map/ppermute | solution.py:255
  49.1 4.1 %all-to-all-start.1 = ((bf16[4,768,128]{2,1,0:T(8,128)(2,1)}), bf16[4,768,128]{2,1,0:T(8,128)(2,1)S(1)}, u32[]{:S(2)}, u32[]{:S(2)}) async-start(bf16[4,768,128]{2,1,0:T(8,128)(2,1)} %broadcast_in_dim.10), calls=%async_computation.1 | async-start | bytes 1572864 | tf_op jit(solution)/shard_map/all_to_all | solution.py:294
  53.2 3.4 %collective-permute-start.5 = (bf16[16,96,128]{2,1,0:T(8,128)(2,1)S(1)}, bf16[16,96,128]{2,1,0:T(8,128)(2,1)S(1)}, u32[]{:S(2)}, u32[]{:S(2)}) collective-permute-start(bf16[16,96,128]{2,1,0:T(8,128)(2,1)S(1)} %slice.86.kv0_ref), channel_id=1, source_target_pairs={{0,32},{32,64},{64,0},{96,128},{128,160},{160,96},{192,224},{224,2... | collective-permute-start | bytes 1179656 | tf_op jit(solution)/shard_map/ppermute | solution.py:290
  56.6 2.8 %collective-permute-start.6 = (bf16[16,96,128]{2,1,0:T(8,128)(2,1)S(1)}, bf16[16,96,128]{2,1,0:T(8,128)(2,1)S(1)}, u32[]{:S(2)}, u32[]{:S(2)}) collective-permute-start(bf16[16,96,128]{2,1,0:T(8,128)(2,1)S(1)} %slice.86.kv0_ref), channel_id=1, source_target_pairs={{0,64},{32,0},{64,32},{96,160},{128,96},{160,128},{192,256},{224,1... | collective-permute-start | bytes 1179656 | tf_op jit(solution)/shard_map/ppermute | solution.py:290
  59.4 1.9 %collective-permute-start.7 = (bf16[2,80,640]{2,1,0:T(8,128)(2,1)S(1)}, bf16[2,80,640]{2,1,0:T(8,128)(2,1)S(1)}, u32[]{:S(2)}, u32[]{:S(2)}) collective-permute-start(bf16[2,80,640]{2,1,0:T(8,128)(2,1)S(1)} %collective-permute-done.4), channel_id=1, source_target_pairs={{0,32},{1,481},{32,64},{33,1},{64,96},{65,33},{96,128},{97,65},{12... | collective-permute-start | bytes 614408 | tf_op jit(solution)/shard_map/ppermute | solution.py:255
  61.4 16.0 %collective-permute-done.7 = bf16[2,80,640]{2,1,0:T(8,128)(2,1)S(1)} collective-permute-done((bf16[2,80,640]{2,1,0:T(8,128)(2,1)S(1)}, bf16[2,80,640]{2,1,0:T(8,128)(2,1)S(1)}, u32[]{:S(2)}, u32[]{:S(2)}) %collective-permute-start.7) | collective-permute-done | bytes 204832 | tf_op jit(solution)/shard_map/ppermute | solution.py:255
  77.5 1.9 %collective-permute-start.8 = (bf16[2,80,640]{2,1,0:T(8,128)(2,1)S(1)}, bf16[2,80,640]{2,1,0:T(8,128)(2,1)S(1)}, u32[]{:S(2)}, u32[]{:S(2)}) collective-permute-start(bf16[2,80,640]{2,1,0:T(8,128)(2,1)S(1)} %collective-permute-done.7), channel_id=1, source_target_pairs={{0,32},{1,481},{32,64},{33,1},{64,96},{65,33},{96,128},{97,65},{12... | collective-permute-start | bytes 614408 | tf_op jit(solution)/shard_map/ppermute | solution.py:255
  79.9 11.6 %shard_map.56 = bf16[4,864,128]{2,1,0:T(8,128)(2,1)} custom-call(s32[1]{0:T(128)} %bitcast.3.third_ref, bf16[4,768,128]{2,1,0:T(8,128)(2,1)S(1)} %all-to-all-done.1.q_ref, bf16[16,96,128]{2,1,0:T(8,128)(2,1)S(1)} %slice.86.kv0_ref, bf16[16,96,128]{2,1,0:T(8,128)(2,1)S(1)} %collective-permute-done.5.kv1_ref, ...), custom_call_target="tpu_custom_call" | custom-call | tf_op jit(solution)/shard_map/pallas_call | solution.py:37
  91.5 4.2 %all-to-all-start.2 = ((bf16[4,864,128]{2,1,0:T(8,128)(2,1)}), bf16[4,864,128]{2,1,0:T(8,128)(2,1)S(1)}, u32[]{:S(2)}, u32[]{:S(2)}) async-start(bf16[4,864,128]{2,1,0:T(8,128)(2,1)} %shard_map.56), calls=%async_computation.2 | async-start | bytes 1769472 | tf_op jit(solution)/shard_map/all_to_all | solution.py:319
  95.8 2.6 %collective-permute-start.9 = (bf16[2,80,640]{2,1,0:T(8,128)(2,1)S(1)}, bf16[2,80,640]{2,1,0:T(8,128)(2,1)S(1)}, u32[]{:S(2)}, u32[]{:S(2)}) collective-permute-start(bf16[2,80,640]{2,1,0:T(8,128)(2,1)S(1)} %collective-permute-done.8), channel_id=1, source_target_pairs={{0,32},{1,481},{32,64},{33,1},{64,96},{65,33},{96,128},{97,65},{12... | collective-permute-start | bytes 614408 | tf_op jit(solution)/shard_map/ppermute | solution.py:255
  99.0 3.5 %collective-permute-done.9 = bf16[2,80,640]{2,1,0:T(8,128)(2,1)S(1)} collective-permute-done((bf16[2,80,640]{2,1,0:T(8,128)(2,1)S(1)}, bf16[2,80,640]{2,1,0:T(8,128)(2,1)S(1)}, u32[]{:S(2)}, u32[]{:S(2)}) %collective-permute-start.9) | collective-permute-done | bytes 204832 | tf_op jit(solution)/shard_map/ppermute | solution.py:255
  102.6 3.8 %collective-permute-start.10 = (bf16[2,80,640]{2,1,0:T(8,128)(2,1)S(1)}, bf16[2,80,640]{2,1,0:T(8,128)(2,1)S(1)}, u32[]{:S(2)}, u32[]{:S(2)}) collective-permute-start(bf16[2,80,640]{2,1,0:T(8,128)(2,1)S(1)} %collective-permute-done.9), channel_id=1, source_target_pairs={{0,32},{1,481},{32,64},{33,1},{64,96},{65,33},{96,128},{97,65},{12... | collective-permute-start | bytes 614408 | tf_op jit(solution)/shard_map/ppermute | solution.py:255
  109.4 13.3 %all-to-all-start.3 = ((bf16[16,48,128]{2,1,0:T(8,128)(2,1)}), bf16[16,48,128]{2,1,0:T(8,128)(2,1)S(1)}, u32[]{:S(2)}, u32[]{:S(2)}) async-start(bf16[16,48,128]{2,1,0:T(8,128)(2,1)} %shard_map.57), calls=%async_computation.3 | async-start | bytes 393216 | tf_op jit(solution)/shard_map/all_to_all | solution.py:323
  124.0 4.5 %collective-permute-start.11 = (bf16[2,80,640]{2,1,0:T(8,128)(2,1)S(1)}, bf16[2,80,640]{2,1,0:T(8,128)(2,1)S(1)}, u32[]{:S(2)}, u32[]{:S(2)}) collective-permute-start(bf16[2,80,640]{2,1,0:T(8,128)(2,1)S(1)} %collective-permute-done.10), channel_id=1, source_target_pairs={{0,32},{1,481},{32,64},{33,1},{64,96},{65,33},{96,128},{97,65},{12... | collective-permute-start | bytes 614408 | tf_op jit(solution)/shard_map/ppermute | solution.py:255
  129.1 6.9 %collective-permute-done.11 = bf16[2,80,640]{2,1,0:T(8,128)(2,1)S(1)} collective-permute-done((bf16[2,80,640]{2,1,0:T(8,128)(2,1)S(1)}, bf16[2,80,640]{2,1,0:T(8,128)(2,1)S(1)}, u32[]{:S(2)}, u32[]{:S(2)}) %collective-permute-start.11) | collective-permute-done | bytes 204832 | tf_op jit(solution)/shard_map/ppermute | solution.py:255
  136.0 3.8 %collective-permute-start.12 = (bf16[2,80,640]{2,1,0:T(8,128)(2,1)S(1)}, bf16[2,80,640]{2,1,0:T(8,128)(2,1)S(1)}, u32[]{:S(2)}, u32[]{:S(2)}) collective-permute-start(bf16[2,80,640]{2,1,0:T(8,128)(2,1)S(1)} %collective-permute-done.11), channel_id=1, source_target_pairs={{0,32},{1,481},{32,64},{33,1},{64,96},{65,33},{96,128},{97,65},{12... | collective-permute-start | bytes 614408 | tf_op jit(solution)/shard_map/ppermute | solution.py:255
  143.8 5.5 %collective-permute-start.13 = (bf16[7,80,640]{2,1,0:T(8,128)(2,1)}, bf16[7,80,640]{2,1,0:T(8,128)(2,1)S(1)}, u32[]{:S(2)}, u32[]{:S(2)}) collective-permute-start(bf16[7,80,640]{2,1,0:T(8,128)(2,1)} %get-tuple-element.34), channel_id=1, source_target_pairs={{0,1},{1,0},{2,3},{3,2},{4,5},{5,4},{6,7},{7,6},{8,9},{9,8},{10,11... | collective-permute-start | bytes 2150408 | tf_op jit(solution)/shard_map/ppermute | solution.py:263
  149.3 4.2 %all-to-all-start.4 = ((bf16[4,720,128]{2,1,0:T(8,128)(2,1)}), bf16[4,720,128]{2,1,0:T(8,128)(2,1)S(1)}, u32[]{:S(2)}, u32[]{:S(2)}) async-start(bf16[4,720,128]{2,1,0:T(8,128)(2,1)} %shard_map.58), calls=%async_computation.4 | async-start | bytes 1474560 | tf_op jit(solution)/shard_map/all_to_all | solution.py:327
  153.5 2.1 %collective-permute-start.14 = (bf16[2,80,640]{2,1,0:T(8,128)(2,1)S(1)}, bf16[2,80,640]{2,1,0:T(8,128)(2,1)S(1)}, u32[]{:S(2)}, u32[]{:S(2)}) collective-permute-start(bf16[2,80,640]{2,1,0:T(8,128)(2,1)S(1)} %collective-permute-done.12), channel_id=1, source_target_pairs={{0,32},{1,481},{32,64},{33,1},{64,96},{65,33},{96,128},{97,65},{12... | collective-permute-start | bytes 614408 | tf_op jit(solution)/shard_map/ppermute | solution.py:255
  155.6 9.5 %all-to-all-done.4.mine_ref = bf16[4,720,128]{2,1,0:T(8,128)(2,1)S(1)} async-done(((bf16[4,720,128]{2,1,0:T(8,128)(2,1)}), bf16[4,720,128]{2,1,0:T(8,128)(2,1)S(1)}, u32[]{:S(2)}, u32[]{:S(2)}) %all-to-all-start.4) | async-done | bytes 737312 | tf_op jit(solution)/shard_map/all_to_all | solution.py:327
  165.2 3.0 %collective-permute-start.15 = (bf16[4,720,128]{2,1,0:T(8,128)(2,1)S(1)}, bf16[4,720,128]{2,1,0:T(8,128)(2,1)S(1)}, u32[]{:S(2)}, u32[]{:S(2)}) collective-permute-start(bf16[4,720,128]{2,1,0:T(8,128)(2,1)S(1)} %all-to-all-done.4.mine_ref), channel_id=1, source_target_pairs={{0,1},{1,0},{2,3},{3,2},{4,5},{5,4},{6,7},{7,6},{8,9},{9,8},{10,11... | collective-permute-start | bytes 2211848 | tf_op jit(solution)/shard_map/ppermute | solution.py:263
  168.3 1.7 collective-permute-done.15.other_ref
  170.0 5.0 %shard_map.59 = bf16[4,128,640]{2,1,0:T(8,128)(2,1)S(1)} custom-call(s32[3]{0:T(128)S(1)} %pad_add_fusion.place_ref, bf16[4,720,128]{2,1,0:T(8,128)(2,1)S(1)} %all-to-all-done.4.mine_ref, bf16[4,720,128]{2,1,0:T(8,128)(2,1)S(1)} %collective-permute-done.15.other_ref, bf16[9,80,640]{2,1,0:T(8,128)(2,1)S(1)} %slice_dynamic-update-slice_fusion.6.refs_0_, ...), custom_call_target="tpu_custom_call" | custom-call | tf_op jit(solution)/shard_map/pallas_call | solution.py:37
  175.0 14.1 %all_to_all.30 = bf16[4,128,640]{2,1,0:T(8,128)(2,1)S(1)} all-to-all(bf16[4,128,640]{2,1,0:T(8,128)(2,1)S(1)} %shard_map.59), channel_id=1, replica_groups=mesh['z'=16,'x'=4,'y'=4,'c'=2] {'x'}, dimensions={0} | all-to-all | bytes 1310720 | tf_op jit(solution)/shard_map/all_to_all | solution.py:343
  (53 shorter events, 13.1 us)
Async XLA Ops:
  2.2 15.9 %copy-start = (bf16[5,16,640]{2,1,0:T(8,128)(2,1)S(1)}, bf16[5,16,640]{2,1,0:T(8,128)(2,1)}, u32[]{:S(2)}) copy-start(bf16[5,16,640]{2,1,0:T(8,128)(2,1)} %get-tuple-element.20) | copy-start | bytes 307204
  2.2 45.9 %all-to-all-start = ((bf16[16,144,128]{2,1,0:T(8,128)(2,1)}), bf16[16,144,128]{2,1,0:T(8,128)(2,1)S(1)}, u32[]{:S(2)}, u32[]{:S(2)}) async-start(bf16[16,144,128]{2,1,0:T(8,128)(2,1)} %get-tuple-element.19), calls=%async_computation | async-start | bytes 1179648 | tf_op jit(solution)/shard_map/all_to_all | solution.py:281
  18.1 10.6 %collective-permute-start = (bf16[16,640]{1,0:T(8,128)(2,1)S(1)}, bf16[16,640]{1,0:T(8,128)(2,1)S(1)}, u32[]{:S(2)}, u32[]{:S(2)}) collective-permute-start(bf16[16,640]{1,0:T(8,128)(2,1)S(1)} %get-tuple-element.49), channel_id=1, source_target_pairs={{0,8},{8,16},{16,24},{24,0},{1,9},{9,17},{17,25},{25,1},{2,10},{10... | collective-permute-start | bytes 61448 | tf_op jit(solution)/shard_map/ppermute | solution.py:245
  21.2 7.5 %collective-permute-start.1 = (bf16[16,640]{1,0:T(8,128)(2,1)S(1)}, bf16[16,640]{1,0:T(8,128)(2,1)S(1)}, u32[]{:S(2)}, u32[]{:S(2)}) collective-permute-start(bf16[16,640]{1,0:T(8,128)(2,1)S(1)} %get-tuple-element.48), channel_id=1, source_target_pairs={{0,16},{8,24},{16,0},{24,8},{1,17},{9,25},{17,1},{25,9},{2,18},{10... | collective-permute-start | bytes 61448 | tf_op jit(solution)/shard_map/ppermute | solution.py:245
  25.6 4.8 %collective-permute-start.2 = (bf16[16,640]{1,0:T(8,128)(2,1)S(1)}, bf16[16,640]{1,0:T(8,128)(2,1)S(1)}, u32[]{:S(2)}, u32[]{:S(2)}) collective-permute-start(bf16[16,640]{1,0:T(8,128)(2,1)S(1)} %get-tuple-element.47), channel_id=1, source_target_pairs={{0,24},{8,0},{16,8},{24,16},{1,25},{9,1},{17,9},{25,17},{2,26},{10... | collective-permute-start | bytes 61448 | tf_op jit(solution)/shard_map/ppermute | solution.py:245
  30.4 5.2 %collective-permute-start.3 = (bf16[80,640]{1,0:T(8,128)(2,1)S(1)}, bf16[80,640]{1,0:T(8,128)(2,1)S(1)}, u32[]{:S(2)}, u32[]{:S(2)}) collective-permute-start(bf16[80,640]{1,0:T(8,128)(2,1)S(1)} %constant_dynamic-update-slice_fusion), channel_id=1, source_target_pairs={{0,1},{1,0},{2,3},{3,2},{4,5},{5,4},{6,7},{7,6},{8,9},{9,8},{10,11... | collective-permute-start | bytes 307208 | tf_op jit(solution)/shard_map/ppermute | solution.py:263
  35.6 12.4 %collective-permute-start.4 = (bf16[2,80,640]{2,1,0:T(8,128)(2,1)S(1)}, bf16[2,80,640]{2,1,0:T(8,128)(2,1)S(1)}, u32[]{:S(2)}, u32[]{:S(2)}) collective-permute-start(bf16[2,80,640]{2,1,0:T(8,128)(2,1)S(1)} %pad_maximum_fusion), channel_id=1, source_target_pairs={{0,32},{1,481},{32,64},{33,1},{64,96},{65,33},{96,128},{97,65},{12... | collective-permute-start | bytes 614408 | tf_op jit(solution)/shard_map/ppermute | solution.py:255
  49.1 30.8 %all-to-all-start.1 = ((bf16[4,768,128]{2,1,0:T(8,128)(2,1)}), bf16[4,768,128]{2,1,0:T(8,128)(2,1)S(1)}, u32[]{:S(2)}, u32[]{:S(2)}) async-start(bf16[4,768,128]{2,1,0:T(8,128)(2,1)} %broadcast_in_dim.10), calls=%async_computation.1 | async-start | bytes 1572864 | tf_op jit(solution)/shard_map/all_to_all | solution.py:294
  53.2 26.6 %collective-permute-start.5 = (bf16[16,96,128]{2,1,0:T(8,128)(2,1)S(1)}, bf16[16,96,128]{2,1,0:T(8,128)(2,1)S(1)}, u32[]{:S(2)}, u32[]{:S(2)}) collective-permute-start(bf16[16,96,128]{2,1,0:T(8,128)(2,1)S(1)} %slice.86.kv0_ref), channel_id=1, source_target_pairs={{0,32},{32,64},{64,0},{96,128},{128,160},{160,96},{192,224},{224,2... | collective-permute-start | bytes 1179656 | tf_op jit(solution)/shard_map/ppermute | solution.py:290
  56.6 23.3 %collective-permute-start.6 = (bf16[16,96,128]{2,1,0:T(8,128)(2,1)S(1)}, bf16[16,96,128]{2,1,0:T(8,128)(2,1)S(1)}, u32[]{:S(2)}, u32[]{:S(2)}) collective-permute-start(bf16[16,96,128]{2,1,0:T(8,128)(2,1)S(1)} %slice.86.kv0_ref), channel_id=1, source_target_pairs={{0,64},{32,0},{64,32},{96,160},{128,96},{160,128},{192,256},{224,1... | collective-permute-start | bytes 1179656 | tf_op jit(solution)/shard_map/ppermute | solution.py:290
  59.4 18.1 %collective-permute-start.7 = (bf16[2,80,640]{2,1,0:T(8,128)(2,1)S(1)}, bf16[2,80,640]{2,1,0:T(8,128)(2,1)S(1)}, u32[]{:S(2)}, u32[]{:S(2)}) collective-permute-start(bf16[2,80,640]{2,1,0:T(8,128)(2,1)S(1)} %collective-permute-done.4), channel_id=1, source_target_pairs={{0,32},{1,481},{32,64},{33,1},{64,96},{65,33},{96,128},{97,65},{12... | collective-permute-start | bytes 614408 | tf_op jit(solution)/shard_map/ppermute | solution.py:255
  61.3 18.0 %copy-start.1 = (pred[48]{0:T(512)(128)(4,1)S(1)}, pred[48]{0:T(512)(128)(4,1)}, u32[]{:S(2)}) copy-start(pred[48]{0:T(512)(128)(4,1)} %constant.24.clone.1) | copy-start | bytes 148
  77.5 14.1 %collective-permute-start.8 = (bf16[2,80,640]{2,1,0:T(8,128)(2,1)S(1)}, bf16[2,80,640]{2,1,0:T(8,128)(2,1)S(1)}, u32[]{:S(2)}, u32[]{:S(2)}) collective-permute-start(bf16[2,80,640]{2,1,0:T(8,128)(2,1)S(1)} %collective-permute-done.7), channel_id=1, source_target_pairs={{0,32},{1,481},{32,64},{33,1},{64,96},{65,33},{96,128},{97,65},{12... | collective-permute-start | bytes 614408 | tf_op jit(solution)/shard_map/ppermute | solution.py:255
  91.5 15.8 %all-to-all-start.2 = ((bf16[4,864,128]{2,1,0:T(8,128)(2,1)}), bf16[4,864,128]{2,1,0:T(8,128)(2,1)S(1)}, u32[]{:S(2)}, u32[]{:S(2)}) async-start(bf16[4,864,128]{2,1,0:T(8,128)(2,1)} %shard_map.56), calls=%async_computation.2 | async-start | bytes 1769472 | tf_op jit(solution)/shard_map/all_to_all | solution.py:319
  95.8 6.8 %collective-permute-start.9 = (bf16[2,80,640]{2,1,0:T(8,128)(2,1)S(1)}, bf16[2,80,640]{2,1,0:T(8,128)(2,1)S(1)}, u32[]{:S(2)}, u32[]{:S(2)}) collective-permute-start(bf16[2,80,640]{2,1,0:T(8,128)(2,1)S(1)} %collective-permute-done.8), channel_id=1, source_target_pairs={{0,32},{1,481},{32,64},{33,1},{64,96},{65,33},{96,128},{97,65},{12... | collective-permute-start | bytes 614408 | tf_op jit(solution)/shard_map/ppermute | solution.py:255
  102.6 6.8 %collective-permute-start.10 = (bf16[2,80,640]{2,1,0:T(8,128)(2,1)S(1)}, bf16[2,80,640]{2,1,0:T(8,128)(2,1)S(1)}, u32[]{:S(2)}, u32[]{:S(2)}) collective-permute-start(bf16[2,80,640]{2,1,0:T(8,128)(2,1)S(1)} %collective-permute-done.9), channel_id=1, source_target_pairs={{0,32},{1,481},{32,64},{33,1},{64,96},{65,33},{96,128},{97,65},{12... | collective-permute-start | bytes 614408 | tf_op jit(solution)/shard_map/ppermute | solution.py:255
  109.4 31.1 %all-to-all-start.3 = ((bf16[16,48,128]{2,1,0:T(8,128)(2,1)}), bf16[16,48,128]{2,1,0:T(8,128)(2,1)S(1)}, u32[]{:S(2)}, u32[]{:S(2)}) async-start(bf16[16,48,128]{2,1,0:T(8,128)(2,1)} %shard_map.57), calls=%async_computation.3 | async-start | bytes 393216 | tf_op jit(solution)/shard_map/all_to_all | solution.py:323
  124.0 12.0 %collective-permute-start.11 = (bf16[2,80,640]{2,1,0:T(8,128)(2,1)S(1)}, bf16[2,80,640]{2,1,0:T(8,128)(2,1)S(1)}, u32[]{:S(2)}, u32[]{:S(2)}) collective-permute-start(bf16[2,80,640]{2,1,0:T(8,128)(2,1)S(1)} %collective-permute-done.10), channel_id=1, source_target_pairs={{0,32},{1,481},{32,64},{33,1},{64,96},{65,33},{96,128},{97,65},{12... | collective-permute-start | bytes 614408 | tf_op jit(solution)/shard_map/ppermute | solution.py:255
  136.0 7.1 %collective-permute-start.12 = (bf16[2,80,640]{2,1,0:T(8,128)(2,1)S(1)}, bf16[2,80,640]{2,1,0:T(8,128)(2,1)S(1)}, u32[]{:S(2)}, u32[]{:S(2)}) collective-permute-start(bf16[2,80,640]{2,1,0:T(8,128)(2,1)S(1)} %collective-permute-done.11), channel_id=1, source_target_pairs={{0,32},{1,481},{32,64},{33,1},{64,96},{65,33},{96,128},{97,65},{12... | collective-permute-start | bytes 614408 | tf_op jit(solution)/shard_map/ppermute | solution.py:255
  143.8 21.3 %collective-permute-start.13 = (bf16[7,80,640]{2,1,0:T(8,128)(2,1)}, bf16[7,80,640]{2,1,0:T(8,128)(2,1)S(1)}, u32[]{:S(2)}, u32[]{:S(2)}) collective-permute-start(bf16[7,80,640]{2,1,0:T(8,128)(2,1)} %get-tuple-element.34), channel_id=1, source_target_pairs={{0,1},{1,0},{2,3},{3,2},{4,5},{5,4},{6,7},{7,6},{8,9},{9,8},{10,11... | collective-permute-start | bytes 2150408 | tf_op jit(solution)/shard_map/ppermute | solution.py:263
  149.3 15.8 %all-to-all-start.4 = ((bf16[4,720,128]{2,1,0:T(8,128)(2,1)}), bf16[4,720,128]{2,1,0:T(8,128)(2,1)S(1)}, u32[]{:S(2)}, u32[]{:S(2)}) async-start(bf16[4,720,128]{2,1,0:T(8,128)(2,1)} %shard_map.58), calls=%async_computation.4 | async-start | bytes 1474560 | tf_op jit(solution)/shard_map/all_to_all | solution.py:327
  153.5 11.6 %collective-permute-start.14 = (bf16[2,80,640]{2,1,0:T(8,128)(2,1)S(1)}, bf16[2,80,640]{2,1,0:T(8,128)(2,1)S(1)}, u32[]{:S(2)}, u32[]{:S(2)}) collective-permute-start(bf16[2,80,640]{2,1,0:T(8,128)(2,1)S(1)} %collective-permute-done.12), channel_id=1, source_target_pairs={{0,32},{1,481},{32,64},{33,1},{64,96},{65,33},{96,128},{97,65},{12... | collective-permute-start | bytes 614408 | tf_op jit(solution)/shard_map/ppermute | solution.py:255
  165.2 4.8 %collective-permute-start.15 = (bf16[4,720,128]{2,1,0:T(8,128)(2,1)S(1)}, bf16[4,720,128]{2,1,0:T(8,128)(2,1)S(1)}, u32[]{:S(2)}, u32[]{:S(2)}) collective-permute-start(bf16[4,720,128]{2,1,0:T(8,128)(2,1)S(1)} %all-to-all-done.4.mine_ref), channel_id=1, source_target_pairs={{0,1},{1,0},{2,3},{3,2},{4,5},{5,4},{6,7},{7,6},{8,9},{9,8},{10,11... | collective-permute-start | bytes 2211848 | tf_op jit(solution)/shard_map/ppermute | solution.py:263

commit v7 on v4

--- a/solution.py
+++ b/solution.py
@@ -27,14 +27,14 @@
 GRANULE = 16
 
 
-def vmem_call(body, mebibytes, shapes, *operands, scalars=None):
+def vmem_call(body, mebibytes, shapes, *operands, scalars=None, kind=BF16):
     specs = [pl.BlockSpec(memory_space=pltpu.VMEM)] * len(operands)
     if scalars is not None:
         specs = [pl.BlockSpec(memory_space=pltpu.SMEM)] + specs
         operands = (scalars,) + operands
     return pl.pallas_call(
         body,
-        out_shape=[jax.ShapeDtypeStruct(shape, BF16) for shape in shapes],
+        out_shape=[jax.ShapeDtypeStruct(shape, kind) for shape in shapes],
         in_specs=specs,
         out_specs=[pl.BlockSpec(memory_space=pltpu.VMEM)] * len(shapes),
         compiler_params=pltpu.CompilerParams(vmem_limit_bytes=mebibytes * 1024 * 1024),
@@ -72,17 +72,10 @@
     out_ref[PARTS * HEADS_HERE] = jnp.zeros((3 * SLOT, HEAD), BF16)
 
 
-def attend(third_ref, q_ref, kv0_ref, kv1_ref, kv2_ref, kcode_ref, out_ref):
-    rows = Z * SLOT
-    third = third_ref[0]
-    order = [third, lax.rem(third + 2, PARTS), lax.rem(third + 1, PARTS)]
-    key_codes = [kcode_ref[pl.ds(j, 1), :] for j in order]
-    keys = [ref[:, :SLOT, :].reshape(rows, HEAD) for ref in (kv0_ref, kv1_ref, kv2_ref)]
-    ones = jnp.ones((rows, HEAD), BF16)
-    vals = [
-        jnp.concatenate([ref[:, SLOT:, :].reshape(rows, HEAD), ones], axis=1)
-        for ref in (kv0_ref, kv1_ref, kv2_ref)
-    ]
+GROUP = 4
+
+
+def query_codes(third, q_ref):
     tile = 16
     at = ID_ROW % tile
     ids = jnp.concatenate(
@@ -97,53 +90,107 @@
     home = (X * (which % Z) + which // Z) * TOK + third * STARTS[1]
     first = ids * POSITIONS
     last = first + (home + lax.broadcasted_iota(jnp.int32, (X * Z, HEAD), 1)).astype(F32)
-    codes = jnp.concatenate([first, last], axis=0).T
+    return jnp.concatenate([first, last], axis=0).T
+
+
+def columns(table, first):
+    return jnp.concatenate([table[:SLOT, first + n : first + n + 1] for n in range(GROUP)], axis=0)
+
+
+def masked_scores(query, keys, key_code, low_code, high_code):
+    score = lax.dot_general(query, keys, (((1,), (1,)), ((), ())), preferred_element_type=F32)
+    allowed = (key_code <= high_code) & (key_code >= low_code)
+    return jnp.where(allowed, score * (HEAD ** (-0.5) * LOG2E), BLOCKED)
+
+
+def keys_values(kv_ref):
+    rows = Z * SLOT
+    values = kv_ref[:, SLOT:, :].reshape(rows, HEAD)
+    return kv_ref[:, :SLOT, :].reshape(rows, HEAD), jnp.concatenate([values, jnp.ones((rows, HEAD), BF16)], axis=1)
+
+
+def attend_first(third_ref, q_ref, kv0_ref, kv1_ref, kcode_ref, sum_ref, stat_ref):
+    third = third_ref[0]
+    key_codes = [kcode_ref[pl.ds(j, 1), :] for j in (third, lax.rem(third + 2, PARTS))]
+    pairs = [keys_values(ref) for ref in (kv0_ref, kv1_ref)]
+    codes = query_codes(third, q_ref)
     lane = lax.broadcasted_iota(jnp.int32, (SLOT, HEAD), 1)
     stats = [jnp.zeros((SLOT, HEAD), F32) for _ in range(2)]
-    group = 4
-    share = lax.broadcasted_iota(jnp.int32, (group * SLOT, HEAD), 1) // SHARE
-    for g in range(Z // group):
-        count = -(-(g + 1) * group * SLOT // HEAD) * HEAD
-        zs = range(g * group, (g + 1) * group)
-        slots = [jnp.zeros((group * SLOT, HEAD), F32) for _ in range(X)]
+    for g in range(Z // GROUP):
+        span = slice(g * GROUP * SLOT, (g + 1) * GROUP * SLOT)
+        count = -(-(g + 1) * GROUP * SLOT // HEAD) * HEAD
         for x in range(X):
-            low_code = jnp.concatenate([codes[:SLOT, x * Z + z : x * Z + z + 1] for z in zs], axis=0)
-            high_code = jnp.concatenate(
-                [codes[:SLOT, (X + x) * Z + z : (X + x) * Z + z + 1] for z in zs], axis=0
+            low_code = columns(codes, x * Z + g * GROUP)
+            high_code = columns(codes, (X + x) * Z + g * GROUP)
+            scores = [
+                masked_scores(q_ref[x, span, :], keys[:count], code[:, :count], low_code, high_code)
+                for (keys, _), code in zip(pairs, key_codes)
+            ]
+            peak = functools.reduce(jnp.maximum, [jnp.max(s, axis=1, keepdims=True) for s in scores])
+            output = functools.reduce(
+                jnp.add,
+                [
+                    jnp.dot(jnp.exp2(s - peak).astype(BF16), values[:count], preferred_element_type=F32)
+                    for s, (_, values) in zip(scores, pairs)
+                ],
             )
-            query = q_ref[x, g * group * SLOT : (g + 1) * group * SLOT, :]
-            scores = []
-            for j in range(PARTS):
-                score = lax.dot_general(
-                    query, keys[j][:count], (((1,), (1,)), ((), ())), preferred_element_type=F32
-                ) * (HEAD ** (-0.5) * LOG2E)
-                key_code = key_codes[j][:, :count]
-                allowed = (key_code <= high_code) & (key_code >= low_code)
-                scores.append(jnp.where(allowed, score, BLOCKED))
-            peak = functools.reduce(jnp.maximum, [jnp.max(s, axis=1, keepdims=True) for s in scores])
-            output = jnp.zeros((group * SLOT, 2 * HEAD), F32)
-            for j in range(PARTS):
-                expo = jnp.exp2(scores[j] - peak)
-                output = output + jnp.dot(
-                    expo.astype(BF16), vals[j][:count], preferred_element_type=F32
-                )
-            normal = output[:, :HEAD] / output[:, HEAD:]
+            sum_ref[x, span, :] = output[:, :HEAD]
+            for n in range(GROUP):
+                for at, column in enumerate((peak, output[:, HEAD : HEAD + 1])):
+                    stats[at] = jnp.where(
+                        lane == x * Z + g * GROUP + n, column[n * SLOT : (n + 1) * SLOT], stats[at]
+                    )
+    for at in range(2):
+        stat_ref[at] = stats[at]
+
+
+def attend_last(third_ref, q_ref, kv_ref, kcode_ref, sum_ref, stat_ref, out_ref):
+    rows = Z * SLOT
+    third = third_ref[0]
+    key_code = kcode_ref[pl.ds(lax.rem(third + 1, PARTS), 1), :]
+    keys, values = keys_values(kv_ref)
+    codes = query_codes(third, q_ref)
+    peaks, totals = stat_ref[0], stat_ref[1]
+    lane = lax.broadcasted_iota(jnp.int32, (SLOT, HEAD), 1)
+    stats = [jnp.zeros((SLOT, HEAD), F32) for _ in range(2)]
+    share = lax.broadcasted_iota(jnp.int32, (GROUP * SLOT, HEAD), 1) // SHARE
+    for g in range(Z // GROUP):
+        span = slice(g * GROUP * SLOT, (g + 1) * GROUP * SLOT)
+        count = -(-(g + 1) * GROUP * SLOT // HEAD) * HEAD
+        slots = [jnp.zeros((GROUP * SLOT, HEAD), F32) for _ in range(X)]
+        for x in range(X):
+            first = x * Z + g * GROUP
+            score = masked_scores(
+                q_ref[x, span, :],
+                keys[:count],
+                key_code[:, :count],
+                columns(codes, first),
+                columns(codes, X * Z + first),
+            )
+            before = columns(peaks, first)
+            peak = jnp.maximum(before, jnp.max(score, axis=1, keepdims=True))
+            kept = jnp.exp2(before - peak)
+            output = jnp.dot(
+                jnp.exp2(score - peak).astype(BF16), values[:count], preferred_element_type=F32
+            )
+            total = output[:, HEAD : HEAD + 1] + kept * columns(totals, first)
+            normal = (output[:, :HEAD] + kept * sum_ref[x, span, :]) / total
             for to in range(X):
                 piece = normal if to == x else pltpu.roll(normal, (SHARE * (x - to)) % HEAD, 1)
                 slots[to] = jnp.where(share == x, piece, slots[to])
-            logsum = peak + jnp.log2(output[:, HEAD : HEAD + 1])
+            logsum = peak + jnp.log2(total)
             high = logsum.astype(BF16).astype(F32)
             rest = logsum - high
             middle = rest.astype(BF16).astype(F32)
             low = rest - middle
-            for n in range(group):
+            for n in range(GROUP):
                 for part, column in enumerate((high, middle, low)):
-                    at = part * X * Z + x * Z + g * group + n
+                    at = part * X * Z + first + n
                     stats[at // HEAD] = jnp.where(
                         lane == at % HEAD, column[n * SLOT : (n + 1) * SLOT], stats[at // HEAD]
                     )
         for x in range(X):
-            out_ref[x, g * group * SLOT : (g + 1) * group * SLOT, :] = slots[x].astype(BF16)
+            out_ref[x, span, :] = slots[x].astype(BF16)
     for x in range(X):
         out_ref[x, rows : rows + SLOT, :] = stats[0].astype(BF16)
         out_ref[x, rows + SLOT :, :] = stats[1].astype(BF16)
@@ -264,16 +311,28 @@
             for start, length in zip(STARTS, LENGTHS)
         ]
     )
-    (part,) = vmem_call(
-        attend,
-        32,
-        [(X, (Z + 2) * SLOT, HEAD)],
+    third = third.reshape(1)
+    sums, stats = vmem_call(
+        attend_first,
+        18,
+        [(X, Z * SLOT, HEAD), (2, SLOT, HEAD)],
         query,
         kv,
         kv_others[0],
+        key_code,
+        scalars=third,
+        kind=F32,
+    )
+    (part,) = vmem_call(
+        attend_last,
+        18,
+        [(X, (Z + 2) * SLOT, HEAD)],
+        query,
         kv_others[1],
         key_code,
-        scalars=third.reshape(1),
+        sums,
+        stats,
+        scalars=third,
     )
     part = lax.all_to_all(part, "x", 0, 0, tiled=True)
     (joined,) = vmem_call(join, 8, [(Z, SLOT, HEAD)], part)

time: 179 us -> 190 us (1.061)
  Pallas kernels: 16.4 us -> 25.6 us
  blocking collectives: 70.9 us -> 74.5 us
  waiting for transfers between devices: 25.3 us -> 22.8 us
    pallas_call x5 -> x6, Pallas kernels: 16.4 us -> 25.6 us  [vmem_call(): pl.pallas_call(body, out_shape=[jax.ShapeDtypeStruct(shape, kind) for sha...]
    all_to_all x1, blocking collectives: 33 us -> 36.7 us  [local(): joined = lax.all_to_all(joined, 'z', 0, 0, tiled=True)]
    ppermute x2, waiting for transfers between devices: 11.8 us -> 9.3 us  [local(): kv_others = [lax.ppermute(kv, 'z', turn) for turn in turns]]
  transfers between devices with their start and end apart: 9 -> 9, of which waited for: 4 -> 4; matrix products, arithmetic and copies ran while one was open for 2% -> 2% of each run, Pallas kernels for 6% -> 11%
where the time goes in v7:
time: 190 us; the launch traced here: 189 us
  blocking collectives  74.5 us (39%)
  starting transfers between devices  45.9 us (24%)
  Pallas kernels  25.6 us (13%)
  waiting for transfers between devices  22.8 us (12%)
  between operations  13.6 us (7%)
  local copies, waits for them, and re-layouts  5.76 us (3%)
    all_to_all x1, blocking collectives, local(): joined = lax.all_to_all(joined, 'z', 0, 0, tiled=True)  36.7 us
    pallas_call x6, Pallas kernels, vmem_call(): pl.pallas_call(body, out_shape=[jax.ShapeDtypeStruct(shape, kind) for sha...  25.6 us
    all_to_all x1, starting transfers between devices, local(): here = lax.all_to_all(send, 'z', 0, 0, tiled=True)  15.7 us
    all_to_all x1, blocking collectives, local(): partial = lax.all_to_all(partial, 'x', 0, 0, tiled=True)  13 us
    all_to_all x1, blocking collectives, local(): part = lax.all_to_all(part, 'x', 0, 0, tiled=True)  12.7 us
    all_to_all x1, blocking collectives, local(): packed = lax.all_to_all(packed, 'y', 0, 0, tiled=True)  12.1 us
    all_to_all x1, waiting for transfers between devices, local(): here = lax.all_to_all(send, 'z', 0, 0, tiled=True)  10.8 us
    ppermute x3, starting transfers between devices, share_rows(): lax.ppermute(granules[n], 'x', [(x, (x + n) % X) for x in range(X)])  10.5 us
  transfers between devices with their start and end apart: 9, of which 4 were waited for; matrix products, arithmetic and copies ran while one was open for 2% of the time, Pallas kernels for 11%

profile of v7, /device:TPU:1, one launch (start us, length us, event | category | flops | bytes accessed | tf_op | source)
XLA Modules:
  0.0 189.1 jit_solution(5914875793005855940)
XLA Ops:
  6.5 2.2 %shard_map.55 = (bf16[16,144,128]{2,1,0:T(8,128)(2,1)}, bf16[5,16,640]{2,1,0:T(8,128)(2,1)}) custom-call(bf16[128,640]{1,0:T(8,128)(2,1)} %q_ref.1, bf16[128,640]{1,0:T(8,128)(2,1)} %k_ref.1, bf16[128,640]{1,0:T(8,128)(2,1)} %v_ref.1, s32[1,128]{1,0:T(1,128)} %bitcast.18, bf16[80,640]{1,0:T(8,128)(2,1)} %weight_ref.1), custom_call_target="tpu_custom_call" | custom-call | tf_op jit(solution)/shard_map/pallas_call | solution.py:35
  8.7 15.7 %all-to-all-start = ((bf16[16,144,128]{2,1,0:T(8,128)(2,1)}), bf16[16,144,128]{2,1,0:T(8,128)(2,1)S(1)}, u32[]{:S(2)}, u32[]{:S(2)}) async-start(bf16[16,144,128]{2,1,0:T(8,128)(2,1)} %get-tuple-element.9), calls=%async_computation | async-start | bytes 1179648 | tf_op jit(solution)/shard_map/all_to_all | solution.py:291
  24.5 0.8 slice_bitcast_fusion
  25.3 3.1 %collective-permute-start.3 = (bf16[16,640]{1,0:T(8,128)(2,1)S(1)}, bf16[16,640]{1,0:T(8,128)(2,1)S(1)}, u32[]{:S(2)}, u32[]{:S(2)}) collective-permute-start(bf16[16,640]{1,0:T(8,128)(2,1)S(1)} %get-tuple-element.15), channel_id=1, source_target_pairs={{0,8},{8,16},{16,24},{24,0},{1,9},{9,17},{17,25},{25,1},{2,10},{10... | collective-permute-start | bytes 61448 | tf_op jit(solution)/shard_map/ppermute | solution.py:272
  28.4 4.4 %collective-permute-start.4 = (bf16[16,640]{1,0:T(8,128)(2,1)S(1)}, bf16[16,640]{1,0:T(8,128)(2,1)S(1)}, u32[]{:S(2)}, u32[]{:S(2)}) collective-permute-start(bf16[16,640]{1,0:T(8,128)(2,1)S(1)} %get-tuple-element.14), channel_id=1, source_target_pairs={{0,16},{8,24},{16,0},{24,8},{1,17},{9,25},{17,1},{25,9},{2,18},{10... | collective-permute-start | bytes 61448 | tf_op jit(solution)/shard_map/ppermute | solution.py:272
  32.8 3.1 %collective-permute-start.5 = (bf16[16,640]{1,0:T(8,128)(2,1)S(1)}, bf16[16,640]{1,0:T(8,128)(2,1)S(1)}, u32[]{:S(2)}, u32[]{:S(2)}) collective-permute-start(bf16[16,640]{1,0:T(8,128)(2,1)S(1)} %get-tuple-element.13), channel_id=1, source_target_pairs={{0,24},{8,0},{16,8},{24,16},{1,25},{9,1},{17,9},{25,17},{2,26},{10... | collective-permute-start | bytes 61448 | tf_op jit(solution)/shard_map/ppermute | solution.py:272
  35.8 0.7 bitcast_dynamic-update-slice_fusion.1
  36.6 1.0 collective-permute-done.5
  37.6 0.7 bitcast_dynamic-update-slice_fusion
  38.3 0.6 copy-done.1
  39.0 10.8 %all-to-all-done = bf16[16,144,128]{2,1,0:T(8,128)(2,1)S(1)} async-done(((bf16[16,144,128]{2,1,0:T(8,128)(2,1)}), bf16[16,144,128]{2,1,0:T(8,128)(2,1)S(1)}, u32[]{:S(2)}, u32[]{:S(2)}) %all-to-all-start) | async-done | bytes 589856 | tf_op jit(solution)/shard_map/all_to_all | solution.py:291
  49.8 4.7 %collective-permute-start = (bf16[16,96,128]{2,1,0:T(8,128)(2,1)S(1)}, bf16[16,96,128]{2,1,0:T(8,128)(2,1)S(1)}, u32[]{:S(2)}, u32[]{:S(2)}) collective-permute-start(bf16[16,96,128]{2,1,0:T(8,128)(2,1)S(1)} %slice.47.kv0_ref), channel_id=1, source_target_pairs={{0,64},{32,0},{64,32},{96,160},{128,96},{160,128},{192,256},{224,1... | collective-permute-start | bytes 1179656 | tf_op jit(solution)/shard_map/ppermute | solution.py:298
  54.5 1.9 %collective-permute-start.1 = (bf16[16,96,128]{2,1,0:T(8,128)(2,1)S(1)}, bf16[16,96,128]{2,1,0:T(8,128)(2,1)S(1)}, u32[]{:S(2)}, u32[]{:S(2)}) collective-permute-start(bf16[16,96,128]{2,1,0:T(8,128)(2,1)S(1)} %slice.47.kv0_ref), channel_id=1, source_target_pairs={{0,32},{32,64},{64,0},{96,128},{128,160},{160,96},{192,224},{224,2... | collective-permute-start | bytes 1179656 | tf_op jit(solution)/shard_map/ppermute | solution.py:298
  56.5 1.0 broadcast_in_dim.10
  57.5 4.0 %all-to-all-start.1 = ((bf16[4,768,128]{2,1,0:T(8,128)(2,1)}), bf16[4,768,128]{2,1,0:T(8,128)(2,1)S(1)}, u32[]{:S(2)}, u32[]{:S(2)}) async-start(bf16[4,768,128]{2,1,0:T(8,128)(2,1)} %broadcast_in_dim.10), calls=%async_computation.1 | async-start | bytes 1572864 | tf_op jit(solution)/shard_map/all_to_all | solution.py:300
  61.7 0.1 stack_reshape.11
  61.8 0.1 stack_reshape.10
  61.9 0.1 stack_reshape.9
  62.0 9.3 %collective-permute-done.1.kv1_ref = bf16[16,96,128]{2,1,0:T(8,128)(2,1)S(1)} collective-permute-done((bf16[16,96,128]{2,1,0:T(8,128)(2,1)S(1)}, bf16[16,96,128]{2,1,0:T(8,128)(2,1)S(1)}, u32[]{:S(2)}, u32[]{:S(2)}) %collective-permute-start.1) | collective-permute-done | bytes 393248 | tf_op jit(solution)/shard_map/ppermute | solution.py:298
  71.3 7.7 %shard_map.56 = (f32[4,768,128]{2,1,0:T(8,128)S(1)}, f32[2,48,128]{2,1,0:T(8,128)S(1)}) custom-call(s32[1]{0:T(128)} %bitcast.2.third_ref, bf16[4,768,128]{2,1,0:T(8,128)(2,1)S(1)} %all-to-all-done.1.q_ref, bf16[16,96,128]{2,1,0:T(8,128)(2,1)S(1)} %slice.47.kv0_ref, bf16[16,96,128]{2,1,0:T(8,128)(2,1)S(1)} %collective-permute-done.1.kv1_ref, ...), custom_call_target="tpu_custom_call" | custom-call | tf_op jit(solution)/shard_map/pallas_call | solution.py:35
  79.0 12.2 %shard_map.57 = bf16[4,864,128]{2,1,0:T(8,128)(2,1)S(1)} custom-call(s32[1]{0:T(128)} %bitcast.2.third_ref, bf16[4,768,128]{2,1,0:T(8,128)(2,1)S(1)} %all-to-all-done.1.q_ref, bf16[16,96,128]{2,1,0:T(8,128)(2,1)S(1)} %collective-permute-done.kv_ref, f32[3,768]{1,0:T(4,128)S(1)} %pad_maximum_fusion.kcode_ref, f32[4,768,128]{2,1,0:T(8,128)S(1)} %get-tuple-element.10.sum_ref, ...), custom_call_target="tpu_custom_call" | custom-call | tf_op jit(solution)/shard_map/pallas_call | solution.py:35
  91.3 12.7 %all_to_all.30.part_ref = bf16[4,864,128]{2,1,0:T(8,128)(2,1)S(1)} all-to-all(bf16[4,864,128]{2,1,0:T(8,128)(2,1)S(1)} %shard_map.57), channel_id=1, replica_groups=mesh['z'=16,'x'=4,'y'=4,'c'=2] {'x'}, dimensions={0} | all-to-all | bytes 1769472 | tf_op jit(solution)/shard_map/all_to_all | solution.py:337
  104.0 0.6 shard_map.58
  104.7 36.7 %all_to_all.31.part_ref = bf16[16,48,128]{2,1,0:T(8,128)(2,1)S(1)} all-to-all(bf16[16,48,128]{2,1,0:T(8,128)(2,1)S(1)} %shard_map.58), channel_id=1, replica_groups=mesh['z'=16,'x'=4,'y'=4,'c'=2] {'z'}, dimensions={0} | all-to-all | bytes 393216 | tf_op jit(solution)/shard_map/all_to_all | solution.py:339
  141.3 0.2 shard_map.59
  141.5 12.1 %all_to_all.32.mine_ref = bf16[4,720,128]{2,1,0:T(8,128)(2,1)S(1)} all-to-all(bf16[4,720,128]{2,1,0:T(8,128)(2,1)S(1)} %shard_map.59), channel_id=1, replica_groups=mesh['z'=16,'x'=4,'y'=4,'c'=2] {'y'}, dimensions={0} | all-to-all | bytes 1474560 | tf_op jit(solution)/shard_map/all_to_all | solution.py:341
  153.6 8.9 %collective-permute-start.2 = (bf16[4,720,128]{2,1,0:T(8,128)(2,1)S(1)}, bf16[4,720,128]{2,1,0:T(8,128)(2,1)S(1)}, u32[]{:S(2)}, u32[]{:S(2)}) collective-permute-start(bf16[4,720,128]{2,1,0:T(8,128)(2,1)S(1)} %all_to_all.32.mine_ref), channel_id=1, source_target_pairs={{0,1},{1,0},{2,3},{3,2},{4,5},{5,4},{6,7},{7,6},{8,9},{9,8},{10,11... | collective-permute-start | bytes 2211848 | tf_op jit(solution)/shard_map/ppermute | solution.py:342
  162.6 1.7 collective-permute-done.2.other_ref
  164.3 1.4 copy-done
  165.8 2.6 %shard_map.60 = bf16[4,128,640]{2,1,0:T(8,128)(2,1)S(1)} custom-call(s32[2]{0:T(128)S(1)} %pad_add_fusion.place_ref, bf16[4,720,128]{2,1,0:T(8,128)(2,1)S(1)} %all_to_all.32.mine_ref, bf16[4,720,128]{2,1,0:T(8,128)(2,1)S(1)} %collective-permute-done.2.other_ref, bf16[1280,640]{1,0:T(8,128)(2,1)S(1)} %copy-done), custom_call_target="tpu_custom_call" | custom-call | tf_op jit(solution)/shard_map/pallas_call | solution.py:35
  168.4 13.0 %all_to_all.33 = bf16[4,128,640]{2,1,0:T(8,128)(2,1)S(1)} all-to-all(bf16[4,128,640]{2,1,0:T(8,128)(2,1)S(1)} %shard_map.60), channel_id=1, replica_groups=mesh['z'=16,'x'=4,'y'=4,'c'=2] {'x'}, dimensions={0} | all-to-all | bytes 1310720 | tf_op jit(solution)/shard_map/all_to_all | solution.py:346
  181.5 0.8 reduce_sum.12
  (26 shorter events, 0.5 us)
Async XLA Ops:
  8.7 41.1 %all-to-all-start = ((bf16[16,144,128]{2,1,0:T(8,128)(2,1)}), bf16[16,144,128]{2,1,0:T(8,128)(2,1)S(1)}, u32[]{:S(2)}, u32[]{:S(2)}) async-start(bf16[16,144,128]{2,1,0:T(8,128)(2,1)} %get-tuple-element.9), calls=%async_computation | async-start | bytes 1179648 | tf_op jit(solution)/shard_map/all_to_all | solution.py:291
  24.5 138.1 %all-gather.2.cloned.1.call-start = ((), (), s32[]{:S(2)}) async-start(), calls=%async_computation.6 | async-start | bytes 1740800 | tf_op jit(solution)/shard_map/all_gather | solution.py:292
  25.3 11.3 %collective-permute-start.3 = (bf16[16,640]{1,0:T(8,128)(2,1)S(1)}, bf16[16,640]{1,0:T(8,128)(2,1)S(1)}, u32[]{:S(2)}, u32[]{:S(2)}) collective-permute-start(bf16[16,640]{1,0:T(8,128)(2,1)S(1)} %get-tuple-element.15), channel_id=1, source_target_pairs={{0,8},{8,16},{16,24},{24,0},{1,9},{9,17},{17,25},{25,1},{2,10},{10... | collective-permute-start | bytes 61448 | tf_op jit(solution)/shard_map/ppermute | solution.py:272
  28.4 8.2 %collective-permute-start.4 = (bf16[16,640]{1,0:T(8,128)(2,1)S(1)}, bf16[16,640]{1,0:T(8,128)(2,1)S(1)}, u32[]{:S(2)}, u32[]{:S(2)}) collective-permute-start(bf16[16,640]{1,0:T(8,128)(2,1)S(1)} %get-tuple-element.14), channel_id=1, source_target_pairs={{0,16},{8,24},{16,0},{24,8},{1,17},{9,25},{17,1},{25,9},{2,18},{10... | collective-permute-start | bytes 61448 | tf_op jit(solution)/shard_map/ppermute | solution.py:272
  32.8 4.8 %collective-permute-start.5 = (bf16[16,640]{1,0:T(8,128)(2,1)S(1)}, bf16[16,640]{1,0:T(8,128)(2,1)S(1)}, u32[]{:S(2)}, u32[]{:S(2)}) collective-permute-start(bf16[16,640]{1,0:T(8,128)(2,1)S(1)} %get-tuple-element.13), channel_id=1, source_target_pairs={{0,24},{8,0},{16,8},{24,16},{1,25},{9,1},{17,9},{25,17},{2,26},{10... | collective-permute-start | bytes 61448 | tf_op jit(solution)/shard_map/ppermute | solution.py:272
  38.3 0.6 copy-start.1
  49.8 12.1 %copy-start.2 = (pred[48]{0:T(512)(128)(4,1)S(1)}, pred[48]{0:T(512)(128)(4,1)}, u32[]{:S(2)}) copy-start(pred[48]{0:T(512)(128)(4,1)} %constant.24.clone.1) | copy-start | bytes 148
  49.8 29.2 %collective-permute-start = (bf16[16,96,128]{2,1,0:T(8,128)(2,1)S(1)}, bf16[16,96,128]{2,1,0:T(8,128)(2,1)S(1)}, u32[]{:S(2)}, u32[]{:S(2)}) collective-permute-start(bf16[16,96,128]{2,1,0:T(8,128)(2,1)S(1)} %slice.47.kv0_ref), channel_id=1, source_target_pairs={{0,64},{32,0},{64,32},{96,160},{128,96},{160,128},{192,256},{224,1... | collective-permute-start | bytes 1179656 | tf_op jit(solution)/shard_map/ppermute | solution.py:298
  54.5 16.8 %collective-permute-start.1 = (bf16[16,96,128]{2,1,0:T(8,128)(2,1)S(1)}, bf16[16,96,128]{2,1,0:T(8,128)(2,1)S(1)}, u32[]{:S(2)}, u32[]{:S(2)}) collective-permute-start(bf16[16,96,128]{2,1,0:T(8,128)(2,1)S(1)} %slice.47.kv0_ref), channel_id=1, source_target_pairs={{0,32},{32,64},{64,0},{96,128},{128,160},{160,96},{192,224},{224,2... | collective-permute-start | bytes 1179656 | tf_op jit(solution)/shard_map/ppermute | solution.py:298
  57.5 13.9 %all-to-all-start.1 = ((bf16[4,768,128]{2,1,0:T(8,128)(2,1)}), bf16[4,768,128]{2,1,0:T(8,128)(2,1)S(1)}, u32[]{:S(2)}, u32[]{:S(2)}) async-start(bf16[4,768,128]{2,1,0:T(8,128)(2,1)} %broadcast_in_dim.10), calls=%async_computation.1 | async-start | bytes 1572864 | tf_op jit(solution)/shard_map/all_to_all | solution.py:300
  153.6 10.8 %collective-permute-start.2 = (bf16[4,720,128]{2,1,0:T(8,128)(2,1)S(1)}, bf16[4,720,128]{2,1,0:T(8,128)(2,1)S(1)}, u32[]{:S(2)}, u32[]{:S(2)}) collective-permute-start(bf16[4,720,128]{2,1,0:T(8,128)(2,1)S(1)} %all_to_all.32.mine_ref), channel_id=1, source_target_pairs={{0,1},{1,0},{2,3},{3,2},{4,5},{5,4},{6,7},{7,6},{8,9},{9,8},{10,11... | collective-permute-start | bytes 2211848 | tf_op jit(solution)/shard_map/ppermute | solution.py:342
  164.3 1.4 copy-start
Sparse Core Ops, SparseCore 0:
  39.1 71.8 all-gather.1

commit v8 on v4

--- a/solution.py
+++ b/solution.py
@@ -23,20 +23,26 @@
 F32 = jnp.float32
 BF16 = jnp.bfloat16
 LOG2E = 1.4426950408889634
-SHARE = 32
+PAIR = 2
+SHARE = 64
 GRANULE = 16
 
 
-def vmem_call(body, mebibytes, shapes, *operands, scalars=None):
+def vmem_call(body, mebibytes, shapes, *operands, scalars=None, left=(), scratch=(), kinds=None, cost=None):
     specs = [pl.BlockSpec(memory_space=pltpu.VMEM)] * len(operands)
+    specs += [pl.BlockSpec(memory_space=pltpu.HBM)] * len(left)
+    operands += tuple(left)
+    kinds = kinds or [BF16] * len(shapes)
     if scalars is not None:
         specs = [pl.BlockSpec(memory_space=pltpu.SMEM)] + specs
         operands = (scalars,) + operands
     return pl.pallas_call(
         body,
-        out_shape=[jax.ShapeDtypeStruct(shape, BF16) for shape in shapes],
+        out_shape=[jax.ShapeDtypeStruct(shape, kind) for shape, kind in zip(shapes, kinds)],
         in_specs=specs,
         out_specs=[pl.BlockSpec(memory_space=pltpu.VMEM)] * len(shapes),
+        scratch_shapes=list(scratch),
+        cost_estimate=cost,
         compiler_params=pltpu.CompilerParams(vmem_limit_bytes=mebibytes * 1024 * 1024),
     )(*operands)
 
@@ -54,7 +60,7 @@
     every = jnp.broadcast_to(ids, (SLOT, HEAD))
     source = lax.broadcasted_iota(jnp.int32, (HEAD, HEAD), 0)
     to = lax.broadcasted_iota(jnp.int32, (HEAD, HEAD), 1)
-    origin = (to % SHARE) // GRANULE * (X * GRANULE) + to // SHARE * GRANULE + to % GRANULE
+    origin = (to % SHARE) // GRANULE * (PAIR * GRANULE) + to // SHARE * GRANULE + to % GRANULE
     turn = jnp.where(source == origin, 1.0, 0.0).astype(BF16)
     for h in range(HEADS_HERE):
         for part, ref in enumerate((q_ref, k_ref, v_ref)):
@@ -99,13 +105,13 @@
     last = first + (home + lax.broadcasted_iota(jnp.int32, (X * Z, HEAD), 1)).astype(F32)
     codes = jnp.concatenate([first, last], axis=0).T
     lane = lax.broadcasted_iota(jnp.int32, (SLOT, HEAD), 1)
-    stats = [jnp.zeros((SLOT, HEAD), F32) for _ in range(2)]
     group = 4
-    share = lax.broadcasted_iota(jnp.int32, (group * SLOT, HEAD), 1) // SHARE
+    halves = lax.broadcasted_iota(jnp.int32, (group * SLOT, HEAD), 1) < SHARE
+    stats = [jnp.zeros((SLOT, HEAD), F32) for _ in range(X // PAIR)]
     for g in range(Z // group):
         count = -(-(g + 1) * group * SLOT // HEAD) * HEAD
         zs = range(g * group, (g + 1) * group)
-        slots = [jnp.zeros((group * SLOT, HEAD), F32) for _ in range(X)]
+        normals = []
         for x in range(X):
             low_code = jnp.concatenate([codes[:SLOT, x * Z + z : x * Z + z + 1] for z in zs], axis=0)
             high_code = jnp.concatenate(
@@ -127,45 +133,42 @@
                 output = output + jnp.dot(
                     expo.astype(BF16), vals[j][:count], preferred_element_type=F32
                 )
-            normal = output[:, :HEAD] / output[:, HEAD:]
-            for to in range(X):
-                piece = normal if to == x else pltpu.roll(normal, (SHARE * (x - to)) % HEAD, 1)
-                slots[to] = jnp.where(share == x, piece, slots[to])
-            logsum = peak + jnp.log2(output[:, HEAD : HEAD + 1])
-            high = logsum.astype(BF16).astype(F32)
-            rest = logsum - high
-            middle = rest.astype(BF16).astype(F32)
-            low = rest - middle
+            normals.append(output[:, :HEAD] / output[:, HEAD:])
+            logsum = peak + jnp.log2(output[:, HEAD:])
             for n in range(group):
-                for part, column in enumerate((high, middle, low)):
-                    at = part * X * Z + x * Z + g * group + n
-                    stats[at // HEAD] = jnp.where(
-                        lane == at % HEAD, column[n * SLOT : (n + 1) * SLOT], stats[at // HEAD]
-                    )
-        for x in range(X):
-            out_ref[x, g * group * SLOT : (g + 1) * group * SLOT, :] = slots[x].astype(BF16)
-    for x in range(X):
-        out_ref[x, rows : rows + SLOT, :] = stats[0].astype(BF16)
-        out_ref[x, rows + SLOT :, :] = stats[1].astype(BF16)
+                at = x % PAIR * Z + g * group + n
+                stats[x // PAIR] = jnp.where(lane == at, logsum[n * SLOT : (n + 1) * SLOT], stats[x // PAIR])
+        for first in range(0, X, PAIR):
+            one, two = normals[first : first + PAIR]
+            span = slice(g * group * SLOT, (g + 1) * group * SLOT)
+            out_ref[first, span, :] = jnp.where(halves, one, pltpu.roll(two, SHARE, 1)).astype(BF16)
+            out_ref[first + 1, span, :] = jnp.where(halves, pltpu.roll(one, SHARE, 1), two).astype(BF16)
+    for pair, logsum in enumerate(stats):
+        high = logsum.astype(BF16).astype(F32)
+        rest = logsum - high
+        middle = rest.astype(BF16).astype(F32)
+        low = rest - middle
+        table = high + pltpu.roll(middle, PAIR * Z, 1) + pltpu.roll(low, 2 * PAIR * Z, 1)
+        for x in range(PAIR):
+            out_ref[PAIR * pair + x, rows:, :] = table.astype(BF16)
 
 
 def join(part_ref, out_ref):
     rows = Z * SLOT
     sums = []
     for x in range(X):
-        stat = part_ref[x, rows : rows + SLOT, :].astype(F32)
-        rest = part_ref[x, rows + SLOT :, :].astype(F32)
-        sums.append(stat + pltpu.roll(stat, HEAD // 2, 1) + rest)
+        stat = part_ref[x, rows:, :].astype(F32)
+        sums.append(stat + pltpu.roll(stat, HEAD - PAIR * Z, 1) + pltpu.roll(stat, HEAD - 2 * PAIR * Z, 1))
     peak = functools.reduce(jnp.maximum, sums)
     weights = [jnp.exp2(s - peak) for s in sums]
     total = functools.reduce(jnp.add, weights)
     weights = [w / total for w in weights]
-    share = lax.broadcasted_iota(jnp.int32, (SLOT, HEAD), 1) // SHARE
+    half = lax.broadcasted_iota(jnp.int32, (SLOT, HEAD), 1) // SHARE
     for z in range(Z):
         joined = functools.reduce(
             jnp.add,
             [
-                jnp.take_along_axis(weights[x], share * Z + z, axis=1)
+                jnp.take_along_axis(weights[x], half * Z + z, axis=1)
                 * part_ref[x, z * SLOT : (z + 1) * SLOT, :].astype(F32)
                 for x in range(X)
             ],
@@ -174,56 +177,80 @@
 
 
 def assemble(part_ref, out_ref):
-    share = lax.broadcasted_iota(jnp.int32, (SLOT, HEAD), 1) // SHARE
+    halves = lax.broadcasted_iota(jnp.int32, (SLOT, HEAD), 1) < SHARE
     for r in range(PARTS):
-        came = [part_ref[PARTS * h + r] for h in range(HEADS_HERE)]
-        wide = [c.astype(F32) for c in came[:4]]
-        for x in range(X):
-            block = jnp.zeros((SLOT, HEAD), F32)
-            for h in range(4):
-                piece = wide[h] if h == x else pltpu.roll(wide[h], (SHARE * (h - x)) % HEAD, 1)
-                block = jnp.where(share == h, piece, block)
-            first = (x * PARTS + r) * SLOT
-            for y in range(Y):
-                out_ref[y, first : first + SLOT, :] = block.astype(BF16)
-        first = (X * PARTS + r) * SLOT
+        for two in range(2):
+            one, other = [part_ref[PARTS * (2 * two + n) + r].astype(F32) for n in range(2)]
+            blocks = (
+                jnp.where(halves, one, pltpu.roll(other, SHARE, 1)),
+                jnp.where(halves, pltpu.roll(one, SHARE, 1), other),
+            )
+            for x, block in enumerate(blocks):
+                first = ((2 * x + two) * PARTS + r) * SLOT
+                for y in range(Y):
+                    out_ref[y, first : first + SLOT, :] = block.astype(BF16)
+        first = (2 * PAIR * PARTS + r) * SLOT
         for y in range(Y):
-            out_ref[y, first : first + SLOT, :] = came[4]
-
-
-def project(place_ref, mine_ref, other_ref, weight_ref, out_ref):
+            out_ref[y, first : first + SLOT, :] = part_ref[PARTS * (HEADS_HERE - 1) + r]
+
+
+def project(place_ref, mine_ref, other_ref, hbm_ref, own_ref, send_ref, weight_ref, sems):
     core, side = place_ref[0], place_ref[1]
-    places = [lax.rem(side + (X + 1) - m, X + 1) * GRANULE for m in range(X + 1)]
-    plane_rows = (X + 1) * GRANULE
-    pieces = SHARE // GRANULE
+    depth = weight_ref.shape[0] // Z
+    copies = [
+        pltpu.make_async_copy(
+            hbm_ref.at[pl.ds(z * depth, depth), :], weight_ref.at[pl.ds(z * depth, depth), :], sems.at[z]
+        )
+        for z in range(Z)
+    ]
+    for copy in copies:
+        copy.start()
+    member = lax.rem(side, PAIR)
+    places = []
+    for m in range(depth // GRANULE):
+        number = 2 * m + member
+        holder, n = lax.div(number, X + 1), lax.rem(number, X + 1)
+        away = lax.rem(holder + X - side, X)
+        base = jnp.where(away == 0, 0, jnp.where(away == 1, 8, jnp.where(away == 2, 3, 6)))
+        places.append((base + lax.div(n, 2)) * GRANULE)
     span = PARTS * SLOT
-    share = lax.broadcasted_iota(jnp.int32, (span, HEAD), 1) // SHARE
+    halves = lax.broadcasted_iota(jnp.int32, (span, HEAD), 1) < SHARE
+    per_head = SHARE // GRANULE
+    inputs = [[] for _ in range(PAIR)]
+    for y in range(Y):
+        for ref in (mine_ref, other_ref):
+            fifth = ref[y, 2 * PAIR * span :, :].astype(F32)
+            for x in range(PAIR):
+                inputs[x] += [ref[y, (2 * x + two) * span : (2 * x + two + 1) * span, :] for two in range(2)]
+                inputs[x].append(jnp.where(halves == (x == 0), fifth, 0.0).astype(BF16))
+    inputs = [jnp.concatenate(blocks, axis=1) for blocks in inputs]
+    for copy in copies:
+        copy.wait()
     weights = []
     for y in range(Y):
         for which in (core, 1 - core):
             rows = []
-            for n in range(HEADS_HERE * pieces):
-                first = (C * y + which) * pieces * plane_rows + n // (X + 1) * plane_rows + places[n % (X + 1)]
+            for n in range(HEADS_HERE * per_head):
+                first = ((C * y + which) * 2 + n // len(places)) * depth + places[n % len(places)]
                 rows.append(weight_ref[pl.ds(pl.multiple_of(first, GRANULE), GRANULE), :])
-            weights += rows[: 4 * pieces] + rows[4 * pieces :] * (HEAD // SHARE)
+            weights += rows + rows[4 * per_head :]
     weights = jnp.concatenate(weights, axis=0)
-    for x in range(X):
-        inputs = []
-        for y in range(Y):
-            for ref in (mine_ref, other_ref):
-                inputs.append(ref[y, x * span : (x + 1) * span, :])
-                fifth = ref[y, X * span :, :].astype(F32)
-                inputs.append(jnp.where(share == x, fifth, 0.0).astype(BF16))
-        total = jnp.dot(jnp.concatenate(inputs, axis=1), weights, preferred_element_type=F32)
+    totals = []
+    for x in range(PAIR):
+        total = jnp.dot(inputs[x], weights, preferred_element_type=F32)
         total = [total[r * SLOT : r * SLOT + length] for r, length in enumerate(LENGTHS)]
-        out_ref[x] = jnp.concatenate(total, axis=0).astype(BF16)
+        totals.append(jnp.concatenate(total, axis=0))
+    own_ref[...] = jnp.where(member == 0, totals[0], totals[1])
+    send_ref[...] = jnp.where(member == 0, totals[1], totals[0]).astype(BF16)
 
 
 def share_rows(granules):
-    came = [granules[0]]
-    for n in range(1, X):
-        came.append(lax.ppermute(granules[n], "x", [(x, (x + n) % X) for x in range(X)]))
-    return jnp.concatenate(came + [granules[X]], axis=0)
+    even = jnp.concatenate([granules[n] for n in range(0, X + 1, 2)], axis=0)
+    odd = jnp.concatenate([granules[n] for n in range(1, X + 1, 2)], axis=0)
+    blocks = [even]
+    for block, away in ((even, 2), (odd, 1), (odd, X - 1)):
+        blocks.append(lax.ppermute(block, "x", [(x, (x + away) % X) for x in range(X)]))
+    return jnp.concatenate(blocks, axis=0)
 
 
 def local(queries, keys_in, values, cluster_ids, out_weight):
@@ -266,26 +293,35 @@
     )
     (part,) = vmem_call(
         attend,
-        32,
-        [(X, (Z + 2) * SLOT, HEAD)],
+        20,
+        [(X, (Z + 1) * SLOT, HEAD)],
         query,
         kv,
         kv_others[0],
         kv_others[1],
         key_code,
         scalars=third.reshape(1),
+        cost=pl.CostEstimate(flops=1 << 36, bytes_accessed=1 << 22, transcendentals=1 << 22),
     )
     part = lax.all_to_all(part, "x", 0, 0, tiled=True)
     (joined,) = vmem_call(join, 8, [(Z, SLOT, HEAD)], part)
     joined = lax.all_to_all(joined, "z", 0, 0, tiled=True)
-    (packed,) = vmem_call(assemble, 8, [(Y, (X + 1) * PARTS * SLOT, HEAD)], joined)
+    (packed,) = vmem_call(assemble, 8, [(Y, (2 * PAIR + 1) * PARTS * SLOT, HEAD)], joined)
     packed = lax.all_to_all(packed, "y", 0, 0, tiled=True)
     others = lax.ppermute(packed, "c", [(0, 1), (1, 0)])
-    (partial,) = vmem_call(
-        project, 24, [(X, TOK, width)], packed, others, weight, scalars=jnp.stack([core, side])
-    )
-    partial = lax.all_to_all(partial, "x", 0, 0, tiled=True)
-    return jnp.sum(partial.astype(F32), axis=0).astype(BF16)
+    own, send = vmem_call(
+        project,
+        24,
+        [(TOK, width), (TOK, width)],
+        packed,
+        others,
+        scalars=jnp.stack([core, side]),
+        left=[weight],
+        scratch=[pltpu.VMEM(weight.shape, BF16), pltpu.SemaphoreType.DMA((Z,))],
+        kinds=[F32, BF16],
+    )
+    came = lax.ppermute(send, "x", [(x, x + 1 - 2 * (x % PAIR)) for x in range(X)])
+    return (own + came.astype(F32)).astype(BF16)
 
 
 def solution(mesh):

time: 179 us -> 180 us (level)
  blocking collectives: 70.9 us -> 54.9 us
  waiting for transfers between devices: 25.3 us -> 34.7 us
  Pallas kernels: 16.4 us -> 19.8 us
  starting transfers between devices: 45.5 us -> 47.6 us
    all_to_all x1 -> x0, blocking collectives: 13 us -> none  [local(): partial = lax.all_to_all(partial, 'x', 0, 0, tiled=True)]
    ppermute x2, waiting for transfers between devices: 11.8 us -> 17.1 us  [local(): kv_others = [lax.ppermute(kv, 'z', turn) for turn in turns]]
    ppermute x3 -> x4, waiting for transfers between devices: 0.97 us -> 5.37 us  [the longest x1 4.27 us: local(): lax.ppermute(send, 'x', [(x, x + 1 - 2 * (x % PAIR)) for x in range(X)])]
    pallas_call x5, Pallas kernels: 16.4 us -> 19.8 us  [vmem_call(): pl.pallas_call(body, out_shape=[jax.ShapeDtypeStruct(shape, kind) for sha...]
    all_to_all x1, blocking collectives: 33 us -> 30.3 us  [local(): joined = lax.all_to_all(joined, 'z', 0, 0, tiled=True)]
    ppermute x3 -> x4, starting transfers between devices: 10.5 us -> 12.9 us  [the longest x3 9.93 us: share_rows(): lax.ppermute(block, 'x', [(x, (x + away) % X) for x in range(X)])]
    unnamed x10 -> x11, local copies, waits for them, and re-layouts: 2.84 us -> 4.82 us
  transfers between devices with their start and end apart: 9 -> 10, of which waited for: 4 -> 5; matrix products, arithmetic and copies ran while one was open for 2% -> 3% of each run, Pallas kernels for 6% -> 6%
where the time goes in v8:
time: 180 us; the launch traced here: 179 us
  blocking collectives  54.9 us (30%)
  starting transfers between devices  47.6 us (26%)
  waiting for transfers between devices  34.7 us (19%)
  Pallas kernels  19.8 us (11%)
  between operations  13.6 us (8%)
  local copies, waits for them, and re-layouts  7.09 us (4%)
    all_to_all x1, blocking collectives, local(): joined = lax.all_to_all(joined, 'z', 0, 0, tiled=True)  30.3 us
    pallas_call x5, Pallas kernels, vmem_call(): pl.pallas_call(body, out_shape=[jax.ShapeDtypeStruct(shape, kind) for sha...  19.8 us
    ppermute x2, waiting for transfers between devices, local(): kv_others = [lax.ppermute(kv, 'z', turn) for turn in turns]  17.1 us
    all_to_all x1, starting transfers between devices, local(): here = lax.all_to_all(send, 'z', 0, 0, tiled=True)  15.7 us
    all_to_all x1, blocking collectives, local(): part = lax.all_to_all(part, 'x', 0, 0, tiled=True)  12.5 us
    all_to_all x1, blocking collectives, local(): packed = lax.all_to_all(packed, 'y', 0, 0, tiled=True)  12.1 us
    all_to_all x1, waiting for transfers between devices, local(): here = lax.all_to_all(send, 'z', 0, 0, tiled=True)  10.4 us
    ppermute x3, starting transfers between devices, share_rows(): lax.ppermute(block, 'x', [(x, (x + away) % X) for x in range(X)])  9.93 us
  transfers between devices with their start and end apart: 10, of which 5 were waited for; matrix products, arithmetic and copies ran while one was open for 3% of the time, Pallas kernels for 6%

profile of v8, /device:TPU:1, one launch (start us, length us, event | category | flops | bytes accessed | tf_op | source)
XLA Modules:
  0.0 178.6 jit_solution(12337891646572312220)
XLA Ops:
  6.5 2.2 %shard_map.55 = (bf16[16,144,128]{2,1,0:T(8,128)(2,1)}, bf16[5,16,640]{2,1,0:T(8,128)(2,1)}) custom-call(bf16[128,640]{1,0:T(8,128)(2,1)} %q_ref.1, bf16[128,640]{1,0:T(8,128)(2,1)} %k_ref.1, bf16[128,640]{1,0:T(8,128)(2,1)} %v_ref.1, s32[1,128]{1,0:T(1,128)} %bitcast.24, bf16[80,640]{1,0:T(8,128)(2,1)} %weight_ref.1), custom_call_target="tpu_custom_call" | custom-call | tf_op jit(solution)/shard_map/pallas_call | solution.py:39
  8.7 15.7 %all-to-all-start = ((bf16[16,144,128]{2,1,0:T(8,128)(2,1)}), bf16[16,144,128]{2,1,0:T(8,128)(2,1)S(1)}, u32[]{:S(2)}, u32[]{:S(2)}) async-start(bf16[16,144,128]{2,1,0:T(8,128)(2,1)} %get-tuple-element.9), calls=%async_computation | async-start | bytes 1179648 | tf_op jit(solution)/shard_map/all_to_all | solution.py:271
  24.5 0.8 slice_bitcast_fusion.1
  25.4 3.1 %collective-permute-start.4 = (bf16[32,640]{1,0:T(8,128)(2,1)S(1)}, bf16[32,640]{1,0:T(8,128)(2,1)S(1)}, u32[]{:S(2)}, u32[]{:S(2)}) collective-permute-start(bf16[32,640]{1,0:T(8,128)(2,1)S(1)} %pad_maximum_fusion.1), channel_id=1, source_target_pairs={{0,8},{8,16},{16,24},{24,0},{1,9},{9,17},{17,25},{25,1},{2,10},{10... | collective-permute-start | bytes 122888 | tf_op jit(solution)/shard_map/ppermute | solution.py:252
  28.5 3.4 %collective-permute-start.5 = (bf16[32,640]{1,0:T(8,128)(2,1)S(1)}, bf16[32,640]{1,0:T(8,128)(2,1)S(1)}, u32[]{:S(2)}, u32[]{:S(2)}) collective-permute-start(bf16[32,640]{1,0:T(8,128)(2,1)S(1)} %pad_maximum_fusion.1), channel_id=1, source_target_pairs={{0,24},{8,0},{16,8},{24,16},{1,25},{9,1},{17,9},{25,17},{2,26},{10... | collective-permute-start | bytes 122888 | tf_op jit(solution)/shard_map/ppermute | solution.py:252
  31.9 3.4 %collective-permute-start.3 = (bf16[48,640]{1,0:T(8,128)(2,1)S(1)}, bf16[48,640]{1,0:T(8,128)(2,1)S(1)}, u32[]{:S(2)}, u32[]{:S(2)}) collective-permute-start(bf16[48,640]{1,0:T(8,128)(2,1)S(1)} %pad_maximum_fusion), channel_id=1, source_target_pairs={{0,16},{8,24},{16,0},{24,8},{1,17},{9,25},{17,1},{25,9},{2,18},{10... | collective-permute-start | bytes 184328 | tf_op jit(solution)/shard_map/ppermute | solution.py:252
  35.3 0.7 constant_dynamic-update-slice_fusion.5
  36.1 0.7 constant_dynamic-update-slice_fusion.4
  36.8 0.7 constant_dynamic-update-slice_fusion.3
  37.6 1.1 collective-permute-done.3
  38.7 0.7 copy-done.1
  39.4 10.4 %all-to-all-done = bf16[16,144,128]{2,1,0:T(8,128)(2,1)S(1)} async-done(((bf16[16,144,128]{2,1,0:T(8,128)(2,1)}), bf16[16,144,128]{2,1,0:T(8,128)(2,1)S(1)}, u32[]{:S(2)}, u32[]{:S(2)}) %all-to-all-start) | async-done | bytes 589856 | tf_op jit(solution)/shard_map/all_to_all | solution.py:271
  49.8 4.6 %collective-permute-start = (bf16[16,96,128]{2,1,0:T(8,128)(2,1)S(1)}, bf16[16,96,128]{2,1,0:T(8,128)(2,1)S(1)}, u32[]{:S(2)}, u32[]{:S(2)}) collective-permute-start(bf16[16,96,128]{2,1,0:T(8,128)(2,1)S(1)} %slice.47.kv0_ref), channel_id=1, source_target_pairs={{0,32},{32,64},{64,0},{96,128},{128,160},{160,96},{192,224},{224,2... | collective-permute-start | bytes 1179656 | tf_op jit(solution)/shard_map/ppermute | solution.py:278
  54.5 2.0 %collective-permute-start.1 = (bf16[16,96,128]{2,1,0:T(8,128)(2,1)S(1)}, bf16[16,96,128]{2,1,0:T(8,128)(2,1)S(1)}, u32[]{:S(2)}, u32[]{:S(2)}) collective-permute-start(bf16[16,96,128]{2,1,0:T(8,128)(2,1)S(1)} %slice.47.kv0_ref), channel_id=1, source_target_pairs={{0,64},{32,0},{64,32},{96,160},{128,96},{160,128},{192,256},{224,1... | collective-permute-start | bytes 1179656 | tf_op jit(solution)/shard_map/ppermute | solution.py:278
  56.5 1.0 broadcast_in_dim.10
  57.5 4.0 %all-to-all-start.1 = ((bf16[4,768,128]{2,1,0:T(8,128)(2,1)}), bf16[4,768,128]{2,1,0:T(8,128)(2,1)S(1)}, u32[]{:S(2)}, u32[]{:S(2)}) async-start(bf16[4,768,128]{2,1,0:T(8,128)(2,1)} %broadcast_in_dim.10), calls=%async_computation.1 | async-start | bytes 1572864 | tf_op jit(solution)/shard_map/all_to_all | solution.py:280
  61.7 0.1 stack_reshape.11
  61.8 0.1 stack_reshape.10
  62.1 17.1 %collective-permute-done.1.kv2_ref = bf16[16,96,128]{2,1,0:T(8,128)(2,1)S(1)} collective-permute-done((bf16[16,96,128]{2,1,0:T(8,128)(2,1)S(1)}, bf16[16,96,128]{2,1,0:T(8,128)(2,1)S(1)}, u32[]{:S(2)}, u32[]{:S(2)}) %collective-permute-start.1) | collective-permute-done | bytes 393248 | tf_op jit(solution)/shard_map/ppermute | solution.py:278
  79.2 10.2 %shard_map.56 = bf16[4,816,128]{2,1,0:T(8,128)(2,1)S(1)} custom-call(s32[1]{0:T(128)} %bitcast.2.third_ref, bf16[4,768,128]{2,1,0:T(8,128)(2,1)S(1)} %all-to-all-done.1.q_ref, bf16[16,96,128]{2,1,0:T(8,128)(2,1)S(1)} %slice.47.kv0_ref, bf16[16,96,128]{2,1,0:T(8,128)(2,1)S(1)} %collective-permute-done.kv1_ref, ...), custom_call_target="tpu_custom_call" | custom-call | flops 68719476736 | bytes 4194304 | tf_op jit(solution)/shard_map/pallas_call | solution.py:39
  89.4 12.5 %all_to_all.25.part_ref = bf16[4,816,128]{2,1,0:T(8,128)(2,1)S(1)} all-to-all(bf16[4,816,128]{2,1,0:T(8,128)(2,1)S(1)} %shard_map.56), channel_id=1, replica_groups=mesh['z'=16,'x'=4,'y'=4,'c'=2] {'x'}, dimensions={0} | all-to-all | bytes 1671168 | tf_op jit(solution)/shard_map/all_to_all | solution.py:306
  101.9 0.6 shard_map.57
  102.6 30.3 %all_to_all.26.part_ref = bf16[16,48,128]{2,1,0:T(8,128)(2,1)S(1)} all-to-all(bf16[16,48,128]{2,1,0:T(8,128)(2,1)S(1)} %shard_map.57), channel_id=1, replica_groups=mesh['z'=16,'x'=4,'y'=4,'c'=2] {'z'}, dimensions={0} | all-to-all | bytes 393216 | tf_op jit(solution)/shard_map/all_to_all | solution.py:308
  132.8 0.1 shard_map.58
  133.0 12.1 %all_to_all.27.mine_ref = bf16[4,720,128]{2,1,0:T(8,128)(2,1)S(1)} all-to-all(bf16[4,720,128]{2,1,0:T(8,128)(2,1)S(1)} %shard_map.58), channel_id=1, replica_groups=mesh['z'=16,'x'=4,'y'=4,'c'=2] {'y'}, dimensions={0} | all-to-all | bytes 1474560 | tf_op jit(solution)/shard_map/all_to_all | solution.py:310
  145.1 8.3 %collective-permute-start.2 = (bf16[4,720,128]{2,1,0:T(8,128)(2,1)S(1)}, bf16[4,720,128]{2,1,0:T(8,128)(2,1)S(1)}, u32[]{:S(2)}, u32[]{:S(2)}) collective-permute-start(bf16[4,720,128]{2,1,0:T(8,128)(2,1)S(1)} %all_to_all.27.mine_ref), channel_id=1, source_target_pairs={{0,1},{1,0},{2,3},{3,2},{4,5},{5,4},{6,7},{7,6},{8,9},{9,8},{10,11... | collective-permute-start | bytes 2211848 | tf_op jit(solution)/shard_map/ppermute | solution.py:311
  153.4 1.7 collective-permute-done.2.other_ref
  155.2 1.9 %copy-done = bf16[2560,640]{1,0:T(8,128)(2,1)S(1)} copy-done((bf16[2560,640]{1,0:T(8,128)(2,1)S(1)}, bf16[2560,640]{1,0:T(8,128)(2,1)}, u32[]{:S(2)}) %copy-start) | copy-done | bytes 3276824
  157.1 6.7 %shard_map.59 = (f32[128,640]{1,0:T(8,128)S(1)}, bf16[128,640]{1,0:T(8,128)(2,1)S(1)}) custom-call(s32[2]{0:T(128)S(1)} %pad_add_fusion.place_ref, bf16[4,720,128]{2,1,0:T(8,128)(2,1)S(1)} %all_to_all.27.mine_ref, bf16[4,720,128]{2,1,0:T(8,128)(2,1)S(1)} %collective-permute-done.2.other_ref, bf16[2560,640]{1,0:T(8,128)(2,1)S(1)} %copy-done), custom_call_target="tpu_custom_call" | custom-call | tf_op jit(solution)/shard_map/pallas_call | solution.py:39
  163.8 3.0 %collective-permute-start.6 = (bf16[128,640]{1,0:T(8,128)(2,1)S(1)}, bf16[128,640]{1,0:T(8,128)(2,1)S(1)}, u32[]{:S(2)}, u32[]{:S(2)}) collective-permute-start(bf16[128,640]{1,0:T(8,128)(2,1)S(1)} %get-tuple-element.12), channel_id=1, source_target_pairs={{0,8},{8,0},{16,24},{24,16},{1,9},{9,1},{17,25},{25,17},{2,10},{10... | collective-permute-start | bytes 491528 | tf_op jit(solution)/shard_map/ppermute | solution.py:323
  166.8 4.3 %collective-permute-done.6 = bf16[128,640]{1,0:T(8,128)(2,1)S(1)} collective-permute-done((bf16[128,640]{1,0:T(8,128)(2,1)S(1)}, bf16[128,640]{1,0:T(8,128)(2,1)S(1)}, u32[]{:S(2)}, u32[]{:S(2)}) %collective-permute-start.6) | collective-permute-done | bytes 163872 | tf_op jit(solution)/shard_map/ppermute | solution.py:323
  171.0 0.7 add_convert_fusion
  (29 shorter events, 0.6 us)
Async XLA Ops:
  6.5 55.4 %copy-start.2 = (pred[48]{0:T(512)(128)(4,1)S(1)}, pred[48]{0:T(512)(128)(4,1)}, u32[]{:S(2)}) copy-start(pred[48]{0:T(512)(128)(4,1)} %constant.22.clone.1) | copy-start | bytes 148
  8.7 41.1 %all-to-all-start = ((bf16[16,144,128]{2,1,0:T(8,128)(2,1)}), bf16[16,144,128]{2,1,0:T(8,128)(2,1)S(1)}, u32[]{:S(2)}, u32[]{:S(2)}) async-start(bf16[16,144,128]{2,1,0:T(8,128)(2,1)} %get-tuple-element.9), calls=%async_computation | async-start | bytes 1179648 | tf_op jit(solution)/shard_map/all_to_all | solution.py:271
  24.5 130.7 %all-gather.2.cloned.1.call-start = ((), (), s32[]{:S(2)}) async-start(), calls=%async_computation.5 | async-start | bytes 3481600 | tf_op jit(solution)/shard_map/all_gather | solution.py:272
  25.4 13.3 %collective-permute-start.4 = (bf16[32,640]{1,0:T(8,128)(2,1)S(1)}, bf16[32,640]{1,0:T(8,128)(2,1)S(1)}, u32[]{:S(2)}, u32[]{:S(2)}) collective-permute-start(bf16[32,640]{1,0:T(8,128)(2,1)S(1)} %pad_maximum_fusion.1), channel_id=1, source_target_pairs={{0,8},{8,16},{16,24},{24,0},{1,9},{9,17},{17,25},{25,1},{2,10},{10... | collective-permute-start | bytes 122888 | tf_op jit(solution)/shard_map/ppermute | solution.py:252
  28.5 10.2 %collective-permute-start.5 = (bf16[32,640]{1,0:T(8,128)(2,1)S(1)}, bf16[32,640]{1,0:T(8,128)(2,1)S(1)}, u32[]{:S(2)}, u32[]{:S(2)}) collective-permute-start(bf16[32,640]{1,0:T(8,128)(2,1)S(1)} %pad_maximum_fusion.1), channel_id=1, source_target_pairs={{0,24},{8,0},{16,8},{24,16},{1,25},{9,1},{17,9},{25,17},{2,26},{10... | collective-permute-start | bytes 122888 | tf_op jit(solution)/shard_map/ppermute | solution.py:252
  31.9 6.8 %collective-permute-start.3 = (bf16[48,640]{1,0:T(8,128)(2,1)S(1)}, bf16[48,640]{1,0:T(8,128)(2,1)S(1)}, u32[]{:S(2)}, u32[]{:S(2)}) collective-permute-start(bf16[48,640]{1,0:T(8,128)(2,1)S(1)} %pad_maximum_fusion), channel_id=1, source_target_pairs={{0,16},{8,24},{16,0},{24,8},{1,17},{9,25},{17,1},{25,9},{2,18},{10... | collective-permute-start | bytes 184328 | tf_op jit(solution)/shard_map/ppermute | solution.py:252
  38.7 0.7 copy-start.1
  49.8 12.2 %collective-permute-start = (bf16[16,96,128]{2,1,0:T(8,128)(2,1)S(1)}, bf16[16,96,128]{2,1,0:T(8,128)(2,1)S(1)}, u32[]{:S(2)}, u32[]{:S(2)}) collective-permute-start(bf16[16,96,128]{2,1,0:T(8,128)(2,1)S(1)} %slice.47.kv0_ref), channel_id=1, source_target_pairs={{0,32},{32,64},{64,0},{96,128},{128,160},{160,96},{192,224},{224,2... | collective-permute-start | bytes 1179656 | tf_op jit(solution)/shard_map/ppermute | solution.py:278
  54.5 24.7 %collective-permute-start.1 = (bf16[16,96,128]{2,1,0:T(8,128)(2,1)S(1)}, bf16[16,96,128]{2,1,0:T(8,128)(2,1)S(1)}, u32[]{:S(2)}, u32[]{:S(2)}) collective-permute-start(bf16[16,96,128]{2,1,0:T(8,128)(2,1)S(1)} %slice.47.kv0_ref), channel_id=1, source_target_pairs={{0,64},{32,0},{64,32},{96,160},{128,96},{160,128},{192,256},{224,1... | collective-permute-start | bytes 1179656 | tf_op jit(solution)/shard_map/ppermute | solution.py:278
  57.5 21.7 %all-to-all-start.1 = ((bf16[4,768,128]{2,1,0:T(8,128)(2,1)}), bf16[4,768,128]{2,1,0:T(8,128)(2,1)S(1)}, u32[]{:S(2)}, u32[]{:S(2)}) async-start(bf16[4,768,128]{2,1,0:T(8,128)(2,1)} %broadcast_in_dim.10), calls=%async_computation.1 | async-start | bytes 1572864 | tf_op jit(solution)/shard_map/all_to_all | solution.py:280
  145.1 10.1 %collective-permute-start.2 = (bf16[4,720,128]{2,1,0:T(8,128)(2,1)S(1)}, bf16[4,720,128]{2,1,0:T(8,128)(2,1)S(1)}, u32[]{:S(2)}, u32[]{:S(2)}) collective-permute-start(bf16[4,720,128]{2,1,0:T(8,128)(2,1)S(1)} %all_to_all.27.mine_ref), channel_id=1, source_target_pairs={{0,1},{1,0},{2,3},{3,2},{4,5},{5,4},{6,7},{7,6},{8,9},{9,8},{10,11... | collective-permute-start | bytes 2211848 | tf_op jit(solution)/shard_map/ppermute | solution.py:311
  155.2 1.9 %copy-start = (bf16[2560,640]{1,0:T(8,128)(2,1)S(1)}, bf16[2560,640]{1,0:T(8,128)(2,1)}, u32[]{:S(2)}) copy-start(bf16[2560,640]{1,0:T(8,128)(2,1)} %all-gather.2.cloned.1.call-done.hbm_ref) | copy-start | bytes 9830404
  163.8 7.3 %collective-permute-start.6 = (bf16[128,640]{1,0:T(8,128)(2,1)S(1)}, bf16[128,640]{1,0:T(8,128)(2,1)S(1)}, u32[]{:S(2)}, u32[]{:S(2)}) collective-permute-start(bf16[128,640]{1,0:T(8,128)(2,1)S(1)} %get-tuple-element.12), channel_id=1, source_target_pairs={{0,8},{8,0},{16,24},{24,16},{1,9},{9,1},{17,25},{25,17},{2,10},{10... | collective-permute-start | bytes 491528 | tf_op jit(solution)/shard_map/ppermute | solution.py:323
Sparse Core Ops, SparseCore 0:
  39.5 81.2 all-gather.1

commit v9 on v8

--- a/solution.py
+++ b/solution.py
@@ -28,20 +28,17 @@
 GRANULE = 16
 
 
-def vmem_call(body, mebibytes, shapes, *operands, scalars=None, left=(), scratch=(), kinds=None, cost=None):
+def vmem_call(body, mebibytes, shapes, *operands, scalars=None, kinds=None, cost=None):
     specs = [pl.BlockSpec(memory_space=pltpu.VMEM)] * len(operands)
-    specs += [pl.BlockSpec(memory_space=pltpu.HBM)] * len(left)
-    operands += tuple(left)
-    kinds = kinds or [BF16] * len(shapes)
     if scalars is not None:
         specs = [pl.BlockSpec(memory_space=pltpu.SMEM)] + specs
         operands = (scalars,) + operands
+    kinds = kinds or [BF16] * len(shapes)
     return pl.pallas_call(
         body,
         out_shape=[jax.ShapeDtypeStruct(shape, kind) for shape, kind in zip(shapes, kinds)],
         in_specs=specs,
         out_specs=[pl.BlockSpec(memory_space=pltpu.VMEM)] * len(shapes),
-        scratch_shapes=list(scratch),
         cost_estimate=cost,
         compiler_params=pltpu.CompilerParams(vmem_limit_bytes=mebibytes * 1024 * 1024),
     )(*operands)
@@ -194,17 +191,8 @@
             out_ref[y, first : first + SLOT, :] = part_ref[PARTS * (HEADS_HERE - 1) + r]
 
 
-def project(place_ref, mine_ref, other_ref, hbm_ref, own_ref, send_ref, weight_ref, sems):
-    core, side = place_ref[0], place_ref[1]
+def multiply(core, side, packed_ref, weight_ref):
     depth = weight_ref.shape[0] // Z
-    copies = [
-        pltpu.make_async_copy(
-            hbm_ref.at[pl.ds(z * depth, depth), :], weight_ref.at[pl.ds(z * depth, depth), :], sems.at[z]
-        )
-        for z in range(Z)
-    ]
-    for copy in copies:
-        copy.start()
     member = lax.rem(side, PAIR)
     places = []
     for m in range(depth // GRANULE):
@@ -217,31 +205,38 @@
     halves = lax.broadcasted_iota(jnp.int32, (span, HEAD), 1) < SHARE
     per_head = SHARE // GRANULE
     inputs = [[] for _ in range(PAIR)]
-    for y in range(Y):
-        for ref in (mine_ref, other_ref):
-            fifth = ref[y, 2 * PAIR * span :, :].astype(F32)
-            for x in range(PAIR):
-                inputs[x] += [ref[y, (2 * x + two) * span : (2 * x + two + 1) * span, :] for two in range(2)]
-                inputs[x].append(jnp.where(halves == (x == 0), fifth, 0.0).astype(BF16))
-    inputs = [jnp.concatenate(blocks, axis=1) for blocks in inputs]
-    for copy in copies:
-        copy.wait()
     weights = []
     for y in range(Y):
-        for which in (core, 1 - core):
-            rows = []
-            for n in range(HEADS_HERE * per_head):
-                first = ((C * y + which) * 2 + n // len(places)) * depth + places[n % len(places)]
-                rows.append(weight_ref[pl.ds(pl.multiple_of(first, GRANULE), GRANULE), :])
-            weights += rows + rows[4 * per_head :]
+        fifth = packed_ref[y, 2 * PAIR * span :, :].astype(F32)
+        for x in range(PAIR):
+            inputs[x] += [packed_ref[y, (2 * x + two) * span : (2 * x + two + 1) * span, :] for two in range(2)]
+            inputs[x].append(jnp.where(halves == (x == 0), fifth, 0.0).astype(BF16))
+        rows = []
+        for n in range(HEADS_HERE * per_head):
+            first = ((C * y + core) * 2 + n // len(places)) * depth + places[n % len(places)]
+            rows.append(weight_ref[pl.ds(pl.multiple_of(first, GRANULE), GRANULE), :])
+        weights += rows + rows[4 * per_head :]
     weights = jnp.concatenate(weights, axis=0)
+    return [
+        jnp.dot(jnp.concatenate(blocks, axis=1), weights, preferred_element_type=F32) for blocks in inputs
+    ]
+
+
+def project_mine(place_ref, packed_ref, weight_ref, sum_ref):
+    for x, total in enumerate(multiply(place_ref[0], place_ref[1], packed_ref, weight_ref)):
+        sum_ref[x] = total
+
+
+def project_other(place_ref, packed_ref, weight_ref, sum_ref, own_ref, send_ref):
+    side = place_ref[1]
     totals = []
-    for x in range(PAIR):
-        total = jnp.dot(inputs[x], weights, preferred_element_type=F32)
+    for x, total in enumerate(multiply(1 - place_ref[0], side, packed_ref, weight_ref)):
+        total = total + sum_ref[x]
         total = [total[r * SLOT : r * SLOT + length] for r, length in enumerate(LENGTHS)]
         totals.append(jnp.concatenate(total, axis=0))
-    own_ref[...] = jnp.where(member == 0, totals[0], totals[1])
-    send_ref[...] = jnp.where(member == 0, totals[1], totals[0]).astype(BF16)
+    first = lax.rem(side, PAIR) == 0
+    own_ref[...] = jnp.where(first, totals[0], totals[1])
+    send_ref[...] = jnp.where(first, totals[1], totals[0]).astype(BF16)
 
 
 def share_rows(granules):
@@ -309,15 +304,25 @@
     (packed,) = vmem_call(assemble, 8, [(Y, (2 * PAIR + 1) * PARTS * SLOT, HEAD)], joined)
     packed = lax.all_to_all(packed, "y", 0, 0, tiled=True)
     others = lax.ppermute(packed, "c", [(0, 1), (1, 0)])
+    place = jnp.stack([core, side])
+    (sums,) = vmem_call(
+        project_mine,
+        16,
+        [(PAIR, PARTS * SLOT, width)],
+        packed,
+        weight,
+        scalars=place,
+        kinds=[F32],
+        cost=pl.CostEstimate(flops=1 << 31, bytes_accessed=1 << 23, transcendentals=0),
+    )
     own, send = vmem_call(
-        project,
-        24,
+        project_other,
+        16,
         [(TOK, width), (TOK, width)],
-        packed,
         others,
-        scalars=jnp.stack([core, side]),
-        left=[weight],
-        scratch=[pltpu.VMEM(weight.shape, BF16), pltpu.SemaphoreType.DMA((Z,))],
+        weight,
+        sums,
+        scalars=place,
         kinds=[F32, BF16],
     )
     came = lax.ppermute(send, "x", [(x, x + 1 - 2 * (x % PAIR)) for x in range(X)])

time: 180 us -> 175 us (0.972)
  Pallas kernels: 19.8 us -> 16.2 us
    pallas_call x5 -> x6, Pallas kernels: 19.8 us -> 16.2 us  [vmem_call(): pl.pallas_call(body, out_shape=[jax.ShapeDtypeStruct(shape, kind) for sha...]
    unnamed x11 -> x13, local copies, waits for them, and re-layouts: 4.82 us -> 5.23 us
  transfers between devices with their start and end apart: 10 -> 10, of which waited for: 5 -> 4; matrix products, arithmetic and copies ran while one was open for 3% -> 3% of each run, Pallas kernels for 6% -> 7%
where the time goes in v9:
time: 175 us; the launch traced here: 174 us
  blocking collectives  54.8 us (31%)
  starting transfers between devices  47.5 us (27%)
  waiting for transfers between devices  33.3 us (19%)
  Pallas kernels  16.2 us (9%)
  between operations  13.6 us (8%)
  local copies, waits for them, and re-layouts  7.48 us (4%)
    all_to_all x1, blocking collectives, local(): joined = lax.all_to_all(joined, 'z', 0, 0, tiled=True)  30.3 us
    ppermute x2, waiting for transfers between devices, local(): kv_others = [lax.ppermute(kv, 'z', turn) for turn in turns]  17.2 us
    pallas_call x6, Pallas kernels, vmem_call(): pl.pallas_call(body, out_shape=[jax.ShapeDtypeStruct(shape, kind) for sha...  16.2 us
    all_to_all x1, starting transfers between devices, local(): here = lax.all_to_all(send, 'z', 0, 0, tiled=True)  15.7 us
    all_to_all x1, blocking collectives, local(): part = lax.all_to_all(part, 'x', 0, 0, tiled=True)  12.4 us
    all_to_all x1, blocking collectives, local(): packed = lax.all_to_all(packed, 'y', 0, 0, tiled=True)  12.1 us
    all_to_all x1, waiting for transfers between devices, local(): here = lax.all_to_all(send, 'z', 0, 0, tiled=True)  10.4 us
    ppermute x3, starting transfers between devices, share_rows(): lax.ppermute(block, 'x', [(x, (x + away) % X) for x in range(X)])  9.93 us
  transfers between devices with their start and end apart: 10, of which 4 were waited for; matrix products, arithmetic and copies ran while one was open for 3% of the time, Pallas kernels for 7%

profile of v9, /device:TPU:1, one launch (start us, length us, event | category | flops | bytes accessed | tf_op | source)
XLA Modules:
  0.0 173.9 jit_solution(10733168198291216490)
XLA Ops:
  6.5 2.2 %shard_map.55 = (bf16[16,144,128]{2,1,0:T(8,128)(2,1)}, bf16[5,16,640]{2,1,0:T(8,128)(2,1)}) custom-call(bf16[128,640]{1,0:T(8,128)(2,1)} %q_ref.1, bf16[128,640]{1,0:T(8,128)(2,1)} %k_ref.1, bf16[128,640]{1,0:T(8,128)(2,1)} %v_ref.1, s32[1,128]{1,0:T(1,128)} %bitcast.24, bf16[80,640]{1,0:T(8,128)(2,1)} %weight_ref.1), custom_call_target="tpu_custom_call" | custom-call | tf_op jit(solution)/shard_map/pallas_call | solution.py:37
  8.7 15.7 %all-to-all-start = ((bf16[16,144,128]{2,1,0:T(8,128)(2,1)}), bf16[16,144,128]{2,1,0:T(8,128)(2,1)S(1)}, u32[]{:S(2)}, u32[]{:S(2)}) async-start(bf16[16,144,128]{2,1,0:T(8,128)(2,1)} %get-tuple-element.9), calls=%async_computation | async-start | bytes 1179648 | tf_op jit(solution)/shard_map/all_to_all | solution.py:266
  24.5 0.8 slice_bitcast_fusion.1
  25.4 3.1 %collective-permute-start.4 = (bf16[32,640]{1,0:T(8,128)(2,1)S(1)}, bf16[32,640]{1,0:T(8,128)(2,1)S(1)}, u32[]{:S(2)}, u32[]{:S(2)}) collective-permute-start(bf16[32,640]{1,0:T(8,128)(2,1)S(1)} %pad_maximum_fusion.1), channel_id=1, source_target_pairs={{0,8},{8,16},{16,24},{24,0},{1,9},{9,17},{17,25},{25,1},{2,10},{10... | collective-permute-start | bytes 122888 | tf_op jit(solution)/shard_map/ppermute | solution.py:247
  28.5 3.4 %collective-permute-start.5 = (bf16[32,640]{1,0:T(8,128)(2,1)S(1)}, bf16[32,640]{1,0:T(8,128)(2,1)S(1)}, u32[]{:S(2)}, u32[]{:S(2)}) collective-permute-start(bf16[32,640]{1,0:T(8,128)(2,1)S(1)} %pad_maximum_fusion.1), channel_id=1, source_target_pairs={{0,24},{8,0},{16,8},{24,16},{1,25},{9,1},{17,9},{25,17},{2,26},{10... | collective-permute-start | bytes 122888 | tf_op jit(solution)/shard_map/ppermute | solution.py:247
  31.9 3.4 %collective-permute-start.3 = (bf16[48,640]{1,0:T(8,128)(2,1)S(1)}, bf16[48,640]{1,0:T(8,128)(2,1)S(1)}, u32[]{:S(2)}, u32[]{:S(2)}) collective-permute-start(bf16[48,640]{1,0:T(8,128)(2,1)S(1)} %pad_maximum_fusion), channel_id=1, source_target_pairs={{0,16},{8,24},{16,0},{24,8},{1,17},{9,25},{17,1},{25,9},{2,18},{10... | collective-permute-start | bytes 184328 | tf_op jit(solution)/shard_map/ppermute | solution.py:247
  35.3 0.7 constant_dynamic-update-slice_fusion.5
  36.1 0.7 constant_dynamic-update-slice_fusion.4
  36.8 0.7 constant_dynamic-update-slice_fusion.3
  37.5 1.1 collective-permute-done.3
  38.7 0.7 copy-done.2
  39.4 10.4 %all-to-all-done = bf16[16,144,128]{2,1,0:T(8,128)(2,1)S(1)} async-done(((bf16[16,144,128]{2,1,0:T(8,128)(2,1)}), bf16[16,144,128]{2,1,0:T(8,128)(2,1)S(1)}, u32[]{:S(2)}, u32[]{:S(2)}) %all-to-all-start) | async-done | bytes 589856 | tf_op jit(solution)/shard_map/all_to_all | solution.py:266
  49.8 4.6 %collective-permute-start = (bf16[16,96,128]{2,1,0:T(8,128)(2,1)S(1)}, bf16[16,96,128]{2,1,0:T(8,128)(2,1)S(1)}, u32[]{:S(2)}, u32[]{:S(2)}) collective-permute-start(bf16[16,96,128]{2,1,0:T(8,128)(2,1)S(1)} %slice.47.kv0_ref), channel_id=1, source_target_pairs={{0,32},{32,64},{64,0},{96,128},{128,160},{160,96},{192,224},{224,2... | collective-permute-start | bytes 1179656 | tf_op jit(solution)/shard_map/ppermute | solution.py:273
  54.5 2.0 %collective-permute-start.1 = (bf16[16,96,128]{2,1,0:T(8,128)(2,1)S(1)}, bf16[16,96,128]{2,1,0:T(8,128)(2,1)S(1)}, u32[]{:S(2)}, u32[]{:S(2)}) collective-permute-start(bf16[16,96,128]{2,1,0:T(8,128)(2,1)S(1)} %slice.47.kv0_ref), channel_id=1, source_target_pairs={{0,64},{32,0},{64,32},{96,160},{128,96},{160,128},{192,256},{224,1... | collective-permute-start | bytes 1179656 | tf_op jit(solution)/shard_map/ppermute | solution.py:273
  56.5 1.0 broadcast_in_dim.10
  57.5 4.0 %all-to-all-start.1 = ((bf16[4,768,128]{2,1,0:T(8,128)(2,1)}), bf16[4,768,128]{2,1,0:T(8,128)(2,1)S(1)}, u32[]{:S(2)}, u32[]{:S(2)}) async-start(bf16[4,768,128]{2,1,0:T(8,128)(2,1)} %broadcast_in_dim.10), calls=%async_computation.1 | async-start | bytes 1572864 | tf_op jit(solution)/shard_map/all_to_all | solution.py:275
  61.7 0.1 stack_reshape.11
  62.0 17.2 %collective-permute-done.1.kv2_ref = bf16[16,96,128]{2,1,0:T(8,128)(2,1)S(1)} collective-permute-done((bf16[16,96,128]{2,1,0:T(8,128)(2,1)S(1)}, bf16[16,96,128]{2,1,0:T(8,128)(2,1)S(1)}, u32[]{:S(2)}, u32[]{:S(2)}) %collective-permute-start.1) | collective-permute-done | bytes 393248 | tf_op jit(solution)/shard_map/ppermute | solution.py:273
  79.3 10.2 %shard_map.56 = bf16[4,816,128]{2,1,0:T(8,128)(2,1)S(1)} custom-call(s32[1]{0:T(128)} %bitcast.2.third_ref, bf16[4,768,128]{2,1,0:T(8,128)(2,1)S(1)} %all-to-all-done.1.q_ref, bf16[16,96,128]{2,1,0:T(8,128)(2,1)S(1)} %slice.47.kv0_ref, bf16[16,96,128]{2,1,0:T(8,128)(2,1)S(1)} %collective-permute-done.kv1_ref, ...), custom_call_target="tpu_custom_call" | custom-call | flops 68719476736 | bytes 4194304 | tf_op jit(solution)/shard_map/pallas_call | solution.py:37
  89.5 12.4 %all_to_all.25.part_ref = bf16[4,816,128]{2,1,0:T(8,128)(2,1)S(1)} all-to-all(bf16[4,816,128]{2,1,0:T(8,128)(2,1)S(1)} %shard_map.56), channel_id=1, replica_groups=mesh['z'=16,'x'=4,'y'=4,'c'=2] {'x'}, dimensions={0} | all-to-all | bytes 1671168 | tf_op jit(solution)/shard_map/all_to_all | solution.py:301
  101.9 0.6 shard_map.57
  102.6 30.3 %all_to_all.26.part_ref = bf16[16,48,128]{2,1,0:T(8,128)(2,1)S(1)} all-to-all(bf16[16,48,128]{2,1,0:T(8,128)(2,1)S(1)} %shard_map.57), channel_id=1, replica_groups=mesh['z'=16,'x'=4,'y'=4,'c'=2] {'z'}, dimensions={0} | all-to-all | bytes 393216 | tf_op jit(solution)/shard_map/all_to_all | solution.py:303
  132.8 0.1 shard_map.58
  132.9 12.1 %all_to_all.27.packed_ref = bf16[4,720,128]{2,1,0:T(8,128)(2,1)S(1)} all-to-all(bf16[4,720,128]{2,1,0:T(8,128)(2,1)S(1)} %shard_map.58), channel_id=1, replica_groups=mesh['z'=16,'x'=4,'y'=4,'c'=2] {'y'}, dimensions={0} | all-to-all | bytes 1474560 | tf_op jit(solution)/shard_map/all_to_all | solution.py:305
  145.1 8.1 %collective-permute-start.2 = (bf16[4,720,128]{2,1,0:T(8,128)(2,1)S(1)}, bf16[4,720,128]{2,1,0:T(8,128)(2,1)S(1)}, u32[]{:S(2)}, u32[]{:S(2)}) collective-permute-start(bf16[4,720,128]{2,1,0:T(8,128)(2,1)S(1)} %all_to_all.27.packed_ref), channel_id=1, source_target_pairs={{0,1},{1,0},{2,3},{3,2},{4,5},{5,4},{6,7},{7,6},{8,9},{9,8},{10,11... | collective-permute-start | bytes 2211848 | tf_op jit(solution)/shard_map/ppermute | solution.py:306
  153.2 1.9 %copy-done = bf16[2560,640]{1,0:T(8,128)(2,1)S(1)} copy-done((bf16[2560,640]{1,0:T(8,128)(2,1)S(1)}, bf16[2560,640]{1,0:T(8,128)(2,1)}, u32[]{:S(2)}) %copy-start) | copy-done | bytes 3276824
  155.1 1.5 shard_map.59.sum_ref
  156.7 0.4 copy-done.1
  157.1 1.5 shard_map.60
  158.6 3.1 %collective-permute-start.6 = (bf16[128,640]{1,0:T(8,128)(2,1)S(1)}, bf16[128,640]{1,0:T(8,128)(2,1)S(1)}, u32[]{:S(2)}, u32[]{:S(2)}) collective-permute-start(bf16[128,640]{1,0:T(8,128)(2,1)S(1)} %get-tuple-element.12), channel_id=1, source_target_pairs={{0,8},{8,0},{16,24},{24,16},{1,9},{9,1},{17,25},{25,17},{2,10},{10... | collective-permute-start | bytes 491528 | tf_op jit(solution)/shard_map/ppermute | solution.py:328
  161.7 4.6 %collective-permute-done.6 = bf16[128,640]{1,0:T(8,128)(2,1)S(1)} collective-permute-done((bf16[128,640]{1,0:T(8,128)(2,1)S(1)}, bf16[128,640]{1,0:T(8,128)(2,1)S(1)}, u32[]{:S(2)}, u32[]{:S(2)}) %collective-permute-start.6) | collective-permute-done | bytes 163872 | tf_op jit(solution)/shard_map/ppermute | solution.py:328
  166.3 0.7 add_convert_fusion
  (32 shorter events, 0.7 us)
Async XLA Ops:
  6.5 55.4 %copy-start.3 = (pred[48]{0:T(512)(128)(4,1)S(1)}, pred[48]{0:T(512)(128)(4,1)}, u32[]{:S(2)}) copy-start(pred[48]{0:T(512)(128)(4,1)} %constant.22.clone.1) | copy-start | bytes 148
  8.7 41.1 %all-to-all-start = ((bf16[16,144,128]{2,1,0:T(8,128)(2,1)}), bf16[16,144,128]{2,1,0:T(8,128)(2,1)S(1)}, u32[]{:S(2)}, u32[]{:S(2)}) async-start(bf16[16,144,128]{2,1,0:T(8,128)(2,1)} %get-tuple-element.9), calls=%async_computation | async-start | bytes 1179648 | tf_op jit(solution)/shard_map/all_to_all | solution.py:266
  24.5 128.7 %all-gather.2.cloned.1.call-start = ((), (), s32[]{:S(2)}) async-start(), calls=%async_computation.5 | async-start | bytes 3481600 | tf_op jit(solution)/shard_map/all_gather | solution.py:267
  25.4 13.3 %collective-permute-start.4 = (bf16[32,640]{1,0:T(8,128)(2,1)S(1)}, bf16[32,640]{1,0:T(8,128)(2,1)S(1)}, u32[]{:S(2)}, u32[]{:S(2)}) collective-permute-start(bf16[32,640]{1,0:T(8,128)(2,1)S(1)} %pad_maximum_fusion.1), channel_id=1, source_target_pairs={{0,8},{8,16},{16,24},{24,0},{1,9},{9,17},{17,25},{25,1},{2,10},{10... | collective-permute-start | bytes 122888 | tf_op jit(solution)/shard_map/ppermute | solution.py:247
  28.5 10.2 %collective-permute-start.5 = (bf16[32,640]{1,0:T(8,128)(2,1)S(1)}, bf16[32,640]{1,0:T(8,128)(2,1)S(1)}, u32[]{:S(2)}, u32[]{:S(2)}) collective-permute-start(bf16[32,640]{1,0:T(8,128)(2,1)S(1)} %pad_maximum_fusion.1), channel_id=1, source_target_pairs={{0,24},{8,0},{16,8},{24,16},{1,25},{9,1},{17,9},{25,17},{2,26},{10... | collective-permute-start | bytes 122888 | tf_op jit(solution)/shard_map/ppermute | solution.py:247
  31.9 6.8 %collective-permute-start.3 = (bf16[48,640]{1,0:T(8,128)(2,1)S(1)}, bf16[48,640]{1,0:T(8,128)(2,1)S(1)}, u32[]{:S(2)}, u32[]{:S(2)}) collective-permute-start(bf16[48,640]{1,0:T(8,128)(2,1)S(1)} %pad_maximum_fusion), channel_id=1, source_target_pairs={{0,16},{8,24},{16,0},{24,8},{1,17},{9,25},{17,1},{25,9},{2,18},{10... | collective-permute-start | bytes 184328 | tf_op jit(solution)/shard_map/ppermute | solution.py:247
  38.7 0.7 copy-start.2
  49.8 12.2 %collective-permute-start = (bf16[16,96,128]{2,1,0:T(8,128)(2,1)S(1)}, bf16[16,96,128]{2,1,0:T(8,128)(2,1)S(1)}, u32[]{:S(2)}, u32[]{:S(2)}) collective-permute-start(bf16[16,96,128]{2,1,0:T(8,128)(2,1)S(1)} %slice.47.kv0_ref), channel_id=1, source_target_pairs={{0,32},{32,64},{64,0},{96,128},{128,160},{160,96},{192,224},{224,2... | collective-permute-start | bytes 1179656 | tf_op jit(solution)/shard_map/ppermute | solution.py:273
  54.5 24.8 %collective-permute-start.1 = (bf16[16,96,128]{2,1,0:T(8,128)(2,1)S(1)}, bf16[16,96,128]{2,1,0:T(8,128)(2,1)S(1)}, u32[]{:S(2)}, u32[]{:S(2)}) collective-permute-start(bf16[16,96,128]{2,1,0:T(8,128)(2,1)S(1)} %slice.47.kv0_ref), channel_id=1, source_target_pairs={{0,64},{32,0},{64,32},{96,160},{128,96},{160,128},{192,256},{224,1... | collective-permute-start | bytes 1179656 | tf_op jit(solution)/shard_map/ppermute | solution.py:273
  57.5 21.8 %all-to-all-start.1 = ((bf16[4,768,128]{2,1,0:T(8,128)(2,1)}), bf16[4,768,128]{2,1,0:T(8,128)(2,1)S(1)}, u32[]{:S(2)}, u32[]{:S(2)}) async-start(bf16[4,768,128]{2,1,0:T(8,128)(2,1)} %broadcast_in_dim.10), calls=%async_computation.1 | async-start | bytes 1572864 | tf_op jit(solution)/shard_map/all_to_all | solution.py:275
  145.1 11.6 %collective-permute-start.2 = (bf16[4,720,128]{2,1,0:T(8,128)(2,1)S(1)}, bf16[4,720,128]{2,1,0:T(8,128)(2,1)S(1)}, u32[]{:S(2)}, u32[]{:S(2)}) collective-permute-start(bf16[4,720,128]{2,1,0:T(8,128)(2,1)S(1)} %all_to_all.27.packed_ref), channel_id=1, source_target_pairs={{0,1},{1,0},{2,3},{3,2},{4,5},{5,4},{6,7},{7,6},{8,9},{9,8},{10,11... | collective-permute-start | bytes 2211848 | tf_op jit(solution)/shard_map/ppermute | solution.py:306
  153.2 1.9 %copy-start = (bf16[2560,640]{1,0:T(8,128)(2,1)S(1)}, bf16[2560,640]{1,0:T(8,128)(2,1)}, u32[]{:S(2)}) copy-start(bf16[2560,640]{1,0:T(8,128)(2,1)} %all-gather.2.cloned.1.call-done.weight_ref) | copy-start | bytes 9830404
  155.1 1.9 %copy-start.1 = (bf16[2560,640]{1,0:T(8,128)(2,1)S(1)}, bf16[2560,640]{1,0:T(8,128)(2,1)}, u32[]{:S(2)}) copy-start(bf16[2560,640]{1,0:T(8,128)(2,1)} %all-gather.2.cloned.1.call-done.weight_ref) | copy-start | bytes 9830404
  158.6 7.7 %collective-permute-start.6 = (bf16[128,640]{1,0:T(8,128)(2,1)S(1)}, bf16[128,640]{1,0:T(8,128)(2,1)S(1)}, u32[]{:S(2)}, u32[]{:S(2)}) collective-permute-start(bf16[128,640]{1,0:T(8,128)(2,1)S(1)} %get-tuple-element.12), channel_id=1, source_target_pairs={{0,8},{8,0},{16,24},{24,16},{1,9},{9,1},{17,25},{25,17},{2,10},{10... | collective-permute-start | bytes 491528 | tf_op jit(solution)/shard_map/ppermute | solution.py:328
Sparse Core Ops, SparseCore 0:
  39.5 81.2 all-gather.1

commit v10 on v9

--- a/solution.py
+++ b/solution.py
@@ -16,6 +16,7 @@
 STARTS = (0, 44, 88)
 LENGTHS = (44, 44, 40)
 SLOT = 48
+ROWS = 44
 ID_ROW = 46
 POSITIONS = 8192
 NEVER = 1e9
@@ -60,19 +61,21 @@
     origin = (to % SHARE) // GRANULE * (PAIR * GRANULE) + to // SHARE * GRANULE + to % GRANULE
     turn = jnp.where(source == origin, 1.0, 0.0).astype(BF16)
     for h in range(HEADS_HERE):
+        blocks = []
         for part, ref in enumerate((q_ref, k_ref, v_ref)):
             block = ref[:, h * HEAD : (h + 1) * HEAD]
             if part == 2:
                 block = jnp.dot(block, turn, preferred_element_type=F32)
-            block = jnp.concatenate([block.astype(F32), jnp.zeros((16, HEAD), F32)], axis=0)
-            for r, (start, length) in enumerate(zip(STARTS, LENGTHS)):
-                piece = jnp.where(row < length, block[start : start + SLOT], 0.0)
-                if part == 0:
-                    piece = jnp.where(row == ID_ROW, id_rows[r], piece)
-                elif part == 1:
-                    piece = jnp.where(row == ID_ROW, every, piece)
-                out_ref[PARTS * h + r, part * SLOT : (part + 1) * SLOT, :] = piece.astype(BF16)
-    out_ref[PARTS * HEADS_HERE] = jnp.zeros((3 * SLOT, HEAD), BF16)
+            blocks.append(jnp.concatenate([block.astype(F32), jnp.zeros((16, HEAD), F32)], axis=0))
+        for r, (start, length) in enumerate(zip(STARTS, LENGTHS)):
+            query, key, value = [
+                jnp.where(row < length, block[start : start + SLOT], 0.0) for block in blocks
+            ]
+            query = jnp.where(row == ID_ROW, id_rows[r], query)
+            query = jnp.where(row == ID_ROW + 1, every, query)
+            slot = jnp.concatenate([query, key[:ROWS], value[:ROWS]], axis=0)
+            out_ref[PARTS * h + r] = slot.astype(BF16)
+    out_ref[PARTS * HEADS_HERE] = jnp.zeros((SLOT + 2 * ROWS, HEAD), BF16)
 
 
 def attend(third_ref, q_ref, kv0_ref, kv1_ref, kv2_ref, kcode_ref, out_ref):
@@ -80,12 +83,13 @@
     third = third_ref[0]
     order = [third, lax.rem(third + 2, PARTS), lax.rem(third + 1, PARTS)]
     key_codes = [kcode_ref[pl.ds(j, 1), :] for j in order]
-    keys = [ref[:, :SLOT, :].reshape(rows, HEAD) for ref in (kv0_ref, kv1_ref, kv2_ref)]
+    parts = [ref[...].astype(F32) for ref in (kv0_ref, kv1_ref, kv2_ref)]
+    keys = [part[:, :SLOT].astype(BF16).reshape(rows, HEAD) for part in parts]
     ones = jnp.ones((rows, HEAD), BF16)
-    vals = [
-        jnp.concatenate([ref[:, SLOT:, :].reshape(rows, HEAD), ones], axis=1)
-        for ref in (kv0_ref, kv1_ref, kv2_ref)
-    ]
+    vals = []
+    for part in parts:
+        turned = [pltpu.roll(part[z, 2 * ROWS - SLOT :], ROWS, 0) for z in range(Z)]
+        vals.append(jnp.concatenate([jnp.concatenate(turned, axis=0).astype(BF16), ones], axis=1))
     tile = 16
     at = ID_ROW % tile
     ids = jnp.concatenate(
@@ -256,7 +260,7 @@
     send, granules = vmem_call(
         scatter_heads,
         56,
-        [(Z, 3 * SLOT, HEAD), (X + 1, GRANULE, width)],
+        [(Z, SLOT + 2 * ROWS, HEAD), (X + 1, GRANULE, width)],
         queries,
         keys_in,
         values,
@@ -275,7 +279,7 @@
     query = lax.all_to_all(query, "x", 0, 0, tiled=True)
 
     home = (X * jnp.arange(Z, dtype=jnp.int32) + side) * TOK
-    key_code = kv[:, ID_ROW, :].astype(F32) * POSITIONS + (
+    key_code = here[:, ID_ROW + 1, :].astype(F32) * POSITIONS + (
         home[:, None] + jnp.arange(HEAD, dtype=jnp.int32)[None, :]
     ).astype(F32)
     key_code = jnp.stack(

time: 175 us -> 172 us (0.983)
  waiting for transfers between devices: 33.3 us -> 26.5 us
  blocking collectives: 54.8 us -> 58.6 us
    ppermute x2, waiting for transfers between devices: 17.2 us -> 10.9 us  [local(): kv_others = [lax.ppermute(kv, 'z', turn) for turn in turns]]
    all_to_all x1, blocking collectives: 30.3 us -> 33.8 us  [local(): joined = lax.all_to_all(joined, 'z', 0, 0, tiled=True)]
where the time goes in v10:
time: 172 us; the launch traced here: 171 us
  blocking collectives  58.6 us (34%)
  starting transfers between devices  47.5 us (28%)
  waiting for transfers between devices  26.5 us (15%)
  Pallas kernels  16.3 us (9%)
  between operations  13.6 us (8%)
  local copies, waits for them, and re-layouts  7.49 us (4%)
    all_to_all x1, blocking collectives, local(): joined = lax.all_to_all(joined, 'z', 0, 0, tiled=True)  33.8 us
    pallas_call x6, Pallas kernels, vmem_call(): pl.pallas_call(body, out_shape=[jax.ShapeDtypeStruct(shape, kind) for sha...  16.3 us
    all_to_all x1, starting transfers between devices, local(): here = lax.all_to_all(send, 'z', 0, 0, tiled=True)  15.7 us
    all_to_all x1, blocking collectives, local(): part = lax.all_to_all(part, 'x', 0, 0, tiled=True)  12.5 us
    all_to_all x1, blocking collectives, local(): packed = lax.all_to_all(packed, 'y', 0, 0, tiled=True)  12.3 us
    ppermute x2, waiting for transfers between devices, local(): kv_others = [lax.ppermute(kv, 'z', turn) for turn in turns]  10.9 us
    ppermute x3, starting transfers between devices, share_rows(): lax.ppermute(block, 'x', [(x, (x + away) % X) for x in range(X)])  9.93 us
    all_to_all x1, waiting for transfers between devices, local(): here = lax.all_to_all(send, 'z', 0, 0, tiled=True)  8.99 us
  transfers between devices with their start and end apart: 10, of which 4 were waited for; matrix products, arithmetic and copies ran while one was open for 3% of the time, Pallas kernels for 7%

profile of v10, /device:TPU:1, one launch (start us, length us, event | category | flops | bytes accessed | tf_op | source)
XLA Modules:
  0.0 170.9 jit_solution(6708858998409157608)
XLA Ops:
  6.5 2.2 %shard_map.55 = (bf16[16,136,128]{2,1,0:T(8,128)(2,1)}, bf16[5,16,640]{2,1,0:T(8,128)(2,1)}) custom-call(bf16[128,640]{1,0:T(8,128)(2,1)} %q_ref.1, bf16[128,640]{1,0:T(8,128)(2,1)} %k_ref.1, bf16[128,640]{1,0:T(8,128)(2,1)} %v_ref.1, s32[1,128]{1,0:T(1,128)} %bitcast.24, bf16[80,640]{1,0:T(8,128)(2,1)} %weight_ref.1), custom_call_target="tpu_custom_call" | custom-call | tf_op jit(solution)/shard_map/pallas_call | solution.py:38
  8.7 15.7 %all-to-all-start = ((bf16[16,136,128]{2,1,0:T(8,128)(2,1)}), bf16[16,136,128]{2,1,0:T(8,128)(2,1)S(1)}, u32[]{:S(2)}, u32[]{:S(2)}) async-start(bf16[16,136,128]{2,1,0:T(8,128)(2,1)} %get-tuple-element.9), calls=%async_computation | async-start | bytes 1114112 | tf_op jit(solution)/shard_map/all_to_all | solution.py:270
  24.5 0.8 slice_bitcast_fusion.1
  25.4 3.1 %collective-permute-start.4 = (bf16[32,640]{1,0:T(8,128)(2,1)S(1)}, bf16[32,640]{1,0:T(8,128)(2,1)S(1)}, u32[]{:S(2)}, u32[]{:S(2)}) collective-permute-start(bf16[32,640]{1,0:T(8,128)(2,1)S(1)} %pad_maximum_fusion.1), channel_id=1, source_target_pairs={{0,8},{8,16},{16,24},{24,0},{1,9},{9,17},{17,25},{25,1},{2,10},{10... | collective-permute-start | bytes 122888 | tf_op jit(solution)/shard_map/ppermute | solution.py:251
  28.5 3.4 %collective-permute-start.5 = (bf16[32,640]{1,0:T(8,128)(2,1)S(1)}, bf16[32,640]{1,0:T(8,128)(2,1)S(1)}, u32[]{:S(2)}, u32[]{:S(2)}) collective-permute-start(bf16[32,640]{1,0:T(8,128)(2,1)S(1)} %pad_maximum_fusion.1), channel_id=1, source_target_pairs={{0,24},{8,0},{16,8},{24,16},{1,25},{9,1},{17,9},{25,17},{2,26},{10... | collective-permute-start | bytes 122888 | tf_op jit(solution)/shard_map/ppermute | solution.py:251
  31.9 3.4 %collective-permute-start.3 = (bf16[48,640]{1,0:T(8,128)(2,1)S(1)}, bf16[48,640]{1,0:T(8,128)(2,1)S(1)}, u32[]{:S(2)}, u32[]{:S(2)}) collective-permute-start(bf16[48,640]{1,0:T(8,128)(2,1)S(1)} %pad_maximum_fusion), channel_id=1, source_target_pairs={{0,16},{8,24},{16,0},{24,8},{1,17},{9,25},{17,1},{25,9},{2,18},{10... | collective-permute-start | bytes 184328 | tf_op jit(solution)/shard_map/ppermute | solution.py:251
  35.3 0.7 constant_dynamic-update-slice_fusion.5
  36.1 0.7 constant_dynamic-update-slice_fusion.4
  36.8 0.7 constant_dynamic-update-slice_fusion.3
  37.5 1.1 collective-permute-done.3
  38.7 0.7 copy-done.2
  39.4 9.0 %all-to-all-done = bf16[16,136,128]{2,1,0:T(8,128)(2,1)S(1)} async-done(((bf16[16,136,128]{2,1,0:T(8,128)(2,1)}), bf16[16,136,128]{2,1,0:T(8,128)(2,1)S(1)}, u32[]{:S(2)}, u32[]{:S(2)}) %all-to-all-start) | async-done | bytes 557088 | tf_op jit(solution)/shard_map/all_to_all | solution.py:270
  48.4 5.0 %collective-permute-start = (bf16[16,88,128]{2,1,0:T(8,128)(2,1)S(1)}, bf16[16,88,128]{2,1,0:T(8,128)(2,1)S(1)}, u32[]{:S(2)}, u32[]{:S(2)}) collective-permute-start(bf16[16,88,128]{2,1,0:T(8,128)(2,1)S(1)} %slice.46.kv0_ref), channel_id=1, source_target_pairs={{0,32},{32,64},{64,0},{96,128},{128,160},{160,96},{192,224},{224,2... | collective-permute-start | bytes 1081352 | tf_op jit(solution)/shard_map/ppermute | solution.py:277
  53.5 1.9 %collective-permute-start.1 = (bf16[16,88,128]{2,1,0:T(8,128)(2,1)S(1)}, bf16[16,88,128]{2,1,0:T(8,128)(2,1)S(1)}, u32[]{:S(2)}, u32[]{:S(2)}) collective-permute-start(bf16[16,88,128]{2,1,0:T(8,128)(2,1)S(1)} %slice.46.kv0_ref), channel_id=1, source_target_pairs={{0,64},{32,0},{64,32},{96,160},{128,96},{160,128},{192,256},{224,1... | collective-permute-start | bytes 1081352 | tf_op jit(solution)/shard_map/ppermute | solution.py:277
  55.4 1.0 broadcast_in_dim.10
  56.4 4.0 %all-to-all-start.1 = ((bf16[4,768,128]{2,1,0:T(8,128)(2,1)}), bf16[4,768,128]{2,1,0:T(8,128)(2,1)S(1)}, u32[]{:S(2)}, u32[]{:S(2)}) async-start(bf16[4,768,128]{2,1,0:T(8,128)(2,1)} %broadcast_in_dim.10), calls=%async_computation.1 | async-start | bytes 1572864 | tf_op jit(solution)/shard_map/all_to_all | solution.py:279
  60.7 0.1 stack_reshape.11
  61.0 10.9 %collective-permute-done.1.kv2_ref = bf16[16,88,128]{2,1,0:T(8,128)(2,1)S(1)} collective-permute-done((bf16[16,88,128]{2,1,0:T(8,128)(2,1)S(1)}, bf16[16,88,128]{2,1,0:T(8,128)(2,1)S(1)}, u32[]{:S(2)}, u32[]{:S(2)}) %collective-permute-start.1) | collective-permute-done | bytes 360480 | tf_op jit(solution)/shard_map/ppermute | solution.py:277
  71.9 10.3 %shard_map.56 = bf16[4,816,128]{2,1,0:T(8,128)(2,1)S(1)} custom-call(s32[1]{0:T(128)} %bitcast.2.third_ref, bf16[4,768,128]{2,1,0:T(8,128)(2,1)S(1)} %all-to-all-done.1.q_ref, bf16[16,88,128]{2,1,0:T(8,128)(2,1)S(1)} %slice.46.kv0_ref, bf16[16,88,128]{2,1,0:T(8,128)(2,1)S(1)} %collective-permute-done.kv1_ref, ...), custom_call_target="tpu_custom_call" | custom-call | flops 68719476736 | bytes 4194304 | tf_op jit(solution)/shard_map/pallas_call | solution.py:38
  82.2 12.5 %all_to_all.25.part_ref = bf16[4,816,128]{2,1,0:T(8,128)(2,1)S(1)} all-to-all(bf16[4,816,128]{2,1,0:T(8,128)(2,1)S(1)} %shard_map.56), channel_id=1, replica_groups=mesh['z'=16,'x'=4,'y'=4,'c'=2] {'x'}, dimensions={0} | all-to-all | bytes 1671168 | tf_op jit(solution)/shard_map/all_to_all | solution.py:305
  94.7 0.6 shard_map.57
  95.4 33.8 %all_to_all.26.part_ref = bf16[16,48,128]{2,1,0:T(8,128)(2,1)S(1)} all-to-all(bf16[16,48,128]{2,1,0:T(8,128)(2,1)S(1)} %shard_map.57), channel_id=1, replica_groups=mesh['z'=16,'x'=4,'y'=4,'c'=2] {'z'}, dimensions={0} | all-to-all | bytes 393216 | tf_op jit(solution)/shard_map/all_to_all | solution.py:307
  129.2 0.1 shard_map.58
  129.3 12.3 %all_to_all.27.packed_ref = bf16[4,720,128]{2,1,0:T(8,128)(2,1)S(1)} all-to-all(bf16[4,720,128]{2,1,0:T(8,128)(2,1)S(1)} %shard_map.58), channel_id=1, replica_groups=mesh['z'=16,'x'=4,'y'=4,'c'=2] {'y'}, dimensions={0} | all-to-all | bytes 1474560 | tf_op jit(solution)/shard_map/all_to_all | solution.py:309
  141.6 8.6 %collective-permute-start.2 = (bf16[4,720,128]{2,1,0:T(8,128)(2,1)S(1)}, bf16[4,720,128]{2,1,0:T(8,128)(2,1)S(1)}, u32[]{:S(2)}, u32[]{:S(2)}) collective-permute-start(bf16[4,720,128]{2,1,0:T(8,128)(2,1)S(1)} %all_to_all.27.packed_ref), channel_id=1, source_target_pairs={{0,1},{1,0},{2,3},{3,2},{4,5},{5,4},{6,7},{7,6},{8,9},{9,8},{10,11... | collective-permute-start | bytes 2211848 | tf_op jit(solution)/shard_map/ppermute | solution.py:310
  150.3 1.9 %copy-done = bf16[2560,640]{1,0:T(8,128)(2,1)S(1)} copy-done((bf16[2560,640]{1,0:T(8,128)(2,1)S(1)}, bf16[2560,640]{1,0:T(8,128)(2,1)}, u32[]{:S(2)}) %copy-start) | copy-done | bytes 3276824
  152.2 1.5 shard_map.59.sum_ref
  153.7 0.4 copy-done.1
  154.1 1.5 shard_map.60
  155.7 2.2 %collective-permute-start.6 = (bf16[128,640]{1,0:T(8,128)(2,1)S(1)}, bf16[128,640]{1,0:T(8,128)(2,1)S(1)}, u32[]{:S(2)}, u32[]{:S(2)}) collective-permute-start(bf16[128,640]{1,0:T(8,128)(2,1)S(1)} %get-tuple-element.12), channel_id=1, source_target_pairs={{0,8},{8,0},{16,24},{24,16},{1,9},{9,1},{17,25},{25,17},{2,10},{10... | collective-permute-start | bytes 491528 | tf_op jit(solution)/shard_map/ppermute | solution.py:332
  157.9 5.5 %collective-permute-done.6 = bf16[128,640]{1,0:T(8,128)(2,1)S(1)} collective-permute-done((bf16[128,640]{1,0:T(8,128)(2,1)S(1)}, bf16[128,640]{1,0:T(8,128)(2,1)S(1)}, u32[]{:S(2)}, u32[]{:S(2)}) %collective-permute-start.6) | collective-permute-done | bytes 163872 | tf_op jit(solution)/shard_map/ppermute | solution.py:332
  163.4 0.7 add_convert_fusion
  (32 shorter events, 0.7 us)
Async XLA Ops:
  6.5 54.3 %copy-start.3 = (pred[48]{0:T(512)(128)(4,1)S(1)}, pred[48]{0:T(512)(128)(4,1)}, u32[]{:S(2)}) copy-start(pred[48]{0:T(512)(128)(4,1)} %constant.22.clone.1) | copy-start | bytes 148
  8.7 39.7 %all-to-all-start = ((bf16[16,136,128]{2,1,0:T(8,128)(2,1)}), bf16[16,136,128]{2,1,0:T(8,128)(2,1)S(1)}, u32[]{:S(2)}, u32[]{:S(2)}) async-start(bf16[16,136,128]{2,1,0:T(8,128)(2,1)} %get-tuple-element.9), calls=%async_computation | async-start | bytes 1114112 | tf_op jit(solution)/shard_map/all_to_all | solution.py:270
  24.5 125.8 %all-gather.2.cloned.1.call-start = ((), (), s32[]{:S(2)}) async-start(), calls=%async_computation.5 | async-start | bytes 3481600 | tf_op jit(solution)/shard_map/all_gather | solution.py:271
  25.4 13.3 %collective-permute-start.4 = (bf16[32,640]{1,0:T(8,128)(2,1)S(1)}, bf16[32,640]{1,0:T(8,128)(2,1)S(1)}, u32[]{:S(2)}, u32[]{:S(2)}) collective-permute-start(bf16[32,640]{1,0:T(8,128)(2,1)S(1)} %pad_maximum_fusion.1), channel_id=1, source_target_pairs={{0,8},{8,16},{16,24},{24,0},{1,9},{9,17},{17,25},{25,1},{2,10},{10... | collective-permute-start | bytes 122888 | tf_op jit(solution)/shard_map/ppermute | solution.py:251
  28.5 10.2 %collective-permute-start.5 = (bf16[32,640]{1,0:T(8,128)(2,1)S(1)}, bf16[32,640]{1,0:T(8,128)(2,1)S(1)}, u32[]{:S(2)}, u32[]{:S(2)}) collective-permute-start(bf16[32,640]{1,0:T(8,128)(2,1)S(1)} %pad_maximum_fusion.1), channel_id=1, source_target_pairs={{0,24},{8,0},{16,8},{24,16},{1,25},{9,1},{17,9},{25,17},{2,26},{10... | collective-permute-start | bytes 122888 | tf_op jit(solution)/shard_map/ppermute | solution.py:251
  31.9 6.8 %collective-permute-start.3 = (bf16[48,640]{1,0:T(8,128)(2,1)S(1)}, bf16[48,640]{1,0:T(8,128)(2,1)S(1)}, u32[]{:S(2)}, u32[]{:S(2)}) collective-permute-start(bf16[48,640]{1,0:T(8,128)(2,1)S(1)} %pad_maximum_fusion), channel_id=1, source_target_pairs={{0,16},{8,24},{16,0},{24,8},{1,17},{9,25},{17,1},{25,9},{2,18},{10... | collective-permute-start | bytes 184328 | tf_op jit(solution)/shard_map/ppermute | solution.py:251
  38.7 0.7 copy-start.2
  48.4 12.5 %collective-permute-start = (bf16[16,88,128]{2,1,0:T(8,128)(2,1)S(1)}, bf16[16,88,128]{2,1,0:T(8,128)(2,1)S(1)}, u32[]{:S(2)}, u32[]{:S(2)}) collective-permute-start(bf16[16,88,128]{2,1,0:T(8,128)(2,1)S(1)} %slice.46.kv0_ref), channel_id=1, source_target_pairs={{0,32},{32,64},{64,0},{96,128},{128,160},{160,96},{192,224},{224,2... | collective-permute-start | bytes 1081352 | tf_op jit(solution)/shard_map/ppermute | solution.py:277
  53.5 18.4 %collective-permute-start.1 = (bf16[16,88,128]{2,1,0:T(8,128)(2,1)S(1)}, bf16[16,88,128]{2,1,0:T(8,128)(2,1)S(1)}, u32[]{:S(2)}, u32[]{:S(2)}) collective-permute-start(bf16[16,88,128]{2,1,0:T(8,128)(2,1)S(1)} %slice.46.kv0_ref), channel_id=1, source_target_pairs={{0,64},{32,0},{64,32},{96,160},{128,96},{160,128},{192,256},{224,1... | collective-permute-start | bytes 1081352 | tf_op jit(solution)/shard_map/ppermute | solution.py:277
  56.4 15.4 %all-to-all-start.1 = ((bf16[4,768,128]{2,1,0:T(8,128)(2,1)}), bf16[4,768,128]{2,1,0:T(8,128)(2,1)S(1)}, u32[]{:S(2)}, u32[]{:S(2)}) async-start(bf16[4,768,128]{2,1,0:T(8,128)(2,1)} %broadcast_in_dim.10), calls=%async_computation.1 | async-start | bytes 1572864 | tf_op jit(solution)/shard_map/all_to_all | solution.py:279
  141.6 12.1 %collective-permute-start.2 = (bf16[4,720,128]{2,1,0:T(8,128)(2,1)S(1)}, bf16[4,720,128]{2,1,0:T(8,128)(2,1)S(1)}, u32[]{:S(2)}, u32[]{:S(2)}) collective-permute-start(bf16[4,720,128]{2,1,0:T(8,128)(2,1)S(1)} %all_to_all.27.packed_ref), channel_id=1, source_target_pairs={{0,1},{1,0},{2,3},{3,2},{4,5},{5,4},{6,7},{7,6},{8,9},{9,8},{10,11... | collective-permute-start | bytes 2211848 | tf_op jit(solution)/shard_map/ppermute | solution.py:310
  150.3 1.9 %copy-start = (bf16[2560,640]{1,0:T(8,128)(2,1)S(1)}, bf16[2560,640]{1,0:T(8,128)(2,1)}, u32[]{:S(2)}) copy-start(bf16[2560,640]{1,0:T(8,128)(2,1)} %all-gather.2.cloned.1.call-done.weight_ref) | copy-start | bytes 9830404
  152.2 1.9 %copy-start.1 = (bf16[2560,640]{1,0:T(8,128)(2,1)S(1)}, bf16[2560,640]{1,0:T(8,128)(2,1)}, u32[]{:S(2)}) copy-start(bf16[2560,640]{1,0:T(8,128)(2,1)} %all-gather.2.cloned.1.call-done.weight_ref) | copy-start | bytes 9830404
  155.7 7.7 %collective-permute-start.6 = (bf16[128,640]{1,0:T(8,128)(2,1)S(1)}, bf16[128,640]{1,0:T(8,128)(2,1)S(1)}, u32[]{:S(2)}, u32[]{:S(2)}) collective-permute-start(bf16[128,640]{1,0:T(8,128)(2,1)S(1)} %get-tuple-element.12), channel_id=1, source_target_pairs={{0,8},{8,0},{16,24},{24,16},{1,9},{9,1},{17,25},{25,17},{2,10},{10... | collective-permute-start | bytes 491528 | tf_op jit(solution)/shard_map/ppermute | solution.py:332
Sparse Core Ops, SparseCore 0:
  39.5 78.8 all-gather.1

commit v11 on v10

--- a/solution.py
+++ b/solution.py
@@ -195,7 +195,8 @@
             out_ref[y, first : first + SLOT, :] = part_ref[PARTS * (HEADS_HERE - 1) + r]
 
 
-def multiply(core, side, packed_ref, weight_ref):
+def order_rows(place_ref, weight_ref, mine_ref, other_ref):
+    core, side = place_ref[0], place_ref[1]
     depth = weight_ref.shape[0] // Z
     member = lax.rem(side, PAIR)
     places = []
@@ -205,40 +206,46 @@
         away = lax.rem(holder + X - side, X)
         base = jnp.where(away == 0, 0, jnp.where(away == 1, 8, jnp.where(away == 2, 3, 6)))
         places.append((base + lax.div(n, 2)) * GRANULE)
+    per_head = SHARE // GRANULE
+    for which, out_ref in ((core, mine_ref), (1 - core, other_ref)):
+        for y in range(Y):
+            rows = []
+            for n in range(HEADS_HERE * per_head):
+                first = ((C * y + which) * 2 + n // len(places)) * depth + places[n % len(places)]
+                rows.append(weight_ref[pl.ds(pl.multiple_of(first, GRANULE), GRANULE), :])
+            rows += rows[4 * per_head :]
+            for n, row in enumerate(rows):
+                first = (y * len(rows) + n) * GRANULE
+                out_ref[first : first + GRANULE, :] = row
+
+
+def multiply(packed_ref, weight_ref):
     span = PARTS * SLOT
     halves = lax.broadcasted_iota(jnp.int32, (span, HEAD), 1) < SHARE
-    per_head = SHARE // GRANULE
     inputs = [[] for _ in range(PAIR)]
-    weights = []
     for y in range(Y):
         fifth = packed_ref[y, 2 * PAIR * span :, :].astype(F32)
         for x in range(PAIR):
             inputs[x] += [packed_ref[y, (2 * x + two) * span : (2 * x + two + 1) * span, :] for two in range(2)]
             inputs[x].append(jnp.where(halves == (x == 0), fifth, 0.0).astype(BF16))
-        rows = []
-        for n in range(HEADS_HERE * per_head):
-            first = ((C * y + core) * 2 + n // len(places)) * depth + places[n % len(places)]
-            rows.append(weight_ref[pl.ds(pl.multiple_of(first, GRANULE), GRANULE), :])
-        weights += rows + rows[4 * per_head :]
-    weights = jnp.concatenate(weights, axis=0)
+    weights = weight_ref[...]
     return [
         jnp.dot(jnp.concatenate(blocks, axis=1), weights, preferred_element_type=F32) for blocks in inputs
     ]
 
 
-def project_mine(place_ref, packed_ref, weight_ref, sum_ref):
-    for x, total in enumerate(multiply(place_ref[0], place_ref[1], packed_ref, weight_ref)):
+def project_mine(packed_ref, weight_ref, sum_ref):
+    for x, total in enumerate(multiply(packed_ref, weight_ref)):
         sum_ref[x] = total
 
 
 def project_other(place_ref, packed_ref, weight_ref, sum_ref, own_ref, send_ref):
-    side = place_ref[1]
     totals = []
-    for x, total in enumerate(multiply(1 - place_ref[0], side, packed_ref, weight_ref)):
+    for x, total in enumerate(multiply(packed_ref, weight_ref)):
         total = total + sum_ref[x]
         total = [total[r * SLOT : r * SLOT + length] for r, length in enumerate(LENGTHS)]
         totals.append(jnp.concatenate(total, axis=0))
-    first = lax.rem(side, PAIR) == 0
+    first = lax.rem(place_ref[1], PAIR) == 0
     own_ref[...] = jnp.where(first, totals[0], totals[1])
     send_ref[...] = jnp.where(first, totals[1], totals[0]).astype(BF16)
 
@@ -307,15 +314,24 @@
     joined = lax.all_to_all(joined, "z", 0, 0, tiled=True)
     (packed,) = vmem_call(assemble, 8, [(Y, (2 * PAIR + 1) * PARTS * SLOT, HEAD)], joined)
     packed = lax.all_to_all(packed, "y", 0, 0, tiled=True)
+    place = jnp.stack([core, side])
+    depth = Y * (HEADS_HERE + 1) * SHARE
+    weight_mine, weight_other = vmem_call(
+        order_rows,
+        12,
+        [(depth, width), (depth, width)],
+        weight,
+        scalars=place,
+        cost=pl.CostEstimate(flops=0, bytes_accessed=1 << 24, transcendentals=0),
+    )
+    packed, weight_other = lax.optimization_barrier((packed, weight_other))
     others = lax.ppermute(packed, "c", [(0, 1), (1, 0)])
-    place = jnp.stack([core, side])
     (sums,) = vmem_call(
         project_mine,
         16,
         [(PAIR, PARTS * SLOT, width)],
         packed,
-        weight,
-        scalars=place,
+        weight_mine,
         kinds=[F32],
         cost=pl.CostEstimate(flops=1 << 31, bytes_accessed=1 << 23, transcendentals=0),
     )
@@ -324,7 +340,7 @@
         16,
         [(TOK, width), (TOK, width)],
         others,
-        weight,
+        weight_other,
         sums,
         scalars=place,
         kinds=[F32, BF16],

time: 172 us -> 171 us (level)
  blocking collectives: 58.6 us -> 46.1 us
  starting transfers between devices: 47.5 us -> 52.3 us
  waiting for transfers between devices: 26.5 us -> 30 us
  local copies, waits for them, and re-layouts: 7.49 us -> 9.9 us
    all_to_all x1 -> x0, blocking collectives: 12.3 us -> none  [local(): packed = lax.all_to_all(packed, 'y', 0, 0, tiled=True)]
    all_to_all x0 -> x1, starting transfers between devices: none -> 4.36 us  [local(): packed = lax.all_to_all(packed, 'y', 0, 0, tiled=True)]
    all_to_all x0 -> x1, waiting for transfers between devices: none -> 3.84 us  [local(): packed = lax.all_to_all(packed, 'y', 0, 0, tiled=True)]
    unnamed x13 -> x15, local copies, waits for them, and re-layouts: 5.23 us -> 7.64 us
    pallas_call x6 -> x7, Pallas kernels: 16.3 us -> 17.3 us  [vmem_call(): pl.pallas_call(body, out_shape=[jax.ShapeDtypeStruct(shape, kind) for sha...]
  transfers between devices with their start and end apart: 10 -> 11, of which waited for: 4 -> 5; matrix products, arithmetic and copies ran while one was open for 3% -> 3% of each run, Pallas kernels for 7% -> 8%
where the time goes in v11:
time: 171 us; the launch traced here: 170 us
  starting transfers between devices  52.3 us (31%)
  blocking collectives  46.1 us (27%)
  waiting for transfers between devices  30 us (18%)
  Pallas kernels  17.3 us (10%)
  between operations  13.7 us (8%)
  local copies, waits for them, and re-layouts  9.9 us (6%)
    all_to_all x1, blocking collectives, local(): joined = lax.all_to_all(joined, 'z', 0, 0, tiled=True)  33.5 us
    pallas_call x7, Pallas kernels, vmem_call(): pl.pallas_call(body, out_shape=[jax.ShapeDtypeStruct(shape, kind) for sha...  17.3 us
    all_to_all x1, starting transfers between devices, local(): here = lax.all_to_all(send, 'z', 0, 0, tiled=True)  15.7 us
    all_to_all x1, blocking collectives, local(): part = lax.all_to_all(part, 'x', 0, 0, tiled=True)  12.6 us
    ppermute x2, waiting for transfers between devices, local(): kv_others = [lax.ppermute(kv, 'z', turn) for turn in turns]  10.9 us
    ppermute x3, starting transfers between devices, share_rows(): lax.ppermute(block, 'x', [(x, (x + away) % X) for x in range(X)])  9.93 us
    all_to_all x1, waiting for transfers between devices, local(): here = lax.all_to_all(send, 'z', 0, 0, tiled=True)  8.99 us
    ppermute x1, starting transfers between devices, local(): others = lax.ppermute(packed, 'c', [(0, 1), (1, 0)])  8.72 us
  transfers between devices with their start and end apart: 11, of which 5 were waited for; matrix products, arithmetic and copies ran while one was open for 3% of the time, Pallas kernels for 8%

profile of v11, /device:TPU:1, one launch (start us, length us, event | category | flops | bytes accessed | tf_op | source)
XLA Modules:
  0.0 170.2 jit_solution(6102631855710727378)
XLA Ops:
  6.5 2.2 %shard_map.55 = (bf16[16,136,128]{2,1,0:T(8,128)(2,1)}, bf16[5,16,640]{2,1,0:T(8,128)(2,1)}) custom-call(bf16[128,640]{1,0:T(8,128)(2,1)} %q_ref.1, bf16[128,640]{1,0:T(8,128)(2,1)} %k_ref.1, bf16[128,640]{1,0:T(8,128)(2,1)} %v_ref.1, s32[1,128]{1,0:T(1,128)} %bitcast.24, bf16[80,640]{1,0:T(8,128)(2,1)} %weight_ref.1), custom_call_target="tpu_custom_call" | custom-call | tf_op jit(solution)/shard_map/pallas_call | solution.py:38
  8.7 15.7 %all-to-all-start = ((bf16[16,136,128]{2,1,0:T(8,128)(2,1)}), bf16[16,136,128]{2,1,0:T(8,128)(2,1)S(1)}, u32[]{:S(2)}, u32[]{:S(2)}) async-start(bf16[16,136,128]{2,1,0:T(8,128)(2,1)} %get-tuple-element.13), calls=%async_computation | async-start | bytes 1114112 | tf_op jit(solution)/shard_map/all_to_all | solution.py:277
  24.5 0.8 slice_bitcast_fusion.1
  25.3 3.1 %collective-permute-start.3 = (bf16[32,640]{1,0:T(8,128)(2,1)S(1)}, bf16[32,640]{1,0:T(8,128)(2,1)S(1)}, u32[]{:S(2)}, u32[]{:S(2)}) collective-permute-start(bf16[32,640]{1,0:T(8,128)(2,1)S(1)} %pad_maximum_fusion.1), channel_id=1, source_target_pairs={{0,8},{8,16},{16,24},{24,0},{1,9},{9,17},{17,25},{25,1},{2,10},{10... | collective-permute-start | bytes 122888 | tf_op jit(solution)/shard_map/ppermute | solution.py:258
  28.5 3.4 %collective-permute-start.4 = (bf16[32,640]{1,0:T(8,128)(2,1)S(1)}, bf16[32,640]{1,0:T(8,128)(2,1)S(1)}, u32[]{:S(2)}, u32[]{:S(2)}) collective-permute-start(bf16[32,640]{1,0:T(8,128)(2,1)S(1)} %pad_maximum_fusion.1), channel_id=1, source_target_pairs={{0,24},{8,0},{16,8},{24,16},{1,25},{9,1},{17,9},{25,17},{2,26},{10... | collective-permute-start | bytes 122888 | tf_op jit(solution)/shard_map/ppermute | solution.py:258
  31.9 3.4 %collective-permute-start.2 = (bf16[48,640]{1,0:T(8,128)(2,1)S(1)}, bf16[48,640]{1,0:T(8,128)(2,1)S(1)}, u32[]{:S(2)}, u32[]{:S(2)}) collective-permute-start(bf16[48,640]{1,0:T(8,128)(2,1)S(1)} %pad_maximum_fusion), channel_id=1, source_target_pairs={{0,16},{8,24},{16,0},{24,8},{1,17},{9,25},{17,1},{25,9},{2,18},{10... | collective-permute-start | bytes 184328 | tf_op jit(solution)/shard_map/ppermute | solution.py:258
  35.3 0.7 constant_dynamic-update-slice_fusion.5
  36.0 0.7 constant_dynamic-update-slice_fusion.4
  36.8 0.7 constant_dynamic-update-slice_fusion.3
  37.5 1.1 collective-permute-done.2
  39.4 9.0 %all-to-all-done = bf16[16,136,128]{2,1,0:T(8,128)(2,1)S(1)} async-done(((bf16[16,136,128]{2,1,0:T(8,128)(2,1)}), bf16[16,136,128]{2,1,0:T(8,128)(2,1)S(1)}, u32[]{:S(2)}, u32[]{:S(2)}) %all-to-all-start) | async-done | bytes 557088 | tf_op jit(solution)/shard_map/all_to_all | solution.py:277
  48.4 5.0 %collective-permute-start = (bf16[16,88,128]{2,1,0:T(8,128)(2,1)S(1)}, bf16[16,88,128]{2,1,0:T(8,128)(2,1)S(1)}, u32[]{:S(2)}, u32[]{:S(2)}) collective-permute-start(bf16[16,88,128]{2,1,0:T(8,128)(2,1)S(1)} %slice.46.kv0_ref), channel_id=1, source_target_pairs={{0,32},{32,64},{64,0},{96,128},{128,160},{160,96},{192,224},{224,2... | collective-permute-start | bytes 1081352 | tf_op jit(solution)/shard_map/ppermute | solution.py:284
  53.4 1.9 %collective-permute-start.1 = (bf16[16,88,128]{2,1,0:T(8,128)(2,1)S(1)}, bf16[16,88,128]{2,1,0:T(8,128)(2,1)S(1)}, u32[]{:S(2)}, u32[]{:S(2)}) collective-permute-start(bf16[16,88,128]{2,1,0:T(8,128)(2,1)S(1)} %slice.46.kv0_ref), channel_id=1, source_target_pairs={{0,64},{32,0},{64,32},{96,160},{128,96},{160,128},{192,256},{224,1... | collective-permute-start | bytes 1081352 | tf_op jit(solution)/shard_map/ppermute | solution.py:284
  55.4 1.0 broadcast_in_dim.10
  56.4 4.0 %all-to-all-start.1 = ((bf16[4,768,128]{2,1,0:T(8,128)(2,1)}), bf16[4,768,128]{2,1,0:T(8,128)(2,1)S(1)}, u32[]{:S(2)}, u32[]{:S(2)}) async-start(bf16[4,768,128]{2,1,0:T(8,128)(2,1)} %broadcast_in_dim.10), calls=%async_computation.1 | async-start | bytes 1572864 | tf_op jit(solution)/shard_map/all_to_all | solution.py:286
  61.0 10.9 %collective-permute-done.1.kv2_ref = bf16[16,88,128]{2,1,0:T(8,128)(2,1)S(1)} collective-permute-done((bf16[16,88,128]{2,1,0:T(8,128)(2,1)S(1)}, bf16[16,88,128]{2,1,0:T(8,128)(2,1)S(1)}, u32[]{:S(2)}, u32[]{:S(2)}) %collective-permute-start.1) | collective-permute-done | bytes 360480 | tf_op jit(solution)/shard_map/ppermute | solution.py:284
  71.9 10.3 %shard_map.56 = bf16[4,816,128]{2,1,0:T(8,128)(2,1)S(1)} custom-call(s32[1]{0:T(128)} %bitcast.2.third_ref, bf16[4,768,128]{2,1,0:T(8,128)(2,1)S(1)} %all-to-all-done.1.q_ref, bf16[16,88,128]{2,1,0:T(8,128)(2,1)S(1)} %slice.46.kv0_ref, bf16[16,88,128]{2,1,0:T(8,128)(2,1)S(1)} %collective-permute-done.kv1_ref, ...), custom_call_target="tpu_custom_call" | custom-call | flops 68719476736 | bytes 4194304 | tf_op jit(solution)/shard_map/pallas_call | solution.py:38
  82.2 12.6 %all_to_all.25.part_ref = bf16[4,816,128]{2,1,0:T(8,128)(2,1)S(1)} all-to-all(bf16[4,816,128]{2,1,0:T(8,128)(2,1)S(1)} %shard_map.56), channel_id=1, replica_groups=mesh['z'=16,'x'=4,'y'=4,'c'=2] {'x'}, dimensions={0} | all-to-all | bytes 1671168 | tf_op jit(solution)/shard_map/all_to_all | solution.py:312
  95.4 33.5 %all_to_all.26.part_ref = bf16[16,48,128]{2,1,0:T(8,128)(2,1)S(1)} all-to-all(bf16[16,48,128]{2,1,0:T(8,128)(2,1)S(1)} %shard_map.57), channel_id=1, replica_groups=mesh['z'=16,'x'=4,'y'=4,'c'=2] {'z'}, dimensions={0} | all-to-all | bytes 393216 | tf_op jit(solution)/shard_map/all_to_all | solution.py:314
  128.9 1.0 shard_map.58
  129.9 4.4 %all-to-all-start.4 = ((bf16[4,720,128]{2,1,0:T(8,128)(2,1)}), bf16[4,720,128]{2,1,0:T(8,128)(2,1)S(1)}, u32[]{:S(2)}, u32[]{:S(2)}) async-start(bf16[4,720,128]{2,1,0:T(8,128)(2,1)} %shard_map.58), calls=%async_computation.4 | async-start | bytes 1474560 | tf_op jit(solution)/shard_map/all_to_all | solution.py:316
  134.3 1.9 %copy-done = bf16[2560,640]{1,0:T(8,128)(2,1)S(1)} copy-done((bf16[2560,640]{1,0:T(8,128)(2,1)S(1)}, bf16[2560,640]{1,0:T(8,128)(2,1)}, u32[]{:S(2)}) %copy-start) | copy-done | bytes 3276824
  136.2 0.9 shard_map.59
  137.2 1.3 copy-done.1
  138.5 3.8 %all-to-all-done.4.packed_ref = bf16[4,720,128]{2,1,0:T(8,128)(2,1)S(1)} async-done(((bf16[4,720,128]{2,1,0:T(8,128)(2,1)}), bf16[4,720,128]{2,1,0:T(8,128)(2,1)S(1)}, u32[]{:S(2)}, u32[]{:S(2)}) %all-to-all-start.4) | async-done | bytes 737312 | tf_op jit(solution)/shard_map/all_to_all | solution.py:316
  142.3 8.7 %collective-permute-start.5 = (bf16[4,720,128]{2,1,0:T(8,128)(2,1)S(1)}, bf16[4,720,128]{2,1,0:T(8,128)(2,1)S(1)}, u32[]{:S(2)}, u32[]{:S(2)}) collective-permute-start(bf16[4,720,128]{2,1,0:T(8,128)(2,1)S(1)} %all-to-all-done.4.packed_ref), channel_id=1, source_target_pairs={{0,1},{1,0},{2,3},{3,2},{4,5},{5,4},{6,7},{7,6},{8,9},{9,8},{10,11... | collective-permute-start | bytes 2211848 | tf_op jit(solution)/shard_map/ppermute | solution.py:328
  151.0 1.5 copy-done.2
  152.6 0.9 shard_map.60.sum_ref
  153.5 1.4 shard_map.61
  154.9 2.5 %collective-permute-start.6 = (bf16[128,640]{1,0:T(8,128)(2,1)S(1)}, bf16[128,640]{1,0:T(8,128)(2,1)S(1)}, u32[]{:S(2)}, u32[]{:S(2)}) collective-permute-start(bf16[128,640]{1,0:T(8,128)(2,1)S(1)} %get-tuple-element.20), channel_id=1, source_target_pairs={{0,8},{8,0},{16,24},{24,16},{1,9},{9,1},{17,25},{25,17},{2,10},{10... | collective-permute-start | bytes 491528 | tf_op jit(solution)/shard_map/ppermute | solution.py:348
  157.4 5.2 %collective-permute-done.6 = bf16[128,640]{1,0:T(8,128)(2,1)S(1)} collective-permute-done((bf16[128,640]{1,0:T(8,128)(2,1)S(1)}, bf16[128,640]{1,0:T(8,128)(2,1)S(1)}, u32[]{:S(2)}, u32[]{:S(2)}) %collective-permute-start.6) | collective-permute-done | bytes 163872 | tf_op jit(solution)/shard_map/ppermute | solution.py:348
  162.6 0.7 add_convert_fusion
  (36 shorter events, 2.1 us)
Async XLA Ops:
  8.7 39.7 %all-to-all-start = ((bf16[16,136,128]{2,1,0:T(8,128)(2,1)}), bf16[16,136,128]{2,1,0:T(8,128)(2,1)S(1)}, u32[]{:S(2)}, u32[]{:S(2)}) async-start(bf16[16,136,128]{2,1,0:T(8,128)(2,1)} %get-tuple-element.13), calls=%async_computation | async-start | bytes 1114112 | tf_op jit(solution)/shard_map/all_to_all | solution.py:277
  24.5 109.9 %all-gather.2.cloned.1.call-start = ((), (), s32[]{:S(2)}) async-start(), calls=%async_computation.5 | async-start | bytes 3481600 | tf_op jit(solution)/shard_map/all_gather | solution.py:278
  25.3 13.3 %collective-permute-start.3 = (bf16[32,640]{1,0:T(8,128)(2,1)S(1)}, bf16[32,640]{1,0:T(8,128)(2,1)S(1)}, u32[]{:S(2)}, u32[]{:S(2)}) collective-permute-start(bf16[32,640]{1,0:T(8,128)(2,1)S(1)} %pad_maximum_fusion.1), channel_id=1, source_target_pairs={{0,8},{8,16},{16,24},{24,0},{1,9},{9,17},{17,25},{25,1},{2,10},{10... | collective-permute-start | bytes 122888 | tf_op jit(solution)/shard_map/ppermute | solution.py:258
  28.5 10.2 %collective-permute-start.4 = (bf16[32,640]{1,0:T(8,128)(2,1)S(1)}, bf16[32,640]{1,0:T(8,128)(2,1)S(1)}, u32[]{:S(2)}, u32[]{:S(2)}) collective-permute-start(bf16[32,640]{1,0:T(8,128)(2,1)S(1)} %pad_maximum_fusion.1), channel_id=1, source_target_pairs={{0,24},{8,0},{16,8},{24,16},{1,25},{9,1},{17,9},{25,17},{2,26},{10... | collective-permute-start | bytes 122888 | tf_op jit(solution)/shard_map/ppermute | solution.py:258
  31.9 6.8 %collective-permute-start.2 = (bf16[48,640]{1,0:T(8,128)(2,1)S(1)}, bf16[48,640]{1,0:T(8,128)(2,1)S(1)}, u32[]{:S(2)}, u32[]{:S(2)}) collective-permute-start(bf16[48,640]{1,0:T(8,128)(2,1)S(1)} %pad_maximum_fusion), channel_id=1, source_target_pairs={{0,16},{8,24},{16,0},{24,8},{1,17},{9,25},{17,1},{25,9},{2,18},{10... | collective-permute-start | bytes 184328 | tf_op jit(solution)/shard_map/ppermute | solution.py:258
  38.7 0.7 copy-start.3
  38.7 22.1 %copy-start.4 = (pred[48]{0:T(512)(128)(4,1)S(1)}, pred[48]{0:T(512)(128)(4,1)}, u32[]{:S(2)}) copy-start(pred[48]{0:T(512)(128)(4,1)} %constant.22.clone.1) | copy-start | bytes 148
  48.4 12.6 %collective-permute-start = (bf16[16,88,128]{2,1,0:T(8,128)(2,1)S(1)}, bf16[16,88,128]{2,1,0:T(8,128)(2,1)S(1)}, u32[]{:S(2)}, u32[]{:S(2)}) collective-permute-start(bf16[16,88,128]{2,1,0:T(8,128)(2,1)S(1)} %slice.46.kv0_ref), channel_id=1, source_target_pairs={{0,32},{32,64},{64,0},{96,128},{128,160},{160,96},{192,224},{224,2... | collective-permute-start | bytes 1081352 | tf_op jit(solution)/shard_map/ppermute | solution.py:284
  53.4 18.4 %collective-permute-start.1 = (bf16[16,88,128]{2,1,0:T(8,128)(2,1)S(1)}, bf16[16,88,128]{2,1,0:T(8,128)(2,1)S(1)}, u32[]{:S(2)}, u32[]{:S(2)}) collective-permute-start(bf16[16,88,128]{2,1,0:T(8,128)(2,1)S(1)} %slice.46.kv0_ref), channel_id=1, source_target_pairs={{0,64},{32,0},{64,32},{96,160},{128,96},{160,128},{192,256},{224,1... | collective-permute-start | bytes 1081352 | tf_op jit(solution)/shard_map/ppermute | solution.py:284
  56.4 15.5 %all-to-all-start.1 = ((bf16[4,768,128]{2,1,0:T(8,128)(2,1)}), bf16[4,768,128]{2,1,0:T(8,128)(2,1)S(1)}, u32[]{:S(2)}, u32[]{:S(2)}) async-start(bf16[4,768,128]{2,1,0:T(8,128)(2,1)} %broadcast_in_dim.10), calls=%async_computation.1 | async-start | bytes 1572864 | tf_op jit(solution)/shard_map/all_to_all | solution.py:286
  129.9 12.4 %all-to-all-start.4 = ((bf16[4,720,128]{2,1,0:T(8,128)(2,1)}), bf16[4,720,128]{2,1,0:T(8,128)(2,1)S(1)}, u32[]{:S(2)}, u32[]{:S(2)}) async-start(bf16[4,720,128]{2,1,0:T(8,128)(2,1)} %shard_map.58), calls=%async_computation.4 | async-start | bytes 1474560 | tf_op jit(solution)/shard_map/all_to_all | solution.py:316
  134.3 1.9 %copy-start = (bf16[2560,640]{1,0:T(8,128)(2,1)S(1)}, bf16[2560,640]{1,0:T(8,128)(2,1)}, u32[]{:S(2)}) copy-start(bf16[2560,640]{1,0:T(8,128)(2,1)} %all-gather.2.cloned.1.call-done.weight_ref) | copy-start | bytes 9830404
  137.2 1.3 copy-start.1
  142.3 11.1 %collective-permute-start.5 = (bf16[4,720,128]{2,1,0:T(8,128)(2,1)S(1)}, bf16[4,720,128]{2,1,0:T(8,128)(2,1)S(1)}, u32[]{:S(2)}, u32[]{:S(2)}) collective-permute-start(bf16[4,720,128]{2,1,0:T(8,128)(2,1)S(1)} %all-to-all-done.4.packed_ref), channel_id=1, source_target_pairs={{0,1},{1,0},{2,3},{3,2},{4,5},{5,4},{6,7},{7,6},{8,9},{9,8},{10,11... | collective-permute-start | bytes 2211848 | tf_op jit(solution)/shard_map/ppermute | solution.py:328
  151.0 1.5 copy-start.2
  154.9 7.7 %collective-permute-start.6 = (bf16[128,640]{1,0:T(8,128)(2,1)S(1)}, bf16[128,640]{1,0:T(8,128)(2,1)S(1)}, u32[]{:S(2)}, u32[]{:S(2)}) collective-permute-start(bf16[128,640]{1,0:T(8,128)(2,1)S(1)} %get-tuple-element.20), channel_id=1, source_target_pairs={{0,8},{8,0},{16,24},{24,16},{1,9},{9,1},{17,25},{25,17},{2,10},{10... | collective-permute-start | bytes 491528 | tf_op jit(solution)/shard_map/ppermute | solution.py:348
Sparse Core Ops, SparseCore 0:
  39.5 78.8 all-gather.1

commit v12 on v11

--- a/solution.py
+++ b/solution.py
@@ -239,15 +239,21 @@
         sum_ref[x] = total
 
 
-def project_other(place_ref, packed_ref, weight_ref, sum_ref, own_ref, send_ref):
-    totals = []
-    for x, total in enumerate(multiply(packed_ref, weight_ref)):
-        total = total + sum_ref[x]
-        total = [total[r * SLOT : r * SLOT + length] for r, length in enumerate(LENGTHS)]
-        totals.append(jnp.concatenate(total, axis=0))
-    first = lax.rem(place_ref[1], PAIR) == 0
-    own_ref[...] = jnp.where(first, totals[0], totals[1])
-    send_ref[...] = jnp.where(first, totals[1], totals[0]).astype(BF16)
+def project_other(place_ref, packed_ref, weight_ref, sum_ref, out_ref):
+    x = place_ref[0]
+    span = PARTS * SLOT
+    halves = lax.broadcasted_iota(jnp.int32, (span, HEAD), 1) // SHARE
+    blocks = []
+    for y in range(Y):
+        fifth = packed_ref[y, 2 * PAIR * span :, :].astype(F32)
+        for two in range(2):
+            first = pl.multiple_of((2 * x + two) * span, GRANULE)
+            blocks.append(packed_ref[y, pl.ds(first, span), :])
+        blocks.append(jnp.where(halves == x, fifth, 0.0).astype(BF16))
+    total = jnp.dot(jnp.concatenate(blocks, axis=1), weight_ref[...], preferred_element_type=F32)
+    total = total + sum_ref[x]
+    total = [total[r * SLOT : r * SLOT + length] for r, length in enumerate(LENGTHS)]
+    out_ref[...] = jnp.concatenate(total, axis=0).astype(out_ref.dtype)
 
 
 def share_rows(granules):
@@ -335,16 +341,21 @@
         kinds=[F32],
         cost=pl.CostEstimate(flops=1 << 31, bytes_accessed=1 << 23, transcendentals=0),
     )
-    own, send = vmem_call(
-        project_other,
-        16,
-        [(TOK, width), (TOK, width)],
-        others,
-        weight_other,
-        sums,
-        scalars=place,
-        kinds=[F32, BF16],
-    )
+    member = lax.rem(side, PAIR)
+    own, send = [
+        vmem_call(
+            project_other,
+            16,
+            [(TOK, width)],
+            others,
+            weight_other,
+            sums,
+            scalars=which.reshape(1),
+            kinds=[kind],
+            cost=pl.CostEstimate(flops=1 << 31, bytes_accessed=1 << 23, transcendentals=0),
+        )[0]
+        for which, kind in ((member, F32), (1 - member, BF16))
+    ]
     came = lax.ppermute(send, "x", [(x, x + 1 - 2 * (x % PAIR)) for x in range(X)])
     return (own + came.astype(F32)).astype(BF16)
 

time: 171 us -> 171 us (level)
    pallas_call x7 -> x8, Pallas kernels: 17.3 us -> 16.9 us  [vmem_call(): pl.pallas_call(body, out_shape=[jax.ShapeDtypeStruct(shape, kind) for sha...]
where the time goes in v12:
time: 171 us; the launch traced here: 169 us
  starting transfers between devices  52 us (30%)
  blocking collectives  46.2 us (27%)
  waiting for transfers between devices  29.6 us (17%)
  Pallas kernels  16.9 us (10%)
  between operations  13.7 us (8%)
  local copies, waits for them, and re-layouts  9.9 us (6%)
    all_to_all x1, blocking collectives, local(): joined = lax.all_to_all(joined, 'z', 0, 0, tiled=True)  33.6 us
    pallas_call x8, Pallas kernels, vmem_call(): pl.pallas_call(body, out_shape=[jax.ShapeDtypeStruct(shape, kind) for sha...  16.9 us
    all_to_all x1, starting transfers between devices, local(): here = lax.all_to_all(send, 'z', 0, 0, tiled=True)  15.7 us
    all_to_all x1, blocking collectives, local(): part = lax.all_to_all(part, 'x', 0, 0, tiled=True)  12.6 us
    ppermute x2, waiting for transfers between devices, local(): kv_others = [lax.ppermute(kv, 'z', turn) for turn in turns]  10.9 us
    ppermute x3, starting transfers between devices, share_rows(): lax.ppermute(block, 'x', [(x, (x + away) % X) for x in range(X)])  9.93 us
    all_to_all x1, waiting for transfers between devices, local(): here = lax.all_to_all(send, 'z', 0, 0, tiled=True)  8.99 us
    ppermute x1, starting transfers between devices, local(): others = lax.ppermute(packed, 'c', [(0, 1), (1, 0)])  8.44 us
  transfers between devices with their start and end apart: 11, of which 5 were waited for; matrix products, arithmetic and copies ran while one was open for 3% of the time, Pallas kernels for 8%

profile of v12, /device:TPU:1, one launch (start us, length us, event | category | flops | bytes accessed | tf_op | source)
XLA Modules:
  0.0 169.2 jit_solution(14719541043217859710)
XLA Ops:
  6.5 2.2 %shard_map.55 = (bf16[16,136,128]{2,1,0:T(8,128)(2,1)}, bf16[5,16,640]{2,1,0:T(8,128)(2,1)}) custom-call(bf16[128,640]{1,0:T(8,128)(2,1)} %q_ref.1, bf16[128,640]{1,0:T(8,128)(2,1)} %k_ref.1, bf16[128,640]{1,0:T(8,128)(2,1)} %v_ref.1, s32[1,128]{1,0:T(1,128)} %bitcast.26, bf16[80,640]{1,0:T(8,128)(2,1)} %weight_ref.1), custom_call_target="tpu_custom_call" | custom-call | tf_op jit(solution)/shard_map/pallas_call | solution.py:38
  8.7 15.7 %all-to-all-start = ((bf16[16,136,128]{2,1,0:T(8,128)(2,1)}), bf16[16,136,128]{2,1,0:T(8,128)(2,1)S(1)}, u32[]{:S(2)}, u32[]{:S(2)}) async-start(bf16[16,136,128]{2,1,0:T(8,128)(2,1)} %get-tuple-element.11), calls=%async_computation | async-start | bytes 1114112 | tf_op jit(solution)/shard_map/all_to_all | solution.py:283
  24.5 0.8 slice_bitcast_fusion.1
  25.3 3.1 %collective-permute-start.3 = (bf16[32,640]{1,0:T(8,128)(2,1)S(1)}, bf16[32,640]{1,0:T(8,128)(2,1)S(1)}, u32[]{:S(2)}, u32[]{:S(2)}) collective-permute-start(bf16[32,640]{1,0:T(8,128)(2,1)S(1)} %pad_maximum_fusion.1), channel_id=1, source_target_pairs={{0,8},{8,16},{16,24},{24,0},{1,9},{9,17},{17,25},{25,1},{2,10},{10... | collective-permute-start | bytes 122888 | tf_op jit(solution)/shard_map/ppermute | solution.py:264
  28.5 3.4 %collective-permute-start.4 = (bf16[32,640]{1,0:T(8,128)(2,1)S(1)}, bf16[32,640]{1,0:T(8,128)(2,1)S(1)}, u32[]{:S(2)}, u32[]{:S(2)}) collective-permute-start(bf16[32,640]{1,0:T(8,128)(2,1)S(1)} %pad_maximum_fusion.1), channel_id=1, source_target_pairs={{0,24},{8,0},{16,8},{24,16},{1,25},{9,1},{17,9},{25,17},{2,26},{10... | collective-permute-start | bytes 122888 | tf_op jit(solution)/shard_map/ppermute | solution.py:264
  31.9 3.4 %collective-permute-start.2 = (bf16[48,640]{1,0:T(8,128)(2,1)S(1)}, bf16[48,640]{1,0:T(8,128)(2,1)S(1)}, u32[]{:S(2)}, u32[]{:S(2)}) collective-permute-start(bf16[48,640]{1,0:T(8,128)(2,1)S(1)} %pad_maximum_fusion), channel_id=1, source_target_pairs={{0,16},{8,24},{16,0},{24,8},{1,17},{9,25},{17,1},{25,9},{2,18},{10... | collective-permute-start | bytes 184328 | tf_op jit(solution)/shard_map/ppermute | solution.py:264
  35.3 0.7 constant_dynamic-update-slice_fusion.5
  36.0 0.7 constant_dynamic-update-slice_fusion.4
  36.8 0.7 constant_dynamic-update-slice_fusion.3
  37.5 1.1 collective-permute-done.2
  38.7 0.7 copy-done.3
  39.4 9.0 %all-to-all-done = bf16[16,136,128]{2,1,0:T(8,128)(2,1)S(1)} async-done(((bf16[16,136,128]{2,1,0:T(8,128)(2,1)}), bf16[16,136,128]{2,1,0:T(8,128)(2,1)S(1)}, u32[]{:S(2)}, u32[]{:S(2)}) %all-to-all-start) | async-done | bytes 557088 | tf_op jit(solution)/shard_map/all_to_all | solution.py:283
  48.4 5.0 %collective-permute-start = (bf16[16,88,128]{2,1,0:T(8,128)(2,1)S(1)}, bf16[16,88,128]{2,1,0:T(8,128)(2,1)S(1)}, u32[]{:S(2)}, u32[]{:S(2)}) collective-permute-start(bf16[16,88,128]{2,1,0:T(8,128)(2,1)S(1)} %slice.46.kv0_ref), channel_id=1, source_target_pairs={{0,32},{32,64},{64,0},{96,128},{128,160},{160,96},{192,224},{224,2... | collective-permute-start | bytes 1081352 | tf_op jit(solution)/shard_map/ppermute | solution.py:290
  53.5 1.9 %collective-permute-start.1 = (bf16[16,88,128]{2,1,0:T(8,128)(2,1)S(1)}, bf16[16,88,128]{2,1,0:T(8,128)(2,1)S(1)}, u32[]{:S(2)}, u32[]{:S(2)}) collective-permute-start(bf16[16,88,128]{2,1,0:T(8,128)(2,1)S(1)} %slice.46.kv0_ref), channel_id=1, source_target_pairs={{0,64},{32,0},{64,32},{96,160},{128,96},{160,128},{192,256},{224,1... | collective-permute-start | bytes 1081352 | tf_op jit(solution)/shard_map/ppermute | solution.py:290
  55.4 1.0 broadcast_in_dim.10
  56.4 4.0 %all-to-all-start.1 = ((bf16[4,768,128]{2,1,0:T(8,128)(2,1)}), bf16[4,768,128]{2,1,0:T(8,128)(2,1)S(1)}, u32[]{:S(2)}, u32[]{:S(2)}) async-start(bf16[4,768,128]{2,1,0:T(8,128)(2,1)} %broadcast_in_dim.10), calls=%async_computation.1 | async-start | bytes 1572864 | tf_op jit(solution)/shard_map/all_to_all | solution.py:292
  61.0 10.9 %collective-permute-done.1.kv2_ref = bf16[16,88,128]{2,1,0:T(8,128)(2,1)S(1)} collective-permute-done((bf16[16,88,128]{2,1,0:T(8,128)(2,1)S(1)}, bf16[16,88,128]{2,1,0:T(8,128)(2,1)S(1)}, u32[]{:S(2)}, u32[]{:S(2)}) %collective-permute-start.1) | collective-permute-done | bytes 360480 | tf_op jit(solution)/shard_map/ppermute | solution.py:290
  71.8 10.3 %shard_map.56 = bf16[4,816,128]{2,1,0:T(8,128)(2,1)S(1)} custom-call(s32[1]{0:T(128)} %bitcast.1.third_ref, bf16[4,768,128]{2,1,0:T(8,128)(2,1)S(1)} %all-to-all-done.1.q_ref, bf16[16,88,128]{2,1,0:T(8,128)(2,1)S(1)} %slice.46.kv0_ref, bf16[16,88,128]{2,1,0:T(8,128)(2,1)S(1)} %collective-permute-done.kv1_ref, ...), custom_call_target="tpu_custom_call" | custom-call | flops 68719476736 | bytes 4194304 | tf_op jit(solution)/shard_map/pallas_call | solution.py:38
  82.2 12.6 %all_to_all.25.part_ref = bf16[4,816,128]{2,1,0:T(8,128)(2,1)S(1)} all-to-all(bf16[4,816,128]{2,1,0:T(8,128)(2,1)S(1)} %shard_map.56), channel_id=1, replica_groups=mesh['z'=16,'x'=4,'y'=4,'c'=2] {'x'}, dimensions={0} | all-to-all | bytes 1671168 | tf_op jit(solution)/shard_map/all_to_all | solution.py:318
  95.4 33.6 %all_to_all.26.part_ref = bf16[16,48,128]{2,1,0:T(8,128)(2,1)S(1)} all-to-all(bf16[16,48,128]{2,1,0:T(8,128)(2,1)S(1)} %shard_map.57), channel_id=1, replica_groups=mesh['z'=16,'x'=4,'y'=4,'c'=2] {'z'}, dimensions={0} | all-to-all | bytes 393216 | tf_op jit(solution)/shard_map/all_to_all | solution.py:320
  129.0 1.0 shard_map.58
  129.9 4.5 %all-to-all-start.4 = ((bf16[4,720,128]{2,1,0:T(8,128)(2,1)}), bf16[4,720,128]{2,1,0:T(8,128)(2,1)S(1)}, u32[]{:S(2)}, u32[]{:S(2)}) async-start(bf16[4,720,128]{2,1,0:T(8,128)(2,1)} %shard_map.58), calls=%async_computation.4 | async-start | bytes 1474560 | tf_op jit(solution)/shard_map/all_to_all | solution.py:322
  134.5 1.9 %copy-done = bf16[2560,640]{1,0:T(8,128)(2,1)S(1)} copy-done((bf16[2560,640]{1,0:T(8,128)(2,1)S(1)}, bf16[2560,640]{1,0:T(8,128)(2,1)}, u32[]{:S(2)}) %copy-start) | copy-done | bytes 3276824
  136.4 0.9 shard_map.59
  137.4 1.3 copy-done.1
  138.7 3.8 %all-to-all-done.4.packed_ref = bf16[4,720,128]{2,1,0:T(8,128)(2,1)S(1)} async-done(((bf16[4,720,128]{2,1,0:T(8,128)(2,1)}), bf16[4,720,128]{2,1,0:T(8,128)(2,1)S(1)}, u32[]{:S(2)}, u32[]{:S(2)}) %all-to-all-start.4) | async-done | bytes 737312 | tf_op jit(solution)/shard_map/all_to_all | solution.py:322
  142.5 8.4 %collective-permute-start.5 = (bf16[4,720,128]{2,1,0:T(8,128)(2,1)S(1)}, bf16[4,720,128]{2,1,0:T(8,128)(2,1)S(1)}, u32[]{:S(2)}, u32[]{:S(2)}) collective-permute-start(bf16[4,720,128]{2,1,0:T(8,128)(2,1)S(1)} %all-to-all-done.4.packed_ref), channel_id=1, source_target_pairs={{0,1},{1,0},{2,3},{3,2},{4,5},{5,4},{6,7},{7,6},{8,9},{9,8},{10,11... | collective-permute-start | bytes 2211848 | tf_op jit(solution)/shard_map/ppermute | solution.py:334
  150.9 1.5 copy-done.2
  152.5 0.9 shard_map.60.sum_ref
  153.9 2.4 %collective-permute-start.6 = (bf16[128,640]{1,0:T(8,128)(2,1)S(1)}, bf16[128,640]{1,0:T(8,128)(2,1)S(1)}, u32[]{:S(2)}, u32[]{:S(2)}) collective-permute-start(bf16[128,640]{1,0:T(8,128)(2,1)S(1)} %shard_map.62), channel_id=1, source_target_pairs={{0,8},{8,0},{16,24},{24,16},{1,9},{9,1},{17,25},{25,17},{2,10},{10... | collective-permute-start | bytes 491528 | tf_op jit(solution)/shard_map/ppermute | solution.py:359
  156.8 4.8 %collective-permute-done.6 = bf16[128,640]{1,0:T(8,128)(2,1)S(1)} collective-permute-done((bf16[128,640]{1,0:T(8,128)(2,1)S(1)}, bf16[128,640]{1,0:T(8,128)(2,1)S(1)}, u32[]{:S(2)}, u32[]{:S(2)}) %collective-permute-start.6) | collective-permute-done | bytes 163872 | tf_op jit(solution)/shard_map/ppermute | solution.py:359
  161.6 0.7 add_convert_fusion
  (37 shorter events, 2.5 us)
Async XLA Ops:
  8.7 39.7 %all-to-all-start = ((bf16[16,136,128]{2,1,0:T(8,128)(2,1)}), bf16[16,136,128]{2,1,0:T(8,128)(2,1)S(1)}, u32[]{:S(2)}, u32[]{:S(2)}) async-start(bf16[16,136,128]{2,1,0:T(8,128)(2,1)} %get-tuple-element.11), calls=%async_computation | async-start | bytes 1114112 | tf_op jit(solution)/shard_map/all_to_all | solution.py:283
  24.5 110.0 %all-gather.2.cloned.1.call-start = ((), (), s32[]{:S(2)}) async-start(), calls=%async_computation.5 | async-start | bytes 3481600 | tf_op jit(solution)/shard_map/all_gather | solution.py:284
  25.3 13.3 %collective-permute-start.3 = (bf16[32,640]{1,0:T(8,128)(2,1)S(1)}, bf16[32,640]{1,0:T(8,128)(2,1)S(1)}, u32[]{:S(2)}, u32[]{:S(2)}) collective-permute-start(bf16[32,640]{1,0:T(8,128)(2,1)S(1)} %pad_maximum_fusion.1), channel_id=1, source_target_pairs={{0,8},{8,16},{16,24},{24,0},{1,9},{9,17},{17,25},{25,1},{2,10},{10... | collective-permute-start | bytes 122888 | tf_op jit(solution)/shard_map/ppermute | solution.py:264
  28.5 10.2 %collective-permute-start.4 = (bf16[32,640]{1,0:T(8,128)(2,1)S(1)}, bf16[32,640]{1,0:T(8,128)(2,1)S(1)}, u32[]{:S(2)}, u32[]{:S(2)}) collective-permute-start(bf16[32,640]{1,0:T(8,128)(2,1)S(1)} %pad_maximum_fusion.1), channel_id=1, source_target_pairs={{0,24},{8,0},{16,8},{24,16},{1,25},{9,1},{17,9},{25,17},{2,26},{10... | collective-permute-start | bytes 122888 | tf_op jit(solution)/shard_map/ppermute | solution.py:264
  31.9 6.8 %collective-permute-start.2 = (bf16[48,640]{1,0:T(8,128)(2,1)S(1)}, bf16[48,640]{1,0:T(8,128)(2,1)S(1)}, u32[]{:S(2)}, u32[]{:S(2)}) collective-permute-start(bf16[48,640]{1,0:T(8,128)(2,1)S(1)} %pad_maximum_fusion), channel_id=1, source_target_pairs={{0,16},{8,24},{16,0},{24,8},{1,17},{9,25},{17,1},{25,9},{2,18},{10... | collective-permute-start | bytes 184328 | tf_op jit(solution)/shard_map/ppermute | solution.py:264
  38.7 0.7 copy-start.3
  38.7 22.1 %copy-start.4 = (pred[48]{0:T(512)(128)(4,1)S(1)}, pred[48]{0:T(512)(128)(4,1)}, u32[]{:S(2)}) copy-start(pred[48]{0:T(512)(128)(4,1)} %constant.27.clone.1) | copy-start | bytes 148
  48.4 12.6 %collective-permute-start = (bf16[16,88,128]{2,1,0:T(8,128)(2,1)S(1)}, bf16[16,88,128]{2,1,0:T(8,128)(2,1)S(1)}, u32[]{:S(2)}, u32[]{:S(2)}) collective-permute-start(bf16[16,88,128]{2,1,0:T(8,128)(2,1)S(1)} %slice.46.kv0_ref), channel_id=1, source_target_pairs={{0,32},{32,64},{64,0},{96,128},{128,160},{160,96},{192,224},{224,2... | collective-permute-start | bytes 1081352 | tf_op jit(solution)/shard_map/ppermute | solution.py:290
  53.5 18.4 %collective-permute-start.1 = (bf16[16,88,128]{2,1,0:T(8,128)(2,1)S(1)}, bf16[16,88,128]{2,1,0:T(8,128)(2,1)S(1)}, u32[]{:S(2)}, u32[]{:S(2)}) collective-permute-start(bf16[16,88,128]{2,1,0:T(8,128)(2,1)S(1)} %slice.46.kv0_ref), channel_id=1, source_target_pairs={{0,64},{32,0},{64,32},{96,160},{128,96},{160,128},{192,256},{224,1... | collective-permute-start | bytes 1081352 | tf_op jit(solution)/shard_map/ppermute | solution.py:290
  56.4 15.5 %all-to-all-start.1 = ((bf16[4,768,128]{2,1,0:T(8,128)(2,1)}), bf16[4,768,128]{2,1,0:T(8,128)(2,1)S(1)}, u32[]{:S(2)}, u32[]{:S(2)}) async-start(bf16[4,768,128]{2,1,0:T(8,128)(2,1)} %broadcast_in_dim.10), calls=%async_computation.1 | async-start | bytes 1572864 | tf_op jit(solution)/shard_map/all_to_all | solution.py:292
  129.9 12.5 %all-to-all-start.4 = ((bf16[4,720,128]{2,1,0:T(8,128)(2,1)}), bf16[4,720,128]{2,1,0:T(8,128)(2,1)S(1)}, u32[]{:S(2)}, u32[]{:S(2)}) async-start(bf16[4,720,128]{2,1,0:T(8,128)(2,1)} %shard_map.58), calls=%async_computation.4 | async-start | bytes 1474560 | tf_op jit(solution)/shard_map/all_to_all | solution.py:322
  134.5 1.9 %copy-start = (bf16[2560,640]{1,0:T(8,128)(2,1)S(1)}, bf16[2560,640]{1,0:T(8,128)(2,1)}, u32[]{:S(2)}) copy-start(bf16[2560,640]{1,0:T(8,128)(2,1)} %all-gather.2.cloned.1.call-done.weight_ref) | copy-start | bytes 9830404
  137.4 1.3 copy-start.1
  142.5 10.9 %collective-permute-start.5 = (bf16[4,720,128]{2,1,0:T(8,128)(2,1)S(1)}, bf16[4,720,128]{2,1,0:T(8,128)(2,1)S(1)}, u32[]{:S(2)}, u32[]{:S(2)}) collective-permute-start(bf16[4,720,128]{2,1,0:T(8,128)(2,1)S(1)} %all-to-all-done.4.packed_ref), channel_id=1, source_target_pairs={{0,1},{1,0},{2,3},{3,2},{4,5},{5,4},{6,7},{7,6},{8,9},{9,8},{10,11... | collective-permute-start | bytes 2211848 | tf_op jit(solution)/shard_map/ppermute | solution.py:334
  150.9 1.5 copy-start.2
  153.9 7.7 %collective-permute-start.6 = (bf16[128,640]{1,0:T(8,128)(2,1)S(1)}, bf16[128,640]{1,0:T(8,128)(2,1)S(1)}, u32[]{:S(2)}, u32[]{:S(2)}) collective-permute-start(bf16[128,640]{1,0:T(8,128)(2,1)S(1)} %shard_map.62), channel_id=1, source_target_pairs={{0,8},{8,0},{16,24},{24,16},{1,9},{9,1},{17,25},{25,17},{2,10},{10... | collective-permute-start | bytes 491528 | tf_op jit(solution)/shard_map/ppermute | solution.py:359
Sparse Core Ops, SparseCore 0:
  39.5 78.8 all-gather.1

commit v13 on v12

--- a/solution.py
+++ b/solution.py
@@ -288,8 +288,7 @@
         for k in (1, 2)
     ]
     kv_others = [lax.ppermute(kv, "z", turn) for turn in turns]
-    query = jnp.broadcast_to(here[:, :SLOT, :].reshape(1, Z * SLOT, HEAD), (X, Z * SLOT, HEAD))
-    query = lax.all_to_all(query, "x", 0, 0, tiled=True)
+    query = lax.all_gather(here[:, :SLOT, :].reshape(Z * SLOT, HEAD), "x", axis=0)
 
     home = (X * jnp.arange(Z, dtype=jnp.int32) + side) * TOK
     key_code = here[:, ID_ROW + 1, :].astype(F32) * POSITIONS + (

time: 171 us -> 170 us (level)
  blocking collectives: 46.2 us -> 57.3 us
  waiting for transfers between devices: 29.6 us -> 23.4 us
  starting transfers between devices: 52 us -> 48.3 us
    all_gather x0 -> x1, blocking collectives: none -> 11.7 us  [local(): lax.all_gather(here[:, :SLOT, :].reshape(Z * SLOT, HEAD), 'x', axis=0)]
    ppermute x2, waiting for transfers between devices: 10.9 us -> 5.16 us  [local(): kv_others = [lax.ppermute(kv, 'z', turn) for turn in turns]]
    all_to_all x1 -> x0, starting transfers between devices: 4.01 us -> none  [local(): query = lax.all_to_all(query, 'x', 0, 0, tiled=True)]
  transfers between devices with their start and end apart: 11 -> 10, of which waited for: 5 -> 5; matrix products, arithmetic and copies ran while one was open for 3% -> 2% of each run, Pallas kernels for 8% -> 8%
where the time goes in v13:
time: 170 us
  blocking collectives  57.3 us (34%)
  starting transfers between devices  48.3 us (28%)
  waiting for transfers between devices  23.4 us (14%)
  Pallas kernels  17.1 us (10%)
  between operations  13.7 us (8%)
  local copies, waits for them, and re-layouts  8.9 us (5%)
    all_to_all x1, blocking collectives, local(): joined = lax.all_to_all(joined, 'z', 0, 0, tiled=True)  33 us
    pallas_call x8, Pallas kernels, vmem_call(): pl.pallas_call(body, out_shape=[jax.ShapeDtypeStruct(shape, kind) for sha...  17.1 us
    all_to_all x1, starting transfers between devices, local(): here = lax.all_to_all(send, 'z', 0, 0, tiled=True)  15.7 us
    all_to_all x1, blocking collectives, local(): part = lax.all_to_all(part, 'x', 0, 0, tiled=True)  12.6 us
    all_gather x1, blocking collectives, local(): lax.all_gather(here[:, :SLOT, :].reshape(Z * SLOT, HEAD), 'x', axis=0)  11.7 us
    ppermute x3, starting transfers between devices, share_rows(): lax.ppermute(block, 'x', [(x, (x + away) % X) for x in range(X)])  9.93 us
    all_to_all x1, waiting for transfers between devices, local(): here = lax.all_to_all(send, 'z', 0, 0, tiled=True)  8.99 us
    ppermute x1, starting transfers between devices, local(): others = lax.ppermute(packed, 'c', [(0, 1), (1, 0)])  8.75 us
  transfers between devices with their start and end apart: 10, of which 5 were waited for; matrix products, arithmetic and copies ran while one was open for 2% of the time, Pallas kernels for 8%

profile of v13, /device:TPU:1, one launch (start us, length us, event | category | flops | bytes accessed | tf_op | source)
XLA Modules:
  0.0 169.5 jit_solution(810683247760641656)
XLA Ops:
  6.5 2.2 %shard_map.55 = (bf16[16,136,128]{2,1,0:T(8,128)(2,1)}, bf16[5,16,640]{2,1,0:T(8,128)(2,1)}) custom-call(bf16[128,640]{1,0:T(8,128)(2,1)} %q_ref.1, bf16[128,640]{1,0:T(8,128)(2,1)} %k_ref.1, bf16[128,640]{1,0:T(8,128)(2,1)} %v_ref.1, s32[1,128]{1,0:T(1,128)} %bitcast.26, bf16[80,640]{1,0:T(8,128)(2,1)} %weight_ref.1), custom_call_target="tpu_custom_call" | custom-call | tf_op jit(solution)/shard_map/pallas_call | solution.py:38
  8.7 15.7 %all-to-all-start = ((bf16[16,136,128]{2,1,0:T(8,128)(2,1)}), bf16[16,136,128]{2,1,0:T(8,128)(2,1)S(1)}, u32[]{:S(2)}, u32[]{:S(2)}) async-start(bf16[16,136,128]{2,1,0:T(8,128)(2,1)} %get-tuple-element.11), calls=%async_computation | async-start | bytes 1114112 | tf_op jit(solution)/shard_map/all_to_all | solution.py:283
  24.5 0.8 slice_bitcast_fusion.1
  25.4 3.1 %collective-permute-start.3 = (bf16[32,640]{1,0:T(8,128)(2,1)S(1)}, bf16[32,640]{1,0:T(8,128)(2,1)S(1)}, u32[]{:S(2)}, u32[]{:S(2)}) collective-permute-start(bf16[32,640]{1,0:T(8,128)(2,1)S(1)} %pad_maximum_fusion.1), channel_id=1, source_target_pairs={{0,8},{8,16},{16,24},{24,0},{1,9},{9,17},{17,25},{25,1},{2,10},{10... | collective-permute-start | bytes 122888 | tf_op jit(solution)/shard_map/ppermute | solution.py:264
  28.5 3.4 %collective-permute-start.4 = (bf16[32,640]{1,0:T(8,128)(2,1)S(1)}, bf16[32,640]{1,0:T(8,128)(2,1)S(1)}, u32[]{:S(2)}, u32[]{:S(2)}) collective-permute-start(bf16[32,640]{1,0:T(8,128)(2,1)S(1)} %pad_maximum_fusion.1), channel_id=1, source_target_pairs={{0,24},{8,0},{16,8},{24,16},{1,25},{9,1},{17,9},{25,17},{2,26},{10... | collective-permute-start | bytes 122888 | tf_op jit(solution)/shard_map/ppermute | solution.py:264
  31.9 3.4 %collective-permute-start.2 = (bf16[48,640]{1,0:T(8,128)(2,1)S(1)}, bf16[48,640]{1,0:T(8,128)(2,1)S(1)}, u32[]{:S(2)}, u32[]{:S(2)}) collective-permute-start(bf16[48,640]{1,0:T(8,128)(2,1)S(1)} %pad_maximum_fusion), channel_id=1, source_target_pairs={{0,16},{8,24},{16,0},{24,8},{1,17},{9,25},{17,1},{25,9},{2,18},{10... | collective-permute-start | bytes 184328 | tf_op jit(solution)/shard_map/ppermute | solution.py:264
  35.3 0.7 constant_dynamic-update-slice_fusion.5
  36.1 0.7 constant_dynamic-update-slice_fusion.4
  36.8 0.7 constant_dynamic-update-slice_fusion.3
  37.5 1.1 collective-permute-done.2
  38.7 0.7 copy-done.3
  39.4 9.0 %all-to-all-done = bf16[16,136,128]{2,1,0:T(8,128)(2,1)S(1)} async-done(((bf16[16,136,128]{2,1,0:T(8,128)(2,1)}), bf16[16,136,128]{2,1,0:T(8,128)(2,1)S(1)}, u32[]{:S(2)}, u32[]{:S(2)}) %all-to-all-start) | async-done | bytes 557088 | tf_op jit(solution)/shard_map/all_to_all | solution.py:283
  48.7 5.0 %collective-permute-start = (bf16[16,88,128]{2,1,0:T(8,128)(2,1)S(1)}, bf16[16,88,128]{2,1,0:T(8,128)(2,1)S(1)}, u32[]{:S(2)}, u32[]{:S(2)}) collective-permute-start(bf16[16,88,128]{2,1,0:T(8,128)(2,1)S(1)} %slice.46.kv0_ref), channel_id=1, source_target_pairs={{0,32},{32,64},{64,0},{96,128},{128,160},{160,96},{192,224},{224,2... | collective-permute-start | bytes 1081352 | tf_op jit(solution)/shard_map/ppermute | solution.py:290
  53.7 1.9 %collective-permute-start.1 = (bf16[16,88,128]{2,1,0:T(8,128)(2,1)S(1)}, bf16[16,88,128]{2,1,0:T(8,128)(2,1)S(1)}, u32[]{:S(2)}, u32[]{:S(2)}) collective-permute-start(bf16[16,88,128]{2,1,0:T(8,128)(2,1)S(1)} %slice.46.kv0_ref), channel_id=1, source_target_pairs={{0,64},{32,0},{64,32},{96,160},{128,96},{160,128},{192,256},{224,1... | collective-permute-start | bytes 1081352 | tf_op jit(solution)/shard_map/ppermute | solution.py:290
  56.0 11.7 %all_gather.6.q_ref = bf16[4,768,128]{2,1,0:T(8,128)(2,1)S(1)} all-gather(bf16[1,768,128]{2,1,0:T(8,128)(2,1)S(1)} %bitcast.24), channel_id=1, replica_groups=mesh['z'=16,'x'=4,'y'=4,'c'=2] {'x'}, dimensions={0}, use_global_device_ids=true | all-gather | bytes 983040 | tf_op jit(solution)/shard_map/all_gather | solution.py:291
  67.7 5.2 %collective-permute-done.1.kv2_ref = bf16[16,88,128]{2,1,0:T(8,128)(2,1)S(1)} collective-permute-done((bf16[16,88,128]{2,1,0:T(8,128)(2,1)S(1)}, bf16[16,88,128]{2,1,0:T(8,128)(2,1)S(1)}, u32[]{:S(2)}, u32[]{:S(2)}) %collective-permute-start.1) | collective-permute-done | bytes 360480 | tf_op jit(solution)/shard_map/ppermute | solution.py:290
  72.8 10.4 %shard_map.56 = bf16[4,816,128]{2,1,0:T(8,128)(2,1)S(1)} custom-call(s32[1]{0:T(128)} %bitcast.1.third_ref, bf16[4,768,128]{2,1,0:T(8,128)(2,1)S(1)} %all_gather.6.q_ref, bf16[16,88,128]{2,1,0:T(8,128)(2,1)S(1)} %slice.46.kv0_ref, bf16[16,88,128]{2,1,0:T(8,128)(2,1)S(1)} %collective-permute-done.kv1_ref, ...), custom_call_target="tpu_custom_call" | custom-call | flops 68719476736 | bytes 4194304 | tf_op jit(solution)/shard_map/pallas_call | solution.py:38
  83.3 12.6 %all_to_all.20.part_ref = bf16[4,816,128]{2,1,0:T(8,128)(2,1)S(1)} all-to-all(bf16[4,816,128]{2,1,0:T(8,128)(2,1)S(1)} %shard_map.56), channel_id=1, replica_groups=mesh['z'=16,'x'=4,'y'=4,'c'=2] {'x'}, dimensions={0} | all-to-all | bytes 1671168 | tf_op jit(solution)/shard_map/all_to_all | solution.py:317
  95.8 0.6 shard_map.57
  96.5 33.0 %all_to_all.21.part_ref = bf16[16,48,128]{2,1,0:T(8,128)(2,1)S(1)} all-to-all(bf16[16,48,128]{2,1,0:T(8,128)(2,1)S(1)} %shard_map.57), channel_id=1, replica_groups=mesh['z'=16,'x'=4,'y'=4,'c'=2] {'z'}, dimensions={0} | all-to-all | bytes 393216 | tf_op jit(solution)/shard_map/all_to_all | solution.py:319
  129.5 1.0 shard_map.58
  130.5 4.0 %all-to-all-start.3 = ((bf16[4,720,128]{2,1,0:T(8,128)(2,1)}), bf16[4,720,128]{2,1,0:T(8,128)(2,1)S(1)}, u32[]{:S(2)}, u32[]{:S(2)}) async-start(bf16[4,720,128]{2,1,0:T(8,128)(2,1)} %shard_map.58), calls=%async_computation.3 | async-start | bytes 1474560 | tf_op jit(solution)/shard_map/all_to_all | solution.py:321
  134.5 1.9 %copy-done = bf16[2560,640]{1,0:T(8,128)(2,1)S(1)} copy-done((bf16[2560,640]{1,0:T(8,128)(2,1)S(1)}, bf16[2560,640]{1,0:T(8,128)(2,1)}, u32[]{:S(2)}) %copy-start) | copy-done | bytes 3276824
  136.5 0.9 shard_map.59
  137.4 1.3 copy-done.1
  138.7 3.8 %all-to-all-done.3.packed_ref = bf16[4,720,128]{2,1,0:T(8,128)(2,1)S(1)} async-done(((bf16[4,720,128]{2,1,0:T(8,128)(2,1)}), bf16[4,720,128]{2,1,0:T(8,128)(2,1)S(1)}, u32[]{:S(2)}, u32[]{:S(2)}) %all-to-all-start.3) | async-done | bytes 737312 | tf_op jit(solution)/shard_map/all_to_all | solution.py:321
  142.5 8.8 %collective-permute-start.5 = (bf16[4,720,128]{2,1,0:T(8,128)(2,1)S(1)}, bf16[4,720,128]{2,1,0:T(8,128)(2,1)S(1)}, u32[]{:S(2)}, u32[]{:S(2)}) collective-permute-start(bf16[4,720,128]{2,1,0:T(8,128)(2,1)S(1)} %all-to-all-done.3.packed_ref), channel_id=1, source_target_pairs={{0,1},{1,0},{2,3},{3,2},{4,5},{5,4},{6,7},{7,6},{8,9},{9,8},{10,11... | collective-permute-start | bytes 2211848 | tf_op jit(solution)/shard_map/ppermute | solution.py:333
  151.3 1.5 copy-done.2
  152.8 0.9 shard_map.60.sum_ref
  154.3 2.9 %collective-permute-start.6 = (bf16[128,640]{1,0:T(8,128)(2,1)S(1)}, bf16[128,640]{1,0:T(8,128)(2,1)S(1)}, u32[]{:S(2)}, u32[]{:S(2)}) collective-permute-start(bf16[128,640]{1,0:T(8,128)(2,1)S(1)} %shard_map.62), channel_id=1, source_target_pairs={{0,8},{8,0},{16,24},{24,16},{1,9},{9,1},{17,25},{25,17},{2,10},{10... | collective-permute-start | bytes 491528 | tf_op jit(solution)/shard_map/ppermute | solution.py:358
  157.7 4.3 %collective-permute-done.6 = bf16[128,640]{1,0:T(8,128)(2,1)S(1)} collective-permute-done((bf16[128,640]{1,0:T(8,128)(2,1)S(1)}, bf16[128,640]{1,0:T(8,128)(2,1)S(1)}, u32[]{:S(2)}, u32[]{:S(2)}) %collective-permute-start.6) | collective-permute-done | bytes 163872 | tf_op jit(solution)/shard_map/ppermute | solution.py:358
  162.0 0.7 add_convert_fusion
  (35 shorter events, 1.8 us)
Async XLA Ops:
  6.5 49.3 %copy-start.4 = (pred[48]{0:T(512)(128)(4,1)S(1)}, pred[48]{0:T(512)(128)(4,1)}, u32[]{:S(2)}) copy-start(pred[48]{0:T(512)(128)(4,1)} %constant.27.clone.1) | copy-start | bytes 148
  8.7 39.7 %all-to-all-start = ((bf16[16,136,128]{2,1,0:T(8,128)(2,1)}), bf16[16,136,128]{2,1,0:T(8,128)(2,1)S(1)}, u32[]{:S(2)}, u32[]{:S(2)}) async-start(bf16[16,136,128]{2,1,0:T(8,128)(2,1)} %get-tuple-element.11), calls=%async_computation | async-start | bytes 1114112 | tf_op jit(solution)/shard_map/all_to_all | solution.py:283
  24.5 110.1 %all-gather.2.cloned.1.call-start = ((), (), s32[]{:S(2)}) async-start(), calls=%async_computation.4 | async-start | bytes 3481600 | tf_op jit(solution)/shard_map/all_gather | solution.py:284
  25.4 13.3 %collective-permute-start.3 = (bf16[32,640]{1,0:T(8,128)(2,1)S(1)}, bf16[32,640]{1,0:T(8,128)(2,1)S(1)}, u32[]{:S(2)}, u32[]{:S(2)}) collective-permute-start(bf16[32,640]{1,0:T(8,128)(2,1)S(1)} %pad_maximum_fusion.1), channel_id=1, source_target_pairs={{0,8},{8,16},{16,24},{24,0},{1,9},{9,17},{17,25},{25,1},{2,10},{10... | collective-permute-start | bytes 122888 | tf_op jit(solution)/shard_map/ppermute | solution.py:264
  28.5 10.2 %collective-permute-start.4 = (bf16[32,640]{1,0:T(8,128)(2,1)S(1)}, bf16[32,640]{1,0:T(8,128)(2,1)S(1)}, u32[]{:S(2)}, u32[]{:S(2)}) collective-permute-start(bf16[32,640]{1,0:T(8,128)(2,1)S(1)} %pad_maximum_fusion.1), channel_id=1, source_target_pairs={{0,24},{8,0},{16,8},{24,16},{1,25},{9,1},{17,9},{25,17},{2,26},{10... | collective-permute-start | bytes 122888 | tf_op jit(solution)/shard_map/ppermute | solution.py:264
  31.9 6.8 %collective-permute-start.2 = (bf16[48,640]{1,0:T(8,128)(2,1)S(1)}, bf16[48,640]{1,0:T(8,128)(2,1)S(1)}, u32[]{:S(2)}, u32[]{:S(2)}) collective-permute-start(bf16[48,640]{1,0:T(8,128)(2,1)S(1)} %pad_maximum_fusion), channel_id=1, source_target_pairs={{0,16},{8,24},{16,0},{24,8},{1,17},{9,25},{17,1},{25,9},{2,18},{10... | collective-permute-start | bytes 184328 | tf_op jit(solution)/shard_map/ppermute | solution.py:264
  38.7 0.7 copy-start.3
  48.7 19.0 %collective-permute-start = (bf16[16,88,128]{2,1,0:T(8,128)(2,1)S(1)}, bf16[16,88,128]{2,1,0:T(8,128)(2,1)S(1)}, u32[]{:S(2)}, u32[]{:S(2)}) collective-permute-start(bf16[16,88,128]{2,1,0:T(8,128)(2,1)S(1)} %slice.46.kv0_ref), channel_id=1, source_target_pairs={{0,32},{32,64},{64,0},{96,128},{128,160},{160,96},{192,224},{224,2... | collective-permute-start | bytes 1081352 | tf_op jit(solution)/shard_map/ppermute | solution.py:290
  53.7 19.1 %collective-permute-start.1 = (bf16[16,88,128]{2,1,0:T(8,128)(2,1)S(1)}, bf16[16,88,128]{2,1,0:T(8,128)(2,1)S(1)}, u32[]{:S(2)}, u32[]{:S(2)}) collective-permute-start(bf16[16,88,128]{2,1,0:T(8,128)(2,1)S(1)} %slice.46.kv0_ref), channel_id=1, source_target_pairs={{0,64},{32,0},{64,32},{96,160},{128,96},{160,128},{192,256},{224,1... | collective-permute-start | bytes 1081352 | tf_op jit(solution)/shard_map/ppermute | solution.py:290
  130.5 12.1 %all-to-all-start.3 = ((bf16[4,720,128]{2,1,0:T(8,128)(2,1)}), bf16[4,720,128]{2,1,0:T(8,128)(2,1)S(1)}, u32[]{:S(2)}, u32[]{:S(2)}) async-start(bf16[4,720,128]{2,1,0:T(8,128)(2,1)} %shard_map.58), calls=%async_computation.3 | async-start | bytes 1474560 | tf_op jit(solution)/shard_map/all_to_all | solution.py:321
  134.5 1.9 %copy-start = (bf16[2560,640]{1,0:T(8,128)(2,1)S(1)}, bf16[2560,640]{1,0:T(8,128)(2,1)}, u32[]{:S(2)}) copy-start(bf16[2560,640]{1,0:T(8,128)(2,1)} %all-gather.2.cloned.1.call-done.weight_ref) | copy-start | bytes 9830404
  137.4 1.3 copy-start.1
  142.5 11.2 %collective-permute-start.5 = (bf16[4,720,128]{2,1,0:T(8,128)(2,1)S(1)}, bf16[4,720,128]{2,1,0:T(8,128)(2,1)S(1)}, u32[]{:S(2)}, u32[]{:S(2)}) collective-permute-start(bf16[4,720,128]{2,1,0:T(8,128)(2,1)S(1)} %all-to-all-done.3.packed_ref), channel_id=1, source_target_pairs={{0,1},{1,0},{2,3},{3,2},{4,5},{5,4},{6,7},{7,6},{8,9},{9,8},{10,11... | collective-permute-start | bytes 2211848 | tf_op jit(solution)/shard_map/ppermute | solution.py:333
  151.3 1.5 copy-start.2
  154.3 7.7 %collective-permute-start.6 = (bf16[128,640]{1,0:T(8,128)(2,1)S(1)}, bf16[128,640]{1,0:T(8,128)(2,1)S(1)}, u32[]{:S(2)}, u32[]{:S(2)}) collective-permute-start(bf16[128,640]{1,0:T(8,128)(2,1)S(1)} %shard_map.62), channel_id=1, source_target_pairs={{0,8},{8,0},{16,24},{24,16},{1,9},{9,1},{17,25},{25,17},{2,10},{10... | collective-permute-start | bytes 491528 | tf_op jit(solution)/shard_map/ppermute | solution.py:358
Sparse Core Ops, SparseCore 0:
  39.5 78.9 all-gather.1
